TPU v7x, 32 devices: a whole 2x2x4 slice. The times are simulated.
32 devices in a mesh: ctx: 8 (over z, y), fsdp: 4 (over x, core).
Axes of the slice: x: 2, y: 2, z: 4, core: 2. Of those that a mesh axis runs over, the one named last changes fastest.
Arguments:
- tokens: bfloat16 [4, 1024, 2560], P('fsdp', 'ctx'), may hold values from -6 to 6
- doc_bounds: int32 [4, 2], P('fsdp'), may hold values from 1 to 1023, as said below
- cotangent: bfloat16 [4, 1024, 2560], P('fsdp', 'ctx'), may hold values from -6 to 6
- norm_one: float32 [2560], replicated, may hold values from 0.25 to 1.75
- query_weight: bfloat16 [2560, 2560], P('fsdp'), may hold values from -0.125 to 0.125
- keyval_weight: bfloat16 [2560, 512], P('fsdp'), may hold values from -0.125 to 0.125
- out_weight: bfloat16 [2560, 2560], P('fsdp'), may hold values from -1 to 1
- norm_two: float32 [2560], replicated, may hold values from 0.25 to 1.75
- gate_up_weight: bfloat16 [2560, 15360], P('fsdp'), may hold values from -0.125 to 0.125
- down_weight: bfloat16 [7680, 2560], P('fsdp'), may hold values from -0.125 to 0.125
Outputs:
- result: bfloat16 [4, 1024, 2560], P('fsdp', 'ctx')
- input_grad: bfloat16 [4, 1024, 2560], P('fsdp', 'ctx')
- norm_one_grad: float32 [2560], P(('ctx', 'fsdp'))
- query_grad: float32 [2560, 2560], P('ctx', 'fsdp')
- keyval_grad: float32 [2560, 512], P('ctx', 'fsdp')
- out_grad: float32 [2560, 2560], P('ctx', 'fsdp')
- norm_two_grad: float32 [2560], P(('ctx', 'fsdp'))
- gate_up_grad: float32 [2560, 15360], P('ctx', 'fsdp')
- down_grad: float32 [7680, 2560], P('ctx', 'fsdp')
Inputs may be any that keep to these rules, and one draw needn't show every extreme that they name: `doc_bounds`: row s holds a and b: its documents are tokens [0, a), [a, b) and [b, 1024), with 1 <= a < 128 and 896 < b < 1024.
All inputs are finite; a program needn't handle non-finite values.
Results may differ from a plain program's by a relative error of at most 0.022.
Values may be sent and summed in bfloat16 or wider, within the bound.
A program may use at most 576 MiB of HBM per device.

v0:
```python
import jax
import jax.numpy as jnp
from jax import lax
from jax.sharding import PartitionSpec as P

HD = 256
WINDOW = 2048


epsilon = 1e-06


def passed_along(value, axis, by):
    length = lax.axis_size(axis)
    pairs = [(i, i + by) for i in range(length) if 0 <= i + by < length]
    return lax.ppermute(value, axis, pairs)


def rms_norm(values, gain):
    return values * lax.rsqrt(jnp.mean(values * values, axis=-1, keepdims=True) + epsilon) * gain


def frequencies(quarter):
    return 10000.0 ** (-jnp.arange(quarter, dtype=jnp.float32) / quarter)


def rotate(values, angles):
    quarter = angles.shape[-1]
    cosine = jnp.cos(angles)[:, None, :]
    sine = jnp.sin(angles)[:, None, :]
    former = values[..., :quarter]
    latter = values[..., quarter : 2 * quarter]
    return jnp.concatenate(
        [
            former * cosine - latter * sine,
            latter * cosine + former * sine,
            values[..., 2 * quarter :],
        ],
        axis=-1,
    )


def documents(index, bounds):
    return (index >= bounds[0]).astype(jnp.int32) + (index >= bounds[1]).astype(jnp.int32)


def rotary_angles(index, bounds):
    member = documents(index, bounds)
    opening = jnp.where(member == 0, 0, jnp.where(member == 1, bounds[0], bounds[1]))
    return (index - opening).astype(jnp.float32)[:, None] * frequencies(HD // 4)[None, :]


def visible(query_index, key_index, bounds):
    apart = query_index[:, None] - key_index[None, :]
    same_doc = documents(query_index, bounds)[:, None] == documents(key_index, bounds)[None, :]
    return (apart >= 0) & (apart < WINDOW) & (key_index[None, :] >= 0) & same_doc


def contract_rows(left, right):
    return lax.dot_general(
        left, right, (((1,), (1,)), ((), ())), preferred_element_type=jnp.float32
    )


def contract_tokens(left, right):
    return lax.dot_general(
        left, right, (((0,), (0,)), ((), ())), preferred_element_type=jnp.float32
    )


def gelu_product(gate_part, up_part):
    return jax.nn.gelu(gate_part, approximate=True) * up_part


def per_device(
    tokens,
    doc_bounds,
    cotangent,
    norm_one,
    query_weight,
    keyval_weight,
    out_weight,
    norm_two,
    gate_up_weight,
    down_weight,
):
    seq_rows = tokens.shape[1]
    inner_width = query_weight.shape[1]
    head_count = inner_width // HD
    hidden_width = gate_up_weight.shape[1] // 2
    reach_blocks = (WINDOW - 1) // seq_rows + 1
    key_span = (reach_blocks + 1) * seq_rows
    ctx_place = lax.axis_index("ctx")
    source = tokens[0].astype(jnp.float32)
    bounds = doc_bounds[0]
    query_index = ctx_place * seq_rows + jnp.arange(seq_rows, dtype=jnp.int32)
    key_index = (ctx_place - reach_blocks) * seq_rows + jnp.arange(key_span, dtype=jnp.int32)
    allowed = visible(query_index, key_index, bounds)
    angles = rotary_angles(query_index, bounds)
    w_query, w_keyval, w_out = (
        lax.all_gather(query_weight, "fsdp", axis=0, tiled=True),
        lax.all_gather(keyval_weight, "fsdp", axis=0, tiled=True),
        lax.all_gather(out_weight, "fsdp", axis=0, tiled=True),
    )
    normed_full, norm_back_one = jax.vjp(rms_norm, source, norm_one)
    normed = normed_full.astype(jnp.bfloat16)
    query_linear = jnp.dot(normed, w_query, preferred_element_type=jnp.float32)
    keyval_linear = jnp.dot(normed, w_keyval, preferred_element_type=jnp.float32)

    def shape_heads(query_part, keyval_part):
        query_rot = rotate(query_part.reshape(seq_rows, head_count, HD), angles) * HD ** (-0.5)
        key_rot = rotate(keyval_part[:, None, :HD], angles)[:, 0]
        return (query_rot, jnp.concatenate([key_rot, keyval_part[:, HD:]], axis=1))

    (queries_full, keyval_full), shape_back = jax.vjp(shape_heads, query_linear, keyval_linear)
    queries = queries_full.astype(jnp.bfloat16)
    keyval = keyval_full.astype(jnp.bfloat16)

    def pass_on(counter, carried):
        moving, stacked = carried
        moving = passed_along(moving, "ctx", 1)
        stacked = lax.dynamic_update_slice_in_dim(
            stacked, moving[None], reach_blocks - 1 - counter, 0
        )
        return (moving, stacked)

    stacked = (
        jnp.zeros((reach_blocks + 1, seq_rows, 2 * HD), jnp.bfloat16).at[reach_blocks].set(keyval)
    )
    moving, stacked = lax.fori_loop(0, reach_blocks, pass_on, (keyval, stacked))
    window = stacked.reshape(key_span, 2 * HD)
    key_rows = window[:, :HD]
    value_rows = window[:, HD:]
    scores = jnp.einsum("thd,kd->htk", queries, key_rows, preferred_element_type=jnp.float32)
    scores = jnp.where(allowed[None], scores, -1e30)
    peak_score = jnp.max(scores, axis=-1, keepdims=True)
    weights = jnp.exp(scores - peak_score)
    denominator = jnp.sum(weights, axis=-1, keepdims=True)
    weights = weights / denominator
    log_total = peak_score + jnp.log(denominator)
    mixed = jnp.einsum(
        "htk,kd->thd", weights.astype(jnp.bfloat16), value_rows, preferred_element_type=jnp.float32
    )
    mixed = mixed.reshape(seq_rows, inner_width).astype(jnp.bfloat16)
    middle = source + jnp.dot(mixed, w_out, preferred_element_type=jnp.float32)
    normed_two_full, norm_back_two = jax.vjp(rms_norm, middle, norm_two)
    normed_two = normed_two_full.astype(jnp.bfloat16)
    columns = normed_two
    projected = jnp.dot(
        columns,
        lax.all_gather(gate_up_weight, "fsdp", axis=0, tiled=True),
        preferred_element_type=jnp.float32,
    )
    hidden_full, gelu_back = jax.vjp(
        gelu_product, projected[:, :hidden_width], projected[:, hidden_width:]
    )
    hidden = hidden_full.astype(jnp.bfloat16)
    columns = hidden
    branch_two = jnp.dot(
        columns,
        lax.all_gather(down_weight, "fsdp", axis=0, tiled=True),
        preferred_element_type=jnp.float32,
    )
    result = (middle + branch_two).astype(jnp.bfloat16)
    grad_last = cotangent[0]
    grad_top = grad_last.astype(jnp.float32)
    grad_hidden = contract_rows(grad_last, lax.all_gather(down_weight, "fsdp", axis=0, tiled=True))
    columns = hidden
    down_part = lax.psum_scatter(
        contract_tokens(columns, grad_last).astype(jnp.bfloat16),
        "ctx",
        scatter_dimension=0,
        tiled=True,
    )
    grad_gate, grad_up = gelu_back(grad_hidden)
    grad_gate_up = jnp.concatenate([grad_gate, grad_up], axis=1).astype(jnp.bfloat16)
    grad_normed_two = contract_rows(
        grad_gate_up, lax.all_gather(gate_up_weight, "fsdp", axis=0, tiled=True)
    )
    columns = normed_two
    gate_up_part = lax.psum_scatter(
        contract_tokens(columns, grad_gate_up).astype(jnp.bfloat16),
        "ctx",
        scatter_dimension=0,
        tiled=True,
    )
    grad_middle_norm, gain_two_term = norm_back_two(grad_normed_two)
    grad_middle = grad_top + grad_middle_norm
    grad_branch = grad_middle.astype(jnp.bfloat16)
    back_query, back_keyval, back_out = (
        lax.all_gather(query_weight, "fsdp", axis=0, tiled=True),
        lax.all_gather(keyval_weight, "fsdp", axis=0, tiled=True),
        lax.all_gather(out_weight, "fsdp", axis=0, tiled=True),
    )
    out_term = contract_tokens(mixed, grad_branch)
    grad_mixed = (
        contract_rows(grad_branch, back_out).astype(jnp.bfloat16).reshape(seq_rows, head_count, HD)
    )
    scores = jnp.einsum("thd,kd->htk", queries, key_rows, preferred_element_type=jnp.float32)
    weights = jnp.where(allowed[None], jnp.exp(scores - log_total), 0.0)
    grad_weights = jnp.einsum(
        "thd,kd->htk", grad_mixed, value_rows, preferred_element_type=jnp.float32
    )
    row_delta = jnp.sum(weights * grad_weights, axis=-1, keepdims=True)
    grad_scores = (weights * (grad_weights - row_delta)).astype(jnp.bfloat16)
    grad_queries = jnp.einsum(
        "htk,kd->thd", grad_scores, key_rows, preferred_element_type=jnp.float32
    )
    grad_keys = jnp.einsum("htk,thd->kd", grad_scores, queries, preferred_element_type=jnp.float32)
    grad_values = jnp.einsum(
        "htk,thd->kd", weights.astype(jnp.bfloat16), grad_mixed, preferred_element_type=jnp.float32
    )
    grad_window = jnp.concatenate([grad_keys, grad_values], axis=1)
    blocks = grad_window.reshape(reach_blocks + 1, seq_rows, 2 * HD)

    def return_step(counter, moving):
        return (
            passed_along(moving.astype(jnp.bfloat16), "ctx", -1).astype(moving.dtype)
            + blocks[counter]
        )

    own_grad = lax.fori_loop(1, reach_blocks + 1, return_step, blocks[0])
    grad_query_linear, grad_keyval_linear = shape_back((grad_queries, own_grad))
    grad_query = grad_query_linear.astype(jnp.bfloat16)
    grad_keyval = grad_keyval_linear.astype(jnp.bfloat16)
    grad_normed = contract_rows(grad_query, back_query) + contract_rows(grad_keyval, back_keyval)
    grad_source_norm, gain_one_term = norm_back_one(grad_normed)
    input_grad = (grad_middle + grad_source_norm).astype(jnp.bfloat16)
    query_term = contract_tokens(normed, grad_query)
    keyval_term = contract_tokens(normed, grad_keyval)
    gain_one_part, query_part, keyval_part, out_part, gain_two_part = (
        lax.psum_scatter(
            gain_one_term.astype(jnp.bfloat16), "ctx", scatter_dimension=0, tiled=True
        ).astype(jnp.float32),
        lax.psum_scatter(
            query_term.astype(jnp.bfloat16), "ctx", scatter_dimension=0, tiled=True
        ).astype(jnp.float32),
        lax.psum_scatter(
            keyval_term.astype(jnp.bfloat16), "ctx", scatter_dimension=0, tiled=True
        ).astype(jnp.float32),
        lax.psum_scatter(
            out_term.astype(jnp.bfloat16), "ctx", scatter_dimension=0, tiled=True
        ).astype(jnp.float32),
        lax.psum_scatter(
            gain_two_term.astype(jnp.bfloat16), "ctx", scatter_dimension=0, tiled=True
        ).astype(jnp.float32),
    )
    gain_one_grad, query_grad, keyval_grad, out_grad, gain_two_grad, gate_up_grad, down_grad = (
        lax.psum_scatter(
            gain_one_part.astype(jnp.bfloat16), "fsdp", scatter_dimension=0, tiled=True
        ).astype(jnp.float32),
        lax.psum_scatter(
            query_part.astype(jnp.bfloat16), "fsdp", scatter_dimension=1, tiled=True
        ).astype(jnp.float32),
        lax.psum_scatter(
            keyval_part.astype(jnp.bfloat16), "fsdp", scatter_dimension=1, tiled=True
        ).astype(jnp.float32),
        lax.psum_scatter(
            out_part.astype(jnp.bfloat16), "fsdp", scatter_dimension=1, tiled=True
        ).astype(jnp.float32),
        lax.psum_scatter(
            gain_two_part.astype(jnp.bfloat16), "fsdp", scatter_dimension=0, tiled=True
        ).astype(jnp.float32),
        lax.psum_scatter(gate_up_part, "fsdp", scatter_dimension=1, tiled=True).astype(jnp.float32),
        lax.psum_scatter(down_part, "fsdp", scatter_dimension=1, tiled=True).astype(jnp.float32),
    )
    return (
        result[None],
        input_grad[None],
        gain_one_grad,
        query_grad,
        keyval_grad,
        out_grad,
        gain_two_grad,
        gate_up_grad,
        down_grad,
    )


def solution(mesh):
    placed = (
        P("fsdp", "ctx", None),
        P("fsdp", None),
        P("fsdp", "ctx", None),
        P(),
        P("fsdp", None),
        P("fsdp", None),
        P("fsdp", None),
        P(),
        P("fsdp", None),
        P("fsdp", None),
    )
    return jax.shard_map(
        per_device,
        mesh=mesh,
        in_specs=placed,
        out_specs=(
            P("fsdp", "ctx", None),
            P("fsdp", "ctx", None),
            P(("ctx", "fsdp")),
            P("ctx", "fsdp"),
            P("ctx", "fsdp"),
            P("ctx", "fsdp"),
            P(("ctx", "fsdp")),
            P("ctx", "fsdp"),
            P("ctx", "fsdp"),
        ),
        check_vma=False,
    )
```

profile of v0, /device:TPU:4, one launch (start us, length us, event | category | flops | bytes accessed | tf_op | source)
XLA Modules:
  0.0 3779.9 jit_solution(12077389134438665676)
XLA Ops:
  17.6 18.8 all-gather.6.cloned.1.call-done
  40.8 82.3 %all-gather.8.cloned.1.call-done = bf16[2560,2560]{1,0:T(8,128)(2,1)} async-done(((bf16[640,2560]{1,0:T(8,128)(2,1)}), bf16[2560,2560]{1,0:T(8,128)(2,1)}) %all-gather.8.cloned.1.call-update) | async-done | bytes 13107216 | tf_op jit(solution)/shard_map/all_gather | solution.py:101
  123.1 18.4 copy.46
  141.5 9.1 fusion.57
  151.0 138.0 %while.31 = (s32[]{:T(128)}, bf16[128,512]{1,0:T(8,128)(2,1)S(1)}, bf16[17,128,512]{2,1,0:T(8,128)(2,1)}, s32[]{:T(128)}, s32[]{:T(128)}, /*index=5*/s32[]{:T(128)}, s32[]{:T(128)}) while((s32[]{:T(128)}, bf16[128,512]{1,0:T(8,128)(2,1)S(1)}, bf16[17,128,512]{2,1,0:T(8,128)(2,1)}, s32[]{:T(128)}, s32[]{:T(128)}, /*index=5*/s32[]{:T(128)}, ...), condition=%wide.region_2.3_spmd, body=%wide.region_1.2_spmd.sunk | while | flops 6 | bytes 1048751 | solution.py:130
  299.4 7.2 multiply_reduce_fusion.2
  307.3 363.0 %all-gather.12.cloned.1.call-done = bf16[2560,15360]{1,0:T(8,128)(2,1)} async-done(((bf16[640,15360]{1,0:T(8,128)(2,1)}), bf16[2560,15360]{1,0:T(8,128)(2,1)}) %all-gather.12.cloned.1.call-update) | async-done | bytes 78643216 | tf_op jit(solution)/shard_map/all_gather | solution.py:151
  670.2 43.1 %fusion.96 = f32[128,15360]{1,0:T(8,128)} fusion(bf16[2560,15360]{1,0:T(8,128)(2,1)} %all-gather.12.cloned.1.call-done, f32[128,2560]{1,0:T(8,128)S(1)} %get-tuple-element.226, f32[2560]{0:T(1024)S(1)} %copy-done.9, f32[128]{0:T(128)S(1)} %fusion.87), kind=kOutput, calls=%fused_computation.162 | convolution fusion | flops 10067312640 | bytes 87828992 | tf_op jit(solution)/shard_map/dot_general | solution.py:149
  713.4 194.2 %all-gather.14.cloned.1.call-done = bf16[7680,2560]{1,0:T(8,128)(2,1)} async-done(((bf16[1920,2560]{1,0:T(8,128)(2,1)}), bf16[7680,2560]{1,0:T(8,128)(2,1)}) %all-gather.14.cloned.1.call-update) | async-done | bytes 39321616 | tf_op jit(solution)/shard_map/all_gather | solution.py:161
  907.6 24.8 fusion.25
  932.4 34.3 multiply_reduce_fusion
  968.7 9.9 convolution_convert_fusion.5
  980.8 6.2 fusion.16
  987.0 6.2 fusion
  1005.4 5.7 copy.58
  1012.2 167.6 %while.32 = (s32[]{:T(128)}, f32[128,512]{1,0:T(8,128)S(1)}, f32[17,128,512]{2,1,0:T(8,128)}, s32[]{:T(128)}, s32[]{:T(128)}, /*index=5*/s32[]{:T(128)}) while((s32[]{:T(128)}, f32[128,512]{1,0:T(8,128)S(1)}, f32[17,128,512]{2,1,0:T(8,128)}, s32[]{:T(128)}, s32[]{:T(128)}, /*index=5*/s32[]{:T(128)}) %tuple.125), condition=%wide.region_9.10_spmd, body=%wide.region_8.9_spmd.sunk | while | flops 196613 | bytes 2097327 | solution.py:222
  1015.3 6.2 collective-permute-done.1
  1025.8 6.0 collective-permute-done.1
  1036.1 6.0 collective-permute-done.1
  1046.5 6.0 collective-permute-done.1
  1056.8 6.0 collective-permute-done.1
  1067.1 6.0 collective-permute-done.1
  1077.4 6.0 collective-permute-done.1
  1087.7 6.7 collective-permute-done.1
  1098.7 7.0 collective-permute-done.1
  1110.0 6.2 collective-permute-done.1
  1120.5 6.0 collective-permute-done.1
  1130.9 6.0 collective-permute-done.1
  1141.2 6.0 collective-permute-done.1
  1151.5 6.0 collective-permute-done.1
  1161.8 6.0 collective-permute-done.1
  1172.1 6.0 collective-permute-done.1
  1183.5 7.9 convolution_convert_fusion.2
  1200.7 7.8 convolution_convert_fusion.3
  1209.0 18.0 convolution_convert_fusion.1
  1227.6 31.4 convolution_convert_fusion
  1261.1 209.1 %reduce-scatter.23.cloned.1.call-done = bf16[320,2560]{1,0:T(8,128)(2,1)} async-done(((bf16[2560,2560]{1,0:T(8,128)(2,1)}), bf16[320,2560]{1,0:T(8,128)(2,1)}) %reduce-scatter.23.cloned.1.call-update) | async-done | bytes 1638416 | tf_op jit(solution)/shard_map/reduce_scatter | solution.py:241
  1474.1 213.5 %reduce-scatter.19.cloned.1.call-done = bf16[320,2560]{1,0:T(8,128)(2,1)} async-done(((bf16[2560,2560]{1,0:T(8,128)(2,1)}), bf16[320,2560]{1,0:T(8,128)(2,1)}) %reduce-scatter.19.cloned.1.call-update) | async-done | bytes 1638416 | tf_op jit(solution)/shard_map/reduce_scatter | solution.py:235
  1691.5 624.9 %reduce-scatter.29.cloned.1.call-done = bf16[960,2560]{1,0:T(8,128)(2,1)} async-done(((bf16[7680,2560]{1,0:T(8,128)(2,1)}), bf16[960,2560]{1,0:T(8,128)(2,1)}) %reduce-scatter.29.cloned.1.call-update) | async-done | bytes 4915216 | tf_op jit(solution)/shard_map/reduce_scatter | solution.py:169
  2316.4 7.9 copy.77
  2324.3 1216.2 %reduce-scatter.25.cloned.1.call-done = bf16[320,15360]{1,0:T(8,128)(2,1)} async-done(((bf16[2560,15360]{1,0:T(8,128)(2,1)}), bf16[320,15360]{1,0:T(8,128)(2,1)}) %reduce-scatter.25.cloned.1.call-update) | async-done | bytes 9830416 | tf_op jit(solution)/shard_map/reduce_scatter | solution.py:181
  3543.7 9.5 fusion.101
  3555.4 31.0 all-reduce.13
  3586.6 6.2 all-reduce.14
  3596.6 16.6 fusion.27
  3617.1 14.3 reduce-scatter.31.cloned.1.call-done
  3633.6 51.6 %reduce-scatter.37.cloned.1.call-done = bf16[640,960]{1,0:T(8,128)(2,1)} async-done(((bf16[2560,960]{1,0:T(8,128)(2,1)}), bf16[640,960]{1,0:T(8,128)(2,1)}) %reduce-scatter.37.cloned.1.call-update) | async-done | bytes 1228816
  3689.0 80.0 %reduce-scatter.27.cloned.1.call-done = bf16[320,3840]{1,0:T(8,128)(2,1)} async-done(((bf16[320,15360]{1,0:T(8,128)(2,1)}), bf16[320,3840]{1,0:T(8,128)(2,1)}) %reduce-scatter.27.cloned.1.call-update) | async-done | bytes 2457616 | tf_op jit(solution)/shard_map/reduce_scatter | solution.py:264
  (328 shorter events, 294.7 us)
Async XLA Ops:
  7.2 29.2 all-gather.6.cloned.1.call-start
  7.9 115.1 %all-gather.8.cloned.1.call-start = ((), (), s32[]{:S(2)}) async-start(), calls=%async_computation.11 | async-start | bytes 16384000 | tf_op jit(solution)/shard_map/all_gather | solution.py:101
  8.7 290.7 %all-gather.10.cloned.1.call-start = ((), (), s32[]{:S(2)}) async-start(), calls=%async_computation.12 | async-start | bytes 16384000 | tf_op jit(solution)/shard_map/all_gather | solution.py:103
  9.4 660.8 %all-gather.12.cloned.1.call-start = ((), (), s32[]{:S(2)}) async-start(), calls=%async_computation.13 | async-start | bytes 98304000 | tf_op jit(solution)/shard_map/all_gather | solution.py:151
  10.0 897.6 %all-gather.14.cloned.1.call-start = ((), (), s32[]{:S(2)}) async-start(), calls=%async_computation.14 | async-start | bytes 49152000 | tf_op jit(solution)/shard_map/all_gather | solution.py:161
  10.6 1248.5 %reduce-scatter.21.cloned.1.call-start = ((), (), s32[]{:S(2)}) async-start(), calls=%async_computation.16 | async-start | bytes 2949120 | tf_op jit(solution)/shard_map/reduce_scatter | solution.py:238
  151.0 7.5 collective-permute-start
  159.2 6.8 collective-permute-start
  166.8 7.7 collective-permute-start
  175.1 7.7 collective-permute-start
  183.5 7.7 collective-permute-start
  192.0 7.9 collective-permute-start
  200.6 9.1 collective-permute-start
  210.4 8.3 collective-permute-start
  219.3 7.8 collective-permute-start
  227.8 7.7 collective-permute-start
  236.2 7.7 collective-permute-start
  244.7 7.7 collective-permute-start
  253.1 8.1 collective-permute-start
  261.9 9.0 collective-permute-start
  271.6 7.8 collective-permute-start
  280.1 7.7 collective-permute-start
  306.6 625.7 %copy-start.25 = (f32[128]{0:T(128)}, f32[128]{0:T(128)S(1)}, u32[]{:S(2)}) copy-start(f32[128]{0:T(128)S(1)} %fusion.87) | copy-start | bytes 1540
  1012.9 8.7 collective-permute-start.1
  1023.9 8.0 collective-permute-start.1
  1034.2 8.0 collective-permute-start.1
  1044.5 8.0 collective-permute-start.1
  1054.8 8.0 collective-permute-start.1
  1065.2 8.0 collective-permute-start.1
  1075.5 8.0 collective-permute-start.1
  1085.8 8.6 collective-permute-start.1
  1096.8 8.9 collective-permute-start.1
  1108.1 8.2 collective-permute-start.1
  1118.6 8.0 collective-permute-start.1
  1128.9 8.0 collective-permute-start.1
  1139.2 8.0 collective-permute-start.1
  1149.6 8.0 collective-permute-start.1
  1159.9 8.0 collective-permute-start.1
  1170.2 8.0 collective-permute-start.1
  1183.5 286.8 %reduce-scatter.23.cloned.1.call-start = ((), (), s32[]{:S(2)}) async-start(), calls=%async_computation.17 | async-start | bytes 14745600 | tf_op jit(solution)/shard_map/reduce_scatter | solution.py:241
  1191.4 496.1 %reduce-scatter.19.cloned.1.call-start = ((), (), s32[]{:S(2)}) async-start(), calls=%async_computation.15 | async-start | bytes 14745600 | tf_op jit(solution)/shard_map/reduce_scatter | solution.py:235
  1208.5 1107.9 %reduce-scatter.29.cloned.1.call-start = ((), (), s32[]{:S(2)}) async-start(), calls=%async_computation.20 | async-start | bytes 44236800 | tf_op jit(solution)/shard_map/reduce_scatter | solution.py:169
  1227.0 2313.6 %reduce-scatter.25.cloned.1.call-start = ((), (), s32[]{:S(2)}) async-start(), calls=%async_computation.18 | async-start | bytes 88473600 | tf_op jit(solution)/shard_map/reduce_scatter | solution.py:181
  1259.0 2354.2 %reduce-scatter.33.cloned.1.call-start = ((), (), s32[]{:S(2)}) async-start(), calls=%async_computation.22 | async-start | bytes 491520
  1261.0 2353.9 %reduce-scatter.35.cloned.1.call-start = ((), (), s32[]{:S(2)}) async-start(), calls=%async_computation.23 | async-start | bytes 2457600
  1474.1 2157.4 %reduce-scatter.31.cloned.1.call-start = ((), (), s32[]{:S(2)}) async-start(), calls=%async_computation.21 | async-start | bytes 2457600
  1691.4 1993.8 %reduce-scatter.37.cloned.1.call-start = ((), (), s32[]{:S(2)}) async-start(), calls=%async_computation.24 | async-start | bytes 6553600
  2324.3 1444.7 %reduce-scatter.27.cloned.1.call-start = ((), (), s32[]{:S(2)}) async-start(), calls=%async_computation.19 | async-start | bytes 12288000 | tf_op jit(solution)/shard_map/reduce_scatter | solution.py:264
  (57 other events, 2027.6 us)
Sparse Core Ops, SparseCore 0:
  9.6 26.7 all-gather.5
  37.9 85.0 all-gather.7
  124.6 85.0 all-gather.9
  211.2 459.0 all-gather.11
  671.6 235.9 all-gather.13
  1183.6 68.9 reduce-scatter.20
  1256.2 213.9 reduce-scatter.22
  1473.9 213.6 reduce-scatter.18
  1691.5 624.8 reduce-scatter.28
  2320.6 1219.8 reduce-scatter.24
  3543.6 19.9 reduce-scatter.32
  3566.6 30.7 reduce-scatter.34
  3600.7 30.6 reduce-scatter.30
  3633.8 51.3 reduce-scatter.36
  3687.9 81.0 reduce-scatter.26
where the time goes:
time: 3790 us; the launch traced here: 3780 us
  waiting for transfers between devices  3210 us (85%)
  matrix products  254 us (7%)
  starting transfers between devices  113 us (3%)
  local copies, waits for them, and re-layouts  80 us (2%)
  other arithmetic  62.5 us (2%)
    reduce_scatter x1, waiting for transfers between devices, per_device(): lax.psum_scatter(contract_tokens(columns, grad_gate_up).astype(jnp.bfloat...  1220 us
    reduce_scatter x1, waiting for transfers between devices, per_device(): lax.psum_scatter(contract_tokens(columns, grad_last).astype(jnp.bfloat16)...  625 us
    all_gather x1, waiting for transfers between devices, per_device(): lax.all_gather(gate_up_weight, 'fsdp', axis=0, tiled=True)  363 us
    reduce_scatter x1, waiting for transfers between devices, per_device(): lax.psum_scatter(query_term.astype(jnp.bfloat16), 'ctx', scatter_dimensio...  213 us
    reduce_scatter x1, waiting for transfers between devices, per_device(): lax.psum_scatter(out_term.astype(jnp.bfloat16), 'ctx', scatter_dimension=...  209 us
    all_gather x1, waiting for transfers between devices, per_device(): lax.all_gather(down_weight, 'fsdp', axis=0, tiled=True)  194 us
    ppermute x32, waiting for transfers between devices, passed_along(): return lax.ppermute(value, axis, pairs)  144 us
    ppermute x32, starting transfers between devices, passed_along(): return lax.ppermute(value, axis, pairs)  112 us
  transfers between devices with their start and end apart: 47, of which 43 were waited for; matrix products, arithmetic and copies ran while one was open for 6% of the time, Pallas kernels for 0%

commit v1 on v0

v1 whole, which is shorter than its diff:
```python
import jax
import jax.numpy as jnp
from jax import lax
from jax.sharding import PartitionSpec as P

HD = 256
WINDOW = 2048


epsilon = 1e-06


def rms_norm(values, gain):
    return values * lax.rsqrt(jnp.mean(values * values, axis=-1, keepdims=True) + epsilon) * gain


def frequencies(quarter):
    return 10000.0 ** (-jnp.arange(quarter, dtype=jnp.float32) / quarter)


def rotate(values, angles):
    quarter = angles.shape[-1]
    cosine = jnp.cos(angles)[:, None, :]
    sine = jnp.sin(angles)[:, None, :]
    former = values[..., :quarter]
    latter = values[..., quarter : 2 * quarter]
    return jnp.concatenate(
        [
            former * cosine - latter * sine,
            latter * cosine + former * sine,
            values[..., 2 * quarter :],
        ],
        axis=-1,
    )


def documents(index, bounds):
    return (index >= bounds[0]).astype(jnp.int32) + (index >= bounds[1]).astype(jnp.int32)


def rotary_angles(index, bounds):
    member = documents(index, bounds)
    opening = jnp.where(member == 0, 0, jnp.where(member == 1, bounds[0], bounds[1]))
    return (index - opening).astype(jnp.float32)[:, None] * frequencies(HD // 4)[None, :]


def visible(query_index, key_index, bounds):
    apart = query_index[:, None] - key_index[None, :]
    same_doc = documents(query_index, bounds)[:, None] == documents(key_index, bounds)[None, :]
    return (apart >= 0) & (apart < WINDOW) & (key_index[None, :] >= 0) & same_doc


def contract_rows(left, right):
    return lax.dot_general(
        left, right, (((1,), (1,)), ((), ())), preferred_element_type=jnp.float32
    )


def contract_tokens(left, right):
    return lax.dot_general(
        left, right, (((0,), (0,)), ((), ())), preferred_element_type=jnp.float32
    )


def gelu_product(gate_part, up_part):
    return jax.nn.gelu(gate_part, approximate=True) * up_part


def owner_block(weight, ctx_size, fsdp_size):
    block = weight.shape[0] * fsdp_size // ctx_size
    per_owner = ctx_size // fsdp_size
    ctx_place = lax.axis_index("ctx")
    fsdp_place = lax.axis_index("fsdp")
    part = lax.dynamic_slice_in_dim(weight, (ctx_place % per_owner) * block, block, 0)
    owner = ctx_place // per_owner
    half = fsdp_size // 2
    over = [
        (c * fsdp_size + c // per_owner, c * fsdp_size + (c // per_owner + half) % fsdp_size)
        for c in range(ctx_size)
    ]
    moved = lax.ppermute(part, ("ctx", "fsdp"), over)
    part = jnp.where(fsdp_place == owner, part, moved)
    twin = [
        (c * fsdp_size + g, c * fsdp_size + (g ^ 1))
        for c in range(ctx_size)
        for g in (c // per_owner, (c // per_owner + half) % fsdp_size)
    ]
    moved = lax.ppermute(part, ("ctx", "fsdp"), twin)
    return jnp.where(fsdp_place % half == owner % half, part, moved)


def per_device(
    tokens,
    doc_bounds,
    cotangent,
    norm_one,
    query_weight,
    keyval_weight,
    out_weight,
    norm_two,
    gate_up_weight,
    down_weight,
):
    ctx_size = lax.axis_size("ctx")
    fsdp_size = lax.axis_size("fsdp")
    rows = tokens.shape[1]
    width = tokens.shape[2]
    length = rows * ctx_size
    inner_width = query_weight.shape[1]
    head_count = inner_width // HD
    hidden_width = gate_up_weight.shape[1] // 2
    part_width = hidden_width // ctx_size
    ctx_place = lax.axis_index("ctx")
    source = tokens[0].astype(jnp.float32)
    bounds = doc_bounds[0]
    query_index = ctx_place * rows + jnp.arange(rows, dtype=jnp.int32)
    key_index = jnp.arange(length, dtype=jnp.int32)
    allowed = visible(query_index, key_index, bounds)
    angles = rotary_angles(query_index, bounds)

    gate_cols = lax.dynamic_slice_in_dim(gate_up_weight, ctx_place * part_width, part_width, 1)
    up_cols = lax.dynamic_slice_in_dim(
        gate_up_weight, hidden_width + ctx_place * part_width, part_width, 1
    )
    cot_rows = cotangent[0]
    cot_all = lax.all_gather(cot_rows, "ctx", axis=0, tiled=True)
    w_gate_up = lax.all_gather(
        jnp.concatenate([gate_cols, up_cols], axis=1), "fsdp", axis=0, tiled=True
    )
    w_down = owner_block(down_weight, ctx_size, fsdp_size)
    w_qkv = jnp.concatenate([query_weight, keyval_weight], axis=1)

    def spread(value):
        return lax.all_to_all(value, "fsdp", split_axis=1, concat_axis=0, tiled=True)

    def collect(value):
        return lax.all_to_all(value, "fsdp", split_axis=0, concat_axis=1, tiled=True)

    normed_full, norm_back_one = jax.vjp(rms_norm, source, norm_one)
    normed = spread(normed_full.astype(jnp.bfloat16))
    linear = lax.psum_scatter(
        jnp.dot(normed, w_qkv, preferred_element_type=jnp.float32).astype(jnp.bfloat16),
        "fsdp",
        scatter_dimension=0,
        tiled=True,
    ).astype(jnp.float32)

    def shape_heads(part):
        query_part, keyval_part = part[:, :inner_width], part[:, inner_width:]
        query_rot = rotate(query_part.reshape(rows, head_count, HD), angles) * HD ** (-0.5)
        key_rot = rotate(keyval_part[:, None, :HD], angles)[:, 0]
        return (query_rot, jnp.concatenate([key_rot, keyval_part[:, HD:]], axis=1))

    (queries_full, keyval_full), shape_back = jax.vjp(shape_heads, linear)
    queries = queries_full.astype(jnp.bfloat16)
    window = lax.all_gather(keyval_full.astype(jnp.bfloat16), "ctx", axis=0, tiled=True)
    key_rows = window[:, :HD]
    value_rows = window[:, HD:]
    scores = jnp.einsum("thd,kd->htk", queries, key_rows, preferred_element_type=jnp.float32)
    scores = jnp.where(allowed[None], scores, -1e30)
    peak_score = jnp.max(scores, axis=-1, keepdims=True)
    weights = jnp.exp(scores - peak_score)
    denominator = jnp.sum(weights, axis=-1, keepdims=True)
    weights = weights / denominator
    log_total = peak_score + jnp.log(denominator)
    mixed = jnp.einsum(
        "htk,kd->thd", weights.astype(jnp.bfloat16), value_rows, preferred_element_type=jnp.float32
    )
    mixed = spread(mixed.reshape(rows, inner_width).astype(jnp.bfloat16))
    middle = source + lax.psum_scatter(
        jnp.dot(mixed, out_weight, preferred_element_type=jnp.float32).astype(jnp.bfloat16),
        "fsdp",
        scatter_dimension=0,
        tiled=True,
    ).astype(jnp.float32)
    normed_two_full, norm_back_two = jax.vjp(rms_norm, middle, norm_two)
    normed_two = lax.all_gather(
        normed_two_full.astype(jnp.bfloat16), "ctx", axis=0, tiled=True
    )
    projected = jnp.dot(normed_two, w_gate_up, preferred_element_type=jnp.float32)
    hidden_full, gelu_back = jax.vjp(
        gelu_product, projected[:, :part_width], projected[:, part_width:]
    )
    hidden = hidden_full.astype(jnp.bfloat16)
    grad_hidden = contract_rows(cot_all, w_down)
    grad_gate, grad_up = gelu_back(grad_hidden)
    grad_gate_up = jnp.concatenate([grad_gate, grad_up], axis=1).astype(jnp.bfloat16)
    grad_normed_two = lax.psum_scatter(
        contract_rows(grad_gate_up, w_gate_up).astype(jnp.bfloat16),
        "ctx",
        scatter_dimension=0,
        tiled=True,
    ).astype(jnp.float32)
    branch_two = lax.psum_scatter(
        jnp.dot(hidden, w_down, preferred_element_type=jnp.float32).astype(jnp.bfloat16),
        "ctx",
        scatter_dimension=0,
        tiled=True,
    ).astype(jnp.float32)
    result = (middle + branch_two).astype(jnp.bfloat16)

    down_grad = lax.psum_scatter(
        contract_tokens(hidden, cot_all).astype(jnp.bfloat16),
        "fsdp",
        scatter_dimension=1,
        tiled=True,
    ).astype(jnp.float32)
    gate_up_part = lax.psum_scatter(
        contract_tokens(normed_two, grad_gate_up).astype(jnp.bfloat16),
        "fsdp",
        scatter_dimension=1,
        tiled=True,
    )
    gate_up_part = lax.all_to_all(
        gate_up_part.reshape(ctx_size, width // ctx_size, -1), "ctx", 0, 0, tiled=True
    )
    core = lax.axis_index("fsdp") % 2
    gate_up_part = gate_up_part.reshape((2, ctx_size // 2) + gate_up_part.shape[1:])
    kept = lax.dynamic_index_in_dim(gate_up_part, core, 0, keepdims=False)
    given = lax.dynamic_index_in_dim(gate_up_part, 1 - core, 0, keepdims=False)
    taken = lax.ppermute(given, "fsdp", [(i, i ^ 1) for i in range(fsdp_size)])
    halves = jnp.where(core == 0, jnp.stack([kept, taken], 2), jnp.stack([taken, kept], 2))
    gate_up_grad = (
        halves.transpose(1, 0, 2, 3).reshape(width // ctx_size, -1).astype(jnp.float32)
    )

    grad_middle_norm, gain_two_term = norm_back_two(grad_normed_two)
    grad_middle = cot_rows.astype(jnp.float32) + grad_middle_norm
    grad_branch = lax.all_gather(grad_middle.astype(jnp.bfloat16), "fsdp", axis=0, tiled=True)
    grad_mixed = collect(contract_rows(grad_branch, out_weight).astype(jnp.bfloat16))
    grad_mixed = grad_mixed.reshape(rows, head_count, HD)

    scores = jnp.einsum("thd,kd->htk", queries, key_rows, preferred_element_type=jnp.float32)
    weights = jnp.where(allowed[None], jnp.exp(scores - log_total), 0.0)
    grad_weights = jnp.einsum(
        "thd,kd->htk", grad_mixed, value_rows, preferred_element_type=jnp.float32
    )
    row_delta = jnp.sum(weights * grad_weights, axis=-1, keepdims=True)
    grad_scores = (weights * (grad_weights - row_delta)).astype(jnp.bfloat16)
    grad_queries = jnp.einsum(
        "htk,kd->thd", grad_scores, key_rows, preferred_element_type=jnp.float32
    )
    grad_keys = jnp.einsum("htk,thd->kd", grad_scores, queries, preferred_element_type=jnp.float32)
    grad_values = jnp.einsum(
        "htk,thd->kd", weights.astype(jnp.bfloat16), grad_mixed, preferred_element_type=jnp.float32
    )
    own_grad = lax.psum_scatter(
        jnp.concatenate([grad_keys, grad_values], axis=1).astype(jnp.bfloat16),
        "ctx",
        scatter_dimension=0,
        tiled=True,
    ).astype(jnp.float32)
    (grad_linear,) = shape_back((grad_queries, own_grad))
    grad_linear = lax.all_gather(grad_linear.astype(jnp.bfloat16), "fsdp", axis=0, tiled=True)
    grad_normed = collect(contract_rows(grad_linear, w_qkv).astype(jnp.bfloat16))
    grad_source_norm, gain_one_term = norm_back_one(grad_normed.astype(jnp.float32))
    input_grad = (grad_middle + grad_source_norm).astype(jnp.bfloat16)

    per_owner = ctx_size // fsdp_size

    def in_blocks(term):
        tall, wide = term.shape
        term = term.astype(jnp.bfloat16)
        term = term.reshape(per_owner, tall // per_owner, fsdp_size, wide // fsdp_size)
        return term.transpose(0, 2, 1, 3).reshape(ctx_size, tall // per_owner, wide // fsdp_size)

    def summed(blocks):
        block = lax.psum_scatter(blocks, "ctx", scatter_dimension=0, tiled=True)[0]
        pairs = [
            ((r * fsdp_size + g) * fsdp_size + f, (per_owner * f + r) * fsdp_size + g)
            for r in range(per_owner)
            for g in range(fsdp_size)
            for f in range(fsdp_size)
        ]
        return lax.ppermute(block, ("ctx", "fsdp"), pairs).astype(jnp.float32)

    out_grad = summed(in_blocks(contract_tokens(mixed, grad_branch)))
    qkv_term = contract_tokens(normed, grad_linear)
    qkv_block = summed(
        jnp.concatenate(
            [in_blocks(qkv_term[:, :inner_width]), in_blocks(qkv_term[:, inner_width:])], axis=2
        )
    )
    query_grad = qkv_block[:, : inner_width // fsdp_size]
    keyval_grad = qkv_block[:, inner_width // fsdp_size :]
    gains = lax.psum_scatter(
        jnp.stack([gain_one_term, gain_two_term]),
        ("ctx", "fsdp"),
        scatter_dimension=1,
        tiled=True,
    )
    return (
        result[None],
        input_grad[None],
        gains[0],
        query_grad,
        keyval_grad,
        out_grad,
        gains[1],
        gate_up_grad,
        down_grad,
    )


def solution(mesh):
    placed = (
        P("fsdp", "ctx", None),
        P("fsdp", None),
        P("fsdp", "ctx", None),
        P(),
        P("fsdp", None),
        P("fsdp", None),
        P("fsdp", None),
        P(),
        P("fsdp", None),
        P("fsdp", None),
    )
    return jax.shard_map(
        per_device,
        mesh=mesh,
        in_specs=placed,
        out_specs=(
            P("fsdp", "ctx", None),
            P("fsdp", "ctx", None),
            P(("ctx", "fsdp")),
            P("ctx", "fsdp"),
            P("ctx", "fsdp"),
            P("ctx", "fsdp"),
            P(("ctx", "fsdp")),
            P("ctx", "fsdp"),
            P("ctx", "fsdp"),
        ),
        check_vma=False,
    )
```

time: 3790 us -> 1400 us (0.37)
  waiting for transfers between devices: 3210 us -> 1030 us
  matrix products: 254 us -> 128 us
  starting transfers between devices: 113 us -> 31.7 us
    reduce_scatter x6 -> x8, waiting for transfers between devices: 2340 us -> 566 us  [the longest x2 194 us: summed(): block = lax.psum_scatter(blocks, 'ctx', scatter_dimension=0, tiled=True)[0]]
    all_gather x5 -> x6, waiting for transfers between devices: 658 us -> 169 us  [the longest x1 69.4 us: per_device(): cot_all = lax.all_gather(cot_rows, 'ctx', axis=0, tiled=True)]
    unnamed x19 -> x18, waiting for transfers between devices: 69.2 us -> 175 us
    ppermute x32 -> x5, starting transfers between devices: 112 us -> 12.6 us  [the longest x1 5.14 us: owner_block(): moved = lax.ppermute(part, ('ctx', 'fsdp'), over)]
    ppermute x32 -> x5, waiting for transfers between devices: 144 us -> 102 us  [the longest x1 102 us: owner_block(): moved = lax.ppermute(part, ('ctx', 'fsdp'), over)]
    dot_general x5 -> x4, matrix products: 80.7 us -> 39.5 us  [contract_rows(): lax.dot_general(left, right, (((1,), (1,)), ((), ())), preferred_element_...]
    dot_general x5 -> x4, matrix products: 78.3 us -> 37.2 us  [the longest x1 17.1 us: per_device(): jnp.dot(normed_two, w_gate_up, preferred_element_type=jnp.float32)]
  transfers between devices with their start and end apart: 47 -> 25, of which waited for: 43 -> 17; matrix products, arithmetic and copies ran while one was open for 6% -> 14% of each run, Pallas kernels for 0% -> 0%
where the time goes in v1:
time: 1400 us; the launch traced here: 1380 us
  waiting for transfers between devices  1030 us (74%)
  matrix products  128 us (9%)
  local copies, waits for them, and re-layouts  111 us (8%)
  other arithmetic  51.7 us (4%)
  starting transfers between devices  31.7 us (2%)
  between operations  14.8 us (1%)
    reduce_scatter x2, waiting for transfers between devices, summed(): block = lax.psum_scatter(blocks, 'ctx', scatter_dimension=0, tiled=True)[0]  194 us
    unnamed x18, waiting for transfers between devices  175 us
    reduce_scatter x1, waiting for transfers between devices, per_device(): lax.psum_scatter(jnp.dot(hidden, w_down, preferred_element_type=jnp.float...  120 us
    ppermute x1, waiting for transfers between devices, owner_block(): moved = lax.ppermute(part, ('ctx', 'fsdp'), over)  102 us
    reduce_scatter x1, waiting for transfers between devices, per_device(): lax.psum_scatter(contract_rows(grad_gate_up, w_gate_up).astype(jnp.bfloat...  102 us
    all_gather x1, waiting for transfers between devices, per_device(): cot_all = lax.all_gather(cot_rows, 'ctx', axis=0, tiled=True)  69.4 us
    reduce_scatter x1, waiting for transfers between devices, per_device(): lax.psum_scatter(jnp.concatenate([grad_keys, grad_values], axis=1).astype...  59.5 us
    all_gather x1, waiting for transfers between devices, per_device(): lax.all_gather(normed_two_full.astype(jnp.bfloat16), 'ctx', axis=0, tiled...  55.8 us
  transfers between devices with their start and end apart: 25, of which 17 were waited for; matrix products, arithmetic and copies ran while one was open for 14% of the time, Pallas kernels for 0%

profile of v1, /device:TPU:4, one launch (start us, length us, event | category | flops | bytes accessed | tf_op | source)
XLA Modules:
  0.0 1378.0 jit_solution(17867866968407596876)
XLA Ops:
  14.8 4.2 all-to-all-start
  19.0 3.9 constant_dynamic-update-slice_fusion.1
  23.9 5.4 all-to-all-done
  29.3 6.6 convolution_convert_fusion.7
  38.4 35.9 %reduce-scatter.15.cloned.1.call-done = bf16[128,3072]{1,0:T(8,128)(2,1)} async-done(((bf16[512,3072]{1,0:T(8,128)(2,1)}), bf16[128,3072]{1,0:T(8,128)(2,1)}) %reduce-scatter.15.cloned.1.call-update) | async-done | bytes 786448 | tf_op jit(solution)/shard_map/reduce_scatter | solution.py:141
  97.8 18.7 %all-gather.8.cloned.1.call-done = bf16[1024,512]{1,0:T(8,128)(2,1)} async-done(((bf16[128,512]{1,0:T(8,128)(2,1)}), bf16[1024,512]{1,0:T(8,128)(2,1)}) %all-gather.8.cloned.1.call-update) | async-done | bytes 1048592 | tf_op jit(solution)/shard_map/all_gather | solution.py:156
  125.7 13.7 all_to_all.66
  140.2 3.7 convolution_convert_fusion.6
  150.0 27.5 %reduce-scatter.17.cloned.1.call-done = bf16[128,2560]{1,0:T(8,128)(2,1)} async-done(((bf16[512,2560]{1,0:T(8,128)(2,1)}), bf16[128,2560]{1,0:T(8,128)(2,1)}) %reduce-scatter.17.cloned.1.call-update) | async-done | bytes 655376 | tf_op jit(solution)/shard_map/reduce_scatter | solution.py:170
  182.6 5.1 constant_dynamic-slice_fusion
  187.7 5.1 collective-permute-start
  193.0 102.1 %collective-permute-done = bf16[960,2560]{1,0:T(8,128)(2,1)} collective-permute-done((bf16[960,2560]{1,0:T(8,128)(2,1)}, bf16[960,2560]{1,0:T(8,128)(2,1)}, u32[]{:S(2)}, u32[]{:S(2)}) %collective-permute-start) | collective-permute-done | bytes 4915232 | tf_op jit(solution)/shard_map/ppermute | solution.py:81
  295.1 6.0 broadcast_select_fusion
  301.0 3.5 collective-permute-start.1
  304.5 55.8 %all-gather.10.cloned.1.call-done = bf16[1024,2560]{1,0:T(8,128)(2,1)} async-done(((bf16[128,2560]{1,0:T(8,128)(2,1)}), bf16[1024,2560]{1,0:T(8,128)(2,1)}) %all-gather.10.cloned.1.call-update) | async-done | bytes 5242896 | tf_op jit(solution)/shard_map/all_gather | solution.py:177
  360.3 17.1 %fusion.85 = f32[1024,1920]{1,0:T(8,128)} fusion(bf16[1024,2560]{1,0:T(8,128)(2,1)} %all-gather.10.cloned.1.call-done, bf16[2560,1920]{1,0:T(8,128)(2,1)} %all-gather.12.cloned.1.call-done), kind=kOutput, calls=%fused_computation.167 | convolution fusion | flops 10066329600 | bytes 22937600 | tf_op jit(solution)/shard_map/dot_general | solution.py:180
  377.4 69.4 %all-gather.18.cloned.1.call-done = bf16[1,1024,2560]{2,1,0:T(8,128)(2,1)} async-done(((bf16[1,128,2560]{2,1,0:T(8,128)(2,1)}), bf16[1,1024,2560]{2,1,0:T(8,128)(2,1)}) %all-gather.18.cloned.1.call-update) | async-done | bytes 5242896 | tf_op jit(solution)/shard_map/all_gather | solution.py:126
  446.9 13.7 fusion.16
  462.6 15.4 %convolution_convert_fusion.1 = bf16[1024,2560]{1,0:T(8,128)(2,1)} fusion(bf16[2560,1920]{1,0:T(8,128)(2,1)} %all-gather.12.cloned.1.call-done, bf16[1024,960]{1,0:T(8,128)(2,1)S(1)} %get-tuple-element.16, bf16[1024,960]{1,0:T(8,128)(2,1)S(1)} %get-tuple-element.15), kind=kOutput, calls=%fused_computation.3 | convolution fusion | flops 10076815360 | bytes 19005440 | tf_op jit(solution)/shard_map/dot_general | solution.py:54
  478.2 101.6 %reduce-scatter.21.cloned.1.call-done = bf16[128,2560]{1,0:T(8,128)(2,1)} async-done(((bf16[1024,2560]{1,0:T(8,128)(2,1)}), bf16[128,2560]{1,0:T(8,128)(2,1)}) %reduce-scatter.21.cloned.1.call-update) | async-done | bytes 655376 | tf_op jit(solution)/shard_map/reduce_scatter | solution.py:188
  586.8 25.5 %all-gather.14.cloned.1.call-done = bf16[512,2560]{1,0:T(8,128)(2,1)} async-done(((bf16[128,2560]{1,0:T(8,128)(2,1)}), bf16[512,2560]{1,0:T(8,128)(2,1)}) %all-gather.14.cloned.1.call-update) | async-done | bytes 2621456 | tf_op jit(solution)/shard_map/all_gather | solution.py:229
  612.3 4.8 convolution_convert_fusion.8
  619.2 3.5 all-to-all-start.2
  623.5 9.4 all-to-all-done.2
  632.9 3.5 fusion.44
  636.5 4.1 fusion
  648.8 59.5 %reduce-scatter.23.cloned.1.call-done = bf16[128,512]{1,0:T(8,128)(2,1)} async-done(((bf16[1024,512]{1,0:T(8,128)(2,1)}), bf16[128,512]{1,0:T(8,128)(2,1)}) %reduce-scatter.23.cloned.1.call-update) | async-done | bytes 131088 | tf_op jit(solution)/shard_map/reduce_scatter | solution.py:247
  711.8 17.6 %convolution_convert_fusion = bf16[2560,1920]{0,1:T(8,128)(2,1)} fusion(bf16[1024,2560]{1,0:T(8,128)(2,1)} %all-gather.10.cloned.1.call-done, bf16[1024,960]{1,0:T(8,128)(2,1)} %copy-done.38, bf16[1024,960]{1,0:T(8,128)(2,1)} %copy-done.37), kind=kOutput, calls=%fused_computation | convolution fusion | flops 10079109120 | bytes 19005440 | tf_op jit(solution)/shard_map/dot_general | solution.py:60
  731.5 3.7 convolution_convert_fusion.4
  735.1 5.6 reshape.337
  744.5 9.7 convolution_convert_fusion.3
  754.2 8.1 copy.139
  762.8 4.3 convolution_convert_fusion.5
  781.9 9.8 convolution_convert_fusion.2
  793.6 5.6 convolution_convert_fusion.9
  799.2 3.5 all-to-all-start.3
  802.7 27.8 %reduce-scatter.29.cloned.1.call-done = bf16[2560,480]{0,1:T(8,128)(2,1)} async-done(((bf16[2560,1920]{0,1:T(8,128)(2,1)}), bf16[2560,480]{0,1:T(8,128)(2,1)}) %reduce-scatter.29.cloned.1.call-update) | async-done | bytes 2457616 | tf_op jit(solution)/shard_map/reduce_scatter | solution.py:208
  830.4 4.3 copy.119
  834.8 6.1 all-to-all-start.4
  840.9 116.2 %reduce-scatter.27.cloned.1.call-done = bf16[1,320,640]{2,1,0:T(8,128)(2,1)} async-done(((bf16[8,320,640]{2,1,0:T(8,128)(2,1)}), bf16[1,320,640]{2,1,0:T(8,128)(2,1)}) %reduce-scatter.27.cloned.1.call-update) | async-done | bytes 409616 | tf_op jit(solution)/shard_map/reduce_scatter | solution.py:268
  959.0 51.3 %reduce-scatter.33.cloned.1.call-done = bf16[640,960]{1,0:T(8,128)(2,1)} async-done(((bf16[2560,960]{1,0:T(8,128)(2,1)}), bf16[640,960]{1,0:T(8,128)(2,1)}) %reduce-scatter.33.cloned.1.call-update) | async-done | bytes 1228816
  1017.4 3.5 dynamic-slice_bitcast_fusion.1
  1020.9 77.6 %reduce-scatter.25.cloned.1.call-done = bf16[1,320,768]{2,1,0:T(8,128)(2,1)} async-done(((bf16[8,320,768]{2,1,0:T(8,128)(2,1)}), bf16[1,320,768]{2,1,0:T(8,128)(2,1)}) %reduce-scatter.25.cloned.1.call-update) | async-done | bytes 491536 | tf_op jit(solution)/shard_map/reduce_scatter | solution.py:268
  1100.6 119.7 %reduce-scatter.19.cloned.1.call-done = bf16[128,2560]{1,0:T(8,128)(2,1)} async-done(((bf16[1024,2560]{1,0:T(8,128)(2,1)}), bf16[128,2560]{1,0:T(8,128)(2,1)}) %reduce-scatter.19.cloned.1.call-update) | async-done | bytes 655376 | tf_op jit(solution)/shard_map/reduce_scatter | solution.py:194
  1223.7 123.9 %reduce-scatter.31.cloned.1.call-done = f32[80,2]{1,0:T(8,128)} async-done(((f32[2560,2]{1,0:T(8,128)}), f32[80,2]{1,0:T(8,128)}) %reduce-scatter.31.cloned.1.call-update) | async-done | bytes 656
  1349.6 3.5 convert_bitcast_fusion
  1353.2 6.4 copy.120
  1359.5 8.2 reshape.344
  (211 shorter events, 122.2 us)
Async XLA Ops:
  7.2 133.1 %copy-start = (bf16[640,2560]{1,0:T(8,128)(2,1)S(1)}, bf16[640,2560]{1,0:T(8,128)(2,1)}, u32[]{:S(2)}) copy-start(bf16[640,2560]{1,0:T(8,128)(2,1)} %param.16) | copy-start | bytes 9830404
  11.2 11.7 copy-start.31
  14.8 14.5 %all-to-all-start = ((bf16[128,4,640]{2,0,1:T(8,128)(2,1)}), bf16[128,4,640]{2,0,1:T(8,128)(2,1)}, u32[]{:S(2)}, u32[]{:S(2)}) async-start(bf16[128,4,640]{2,0,1:T(8,128)(2,1)} %fusion.43), calls=%async_computation | async-start | bytes 1310720 | tf_op jit(solution)/shard_map/all_to_all | solution.py:134
  19.0 55.3 %reduce-scatter.15.cloned.1.call-start = ((), (), s32[]{:S(2)}) async-start(), calls=%async_computation.15 | async-start | bytes 3932160 | tf_op jit(solution)/shard_map/reduce_scatter | solution.py:141
  19.0 3.9 copy-start.9
  35.9 80.6 %all-gather.8.cloned.1.call-start = ((), (), s32[]{:S(2)}) async-start(), calls=%async_computation.16 | async-start | bytes 1179648 | tf_op jit(solution)/shard_map/all_gather | solution.py:156
  36.5 45.8 %copy-start.23 = (f32[64]{0:T(128)}, f32[64]{0:T(128)S(1)}, u32[]{:S(2)}) copy-start(f32[64]{0:T(128)S(1)} %multiply_power_fusion) | copy-start | bytes 772
  76.8 100.7 %reduce-scatter.17.cloned.1.call-start = ((), (), s32[]{:S(2)}) async-start(), calls=%async_computation.17 | async-start | bytes 3276800 | tf_op jit(solution)/shard_map/reduce_scatter | solution.py:170
  119.2 4.4 copy-start.2
  119.2 4.3 copy-start.19
  121.2 2.3 copy-start.20
  144.0 160.5 %all-gather.12.cloned.1.call-start = ((), (), s32[]{:S(2)}) async-start(), calls=%async_computation.19 | async-start | bytes 12288000 | tf_op jit(solution)/shard_map/all_gather | solution.py:127
  150.0 30.2 %copy-start.15 = (f32[2560]{0:T(1024)S(1)}, f32[2560]{0:T(1024)}, u32[]{:S(2)}) copy-start(f32[2560]{0:T(1024)} %param.17) | copy-start | bytes 30724
  150.0 210.3 %all-gather.10.cloned.1.call-start = ((), (), s32[]{:S(2)}) async-start(), calls=%async_computation.18 | async-start | bytes 5898240 | tf_op jit(solution)/shard_map/all_gather | solution.py:177
  182.6 264.3 %all-gather.18.cloned.1.call-start = ((), (), s32[]{:S(2)}) async-start(), calls=%async_computation.28 | async-start | bytes 5898240 | tf_op jit(solution)/shard_map/all_gather | solution.py:126
  187.7 107.3 %collective-permute-start = (bf16[960,2560]{1,0:T(8,128)(2,1)}, bf16[960,2560]{1,0:T(8,128)(2,1)}, u32[]{:S(2)}, u32[]{:S(2)}) collective-permute-start(bf16[960,2560]{1,0:T(8,128)(2,1)} %constant_dynamic-slice_fusion), channel_id=1, source_target_pairs={{0,2},{4,6},{9,11},{13,15},{18,16},{22,20},{27,25},{31,29}} | collective-permute-start | bytes 14745608 | tf_op jit(solution)/shard_map/ppermute | solution.py:81
  192.9 386.9 %reduce-scatter.21.cloned.1.call-start = ((), (), s32[]{:S(2)}) async-start(), calls=%async_computation.21 | async-start | bytes 5898240 | tf_op jit(solution)/shard_map/reduce_scatter | solution.py:188
  301.0 145.8 %collective-permute-start.1 = (bf16[960,2560]{1,0:T(8,128)(2,1)}, bf16[960,2560]{1,0:T(8,128)(2,1)}, u32[]{:S(2)}, u32[]{:S(2)}) collective-permute-start(bf16[960,2560]{1,0:T(8,128)(2,1)} %broadcast_select_fusion), channel_id=1, source_target_pairs={{0,1},{2,3},{4,5},{6,7},{9,8},{11,10},{13,12},{15,14},{18,19},{16,... | collective-permute-start | bytes 14745608 | tf_op jit(solution)/shard_map/ppermute | solution.py:88
  478.0 134.3 %all-gather.14.cloned.1.call-start = ((), (), s32[]{:S(2)}) async-start(), calls=%async_computation.22 | async-start | bytes 3276800 | tf_op jit(solution)/shard_map/all_gather | solution.py:229
  619.2 13.7 all-to-all-start.2
  622.7 85.6 %reduce-scatter.23.cloned.1.call-start = ((), (), s32[]{:S(2)}) async-start(), calls=%async_computation.23 | async-start | bytes 1179648 | tf_op jit(solution)/shard_map/reduce_scatter | solution.py:247
  623.5 13.0 copy-start.16
  632.9 3.6 copy-start.8
  632.9 7.7 slice-start
  636.5 4.2 slice-start.1
  640.7 2.1 copy-start.12
  640.7 2.1 copy-start.13
  645.0 117.8 %all-gather.16.cloned.1.call-start = ((), (), s32[]{:S(2)}) async-start(), calls=%async_computation.24 | async-start | bytes 3932160 | tf_op jit(solution)/shard_map/all_gather | solution.py:254
  648.0 61.3 %copy-start.24 = (f32[64]{0:T(128)S(1)}, f32[64]{0:T(128)}, u32[]{:S(2)}) copy-start(f32[64]{0:T(128)} %copy-done.23) | copy-start | bytes 772
  711.6 118.9 %reduce-scatter.29.cloned.1.call-start = ((), (), s32[]{:S(2)}) async-start(), calls=%async_computation.27 | async-start | bytes 12288000 | tf_op jit(solution)/shard_map/reduce_scatter | solution.py:208
  729.5 227.5 %reduce-scatter.27.cloned.1.call-start = ((), (), s32[]{:S(2)}) async-start(), calls=%async_computation.26 | async-start | bytes 3686400 | tf_op jit(solution)/shard_map/reduce_scatter | solution.py:268
  742.9 267.3 %reduce-scatter.33.cloned.1.call-start = ((), (), s32[]{:S(2)}) async-start(), calls=%async_computation.30 | async-start | bytes 6553600
  762.3 336.2 %reduce-scatter.25.cloned.1.call-start = ((), (), s32[]{:S(2)}) async-start(), calls=%async_computation.25 | async-start | bytes 4423680 | tf_op jit(solution)/shard_map/reduce_scatter | solution.py:268
  775.6 2.5 copy-start.6
  780.4 440.0 %reduce-scatter.19.cloned.1.call-start = ((), (), s32[]{:S(2)}) async-start(), calls=%async_computation.20 | async-start | bytes 5898240 | tf_op jit(solution)/shard_map/reduce_scatter | solution.py:194
  799.2 35.6 %all-to-all-start.3 = ((bf16[4,128,640]{2,1,0:T(8,128)(2,1)}), bf16[4,128,640]{2,1,0:T(8,128)(2,1)S(1)}, u32[]{:S(2)}, u32[]{:S(2)}) async-start(bf16[4,128,640]{2,1,0:T(8,128)(2,1)} %bitcast.32), calls=%async_computation.8 | async-start | bytes 1310720 | tf_op jit(solution)/shard_map/all_to_all | solution.py:137
  834.8 182.6 %all-to-all-start.4 = ((bf16[8,320,480]{2,1,0:T(8,128)(2,1)}), bf16[8,320,480]{2,1,0:T(8,128)(2,1)}, u32[]{:S(2)}, u32[]{:S(2)}) async-start(bf16[8,320,480]{2,1,0:T(8,128)(2,1)} %bitcast.47), calls=%async_computation.12 | async-start | bytes 5242880 | tf_op jit(solution)/shard_map/all_to_all | solution.py:214
  840.9 173.1 %copy-start.18 = (f32[2560]{0:T(1024)S(1)}, f32[2560]{0:T(1024)}, u32[]{:S(2)}) copy-start(f32[2560]{0:T(1024)} %get-tuple-element.11) | copy-start | bytes 30724
  840.9 506.7 %reduce-scatter.31.cloned.1.call-start = ((), (), s32[]{:S(2)}) async-start(), calls=%async_computation.29 | async-start | bytes 1351680
  957.0 57.0 %collective-permute-start.3 = (bf16[320,640]{1,0:T(8,128)(2,1)}, bf16[320,640]{1,0:T(8,128)(2,1)S(1)}, u32[]{:S(2)}, u32[]{:S(2)}) collective-permute-start(bf16[320,640]{1,0:T(8,128)(2,1)} %bitcast.224), channel_id=1, source_target_pairs={{0,0},{1,8},{2,16},{3,24},{4,1},{5,9},{6,17},{7,25},{8,2},{9,10},{... | collective-permute-start | bytes 1228808 | tf_op jit(solution)/shard_map/ppermute | solution.py:275
  1017.4 3.6 copy-start.32
  1017.4 203.0 %copy-start.4 = (bf16[128,2560]{1,0:T(8,128)(2,1)S(1)}, bf16[128,2560]{1,0:T(8,128)(2,1)}, u32[]{:S(2)}) copy-start(bf16[128,2560]{1,0:T(8,128)(2,1)} %reduce-scatter.17.cloned.1.call-done) | copy-start | bytes 1966084
  1017.4 203.0 %copy-start.5 = (bf16[128,2560]{1,0:T(8,128)(2,1)S(1)}, bf16[128,2560]{1,0:T(8,128)(2,1)}, u32[]{:S(2)}) copy-start(bf16[128,2560]{1,0:T(8,128)(2,1)} %reduce-scatter.21.cloned.1.call-done) | copy-start | bytes 1966084
  1017.4 203.0 %copy-start.22 = (f32[128]{0:T(128)S(1)}, f32[128]{0:T(128)}, u32[]{:S(2)}) copy-start(f32[128]{0:T(128)} %copy-done.21) | copy-start | bytes 1540
  1017.4 203.0 %copy-start.29 = (f32[128]{0:T(128)S(1)}, f32[128]{0:T(128)}, u32[]{:S(2)}) copy-start(f32[128]{0:T(128)} %copy-done.28) | copy-start | bytes 1540
  1020.9 328.7 %collective-permute-start.4 = (bf16[4,320,480]{2,1,0:T(8,128)(2,1)}, bf16[4,320,480]{2,1,0:T(8,128)(2,1)}, u32[]{:S(2)}, u32[]{:S(2)}) collective-permute-start(bf16[4,320,480]{2,1,0:T(8,128)(2,1)} %get-tuple-element.19), channel_id=1, source_target_pairs={{0,1},{1,0},{2,3},{3,2},{4,5},{5,4},{6,7},{7,6},{8,9},{9,8},{10,11... | collective-permute-start | bytes 3686408 | tf_op jit(solution)/shard_map/ppermute | solution.py:221
  1098.5 269.2 %collective-permute-start.2 = (bf16[320,768]{1,0:T(8,128)(2,1)}, bf16[320,768]{1,0:T(8,128)(2,1)}, u32[]{:S(2)}, u32[]{:S(2)}) collective-permute-start(bf16[320,768]{1,0:T(8,128)(2,1)} %bitcast.223), channel_id=1, source_target_pairs={{0,0},{1,8},{2,16},{3,24},{4,1},{5,9},{6,17},{7,25},{8,2},{9,10},{... | collective-permute-start | bytes 1474568 | tf_op jit(solution)/shard_map/ppermute | solution.py:275
  1359.5 11.7 copy-start.1
  (19 other events, 24.9 us)
Sparse Core Ops, SparseCore 0:
  36.0 38.2 reduce-scatter.14
  77.2 39.2 all-gather.7
  144.1 33.3 reduce-scatter.16
  179.5 88.4 all-gather.11
  270.7 89.6 all-gather.9
  362.4 84.4 all-gather.17
  478.1 101.6 reduce-scatter.20
  586.9 25.3 all-gather.13
  645.1 63.1 reduce-scatter.22
  711.7 27.8 all-gather.15
  742.4 88.0 reduce-scatter.28
  834.3 122.6 reduce-scatter.26
  959.6 50.6 reduce-scatter.32
  1014.2 84.2 reduce-scatter.24
  1102.0 118.3 reduce-scatter.18
  1222.4 125.0 reduce-scatter.30

commit v2 on v1

v2 whole, which is shorter than its diff:
```python
import functools

import jax
import jax.numpy as jnp
from jax import lax
from jax.experimental import pallas as pl
from jax.experimental.pallas import tpu as pltpu
from jax.sharding import PartitionSpec as P

HD = 256
WINDOW = 2048


epsilon = 1e-06
f32 = jnp.float32
bf16 = jnp.bfloat16
VMEM = pltpu.VMEM
DMA = pltpu.SemaphoreType.DMA
vmem_bytes = 58 * 1024 * 1024


def rms_norm(values, gain):
    return values * lax.rsqrt(jnp.mean(values * values, axis=-1, keepdims=True) + epsilon) * gain


def frequencies(quarter):
    return 10000.0 ** (-jnp.arange(quarter, dtype=jnp.float32) / quarter)


def documents(index, bounds):
    return (index >= bounds[0]).astype(jnp.int32) + (index >= bounds[1]).astype(jnp.int32)


def rotary_angles(index, bounds):
    member = documents(index, bounds)
    opening = jnp.where(member == 0, 0, jnp.where(member == 1, bounds[0], bounds[1]))
    return (index - opening).astype(jnp.float32)[:, None] * frequencies(HD // 4)[None, :]


def visible(query_index, key_index, bounds):
    apart = query_index[:, None] - key_index[None, :]
    same_doc = documents(query_index, bounds)[:, None] == documents(key_index, bounds)[None, :]
    return (apart >= 0) & (apart < WINDOW) & (key_index[None, :] >= 0) & same_doc


def contract_rows(left, right):
    return lax.dot_general(
        left, right, (((1,), (1,)), ((), ())), preferred_element_type=jnp.float32
    )


def contract_tokens(left, right):
    return lax.dot_general(
        left, right, (((0,), (0,)), ((), ())), preferred_element_type=jnp.float32
    )


def gelu_product(gate_part, up_part):
    return jax.nn.gelu(gate_part, approximate=True) * up_part


def remote(src, dst, send_sem, recv_sem, device):
    return pltpu.make_async_remote_copy(
        src_ref=src,
        dst_ref=dst,
        send_sem=send_sem,
        recv_sem=recv_sem,
        device_id=device,
        device_id_type=pl.DeviceIdType.MESH,
    )


class Place:
    def __init__(self, lines):
        self.lines = lines
        self.c = lax.axis_index("ctx")
        self.f = lax.axis_index("fsdp")
        self.line = self.c // 2
        self.lane = self.c % 2
        self.chip = self.f // 2
        self.core = self.f % 2
        self.twin_f = self.f + 1 - 2 * self.core
        self.cross_f = (self.f + 2) % 4
        self.diag_f = (self.twin_f + 2) % 4
        self.twin = {"fsdp": self.twin_f}
        self.cross = {"fsdp": self.cross_f}
        self.diag = {"fsdp": self.diag_f}
        self.beside = {"ctx": self.c + 1 - 2 * self.lane}
        self.right = {"ctx": self.c + 2}
        self.left = {"ctx": self.c - 2}
        self.has_right = self.line < lines - 1
        self.has_left = self.line > 0

    def barrier(self, ctx=True, fsdp=True):
        sem = pltpu.get_barrier_semaphore()

        def greet(device):
            pl.semaphore_signal(sem, 1, device_id=device, device_id_type=pl.DeviceIdType.MESH)

        count = 0
        if fsdp:
            for device in (self.twin, self.cross, self.diag):
                greet(device)
            count = 3
        if ctx:
            greet(self.beside)
            pl.when(self.has_right)(lambda: greet(self.right))
            pl.when(self.has_left)(lambda: greet(self.left))
            count = (
                count + 1 + self.has_right.astype(jnp.int32) + self.has_left.astype(jnp.int32)
            )
        pl.semaphore_wait(sem, count)


class LineGather:
    sems = 6

    def __init__(self, place, own, slots, sems):
        self.p, self.own, self.slots, self.s = place, own, slots, sems

    def rightward(self, step):
        at = 2 * (self.p.line - step) + self.p.lane
        src = self.own if step == 0 else self.slots.at[at]
        return remote(src, self.slots.at[at], self.s.at[0, step], self.s.at[1, step], self.p.right)

    def leftward(self, step):
        at = 2 * (self.p.line + step) + self.p.lane
        src = self.own if step == 0 else self.slots.at[at]
        return remote(src, self.slots.at[at], self.s.at[2, step], self.s.at[3, step], self.p.left)

    def across(self, line, own=False):
        at = 2 * line + self.p.lane
        src = self.own if own else self.slots.at[at]
        return remote(
            src, self.slots.at[at], self.s.at[4, line], self.s.at[5, line], self.p.beside
        )

    def from_left(self, step):
        at = 2 * (self.p.line - 1 - step) + self.p.lane
        slot = self.slots.at[at]
        return remote(slot, slot, self.s.at[0, step], self.s.at[1, step], self.p.right)

    def from_right(self, step):
        at = 2 * (self.p.line + 1 + step) + self.p.lane
        slot = self.slots.at[at]
        return remote(slot, slot, self.s.at[2, step], self.s.at[3, step], self.p.left)

    def start(self):
        pl.when(self.p.has_right)(lambda: self.rightward(0).start())
        pl.when(self.p.has_left)(lambda: self.leftward(0).start())
        self.across(self.p.line, True).start()

    def step(self, step):
        p = self.p

        @pl.when(p.line - 1 - step >= 0)
        def _():
            self.from_left(step).wait_recv()
            if step + 1 < p.lines - 1:
                pl.when(p.has_right)(lambda: self.rightward(step + 1).start())
            self.across(p.line - 1 - step).start()

        @pl.when(p.line + 1 + step <= p.lines - 1)
        def _():
            self.from_right(step).wait_recv()
            if step + 1 < p.lines - 1:
                pl.when(p.has_left)(lambda: self.leftward(step + 1).start())
            self.across(p.line + 1 + step).start()

    def steps(self):
        for step in range(self.p.lines - 1):
            self.step(step)

    def arrived_across(self, line):
        at = 2 * line + 1 - self.p.lane
        slot = self.slots.at[at]
        remote(slot, slot, self.s.at[4, line], self.s.at[5, line], self.p.beside).wait_recv()

    def finish(self, arrivals=True):
        p = self.p
        if arrivals:
            for line in range(p.lines):
                self.arrived_across(line)
        for step in range(p.lines - 1):
            pl.when(p.has_right & (p.line - step >= 0))(
                lambda step=step: self.rightward(step).wait_send()
            )
            pl.when(p.has_left & (p.line + step <= p.lines - 1))(
                lambda step=step: self.leftward(step).wait_send()
            )
        for line in range(p.lines):
            self.across(line).wait_send()


class LineSum:
    sems = 6

    def __init__(self, place, parts, side, chain, sems):
        self.p, self.parts, self.side, self.chain, self.s = place, parts, side, chain, sems

    def order(self, turn):
        lines, line = self.p.lines, self.p.line
        value = 0
        for a in range(lines):
            far = sorted(range(lines), key=lambda t: (-abs(t - a), t))
            value = value + jnp.where(line == a, far[turn], 0)
        return value

    def across(self, turn):
        t = self.order(turn)
        at = 2 * t + 1 - self.p.lane
        return remote(
            self.parts.at[at],
            self.side.at[t],
            self.s.at[0, t],
            self.s.at[1, t],
            self.p.beside,
        )

    def rightward(self, t):
        step = self.p.lines - 1 - t
        return remote(
            self.parts.at[2 * t + self.p.lane],
            self.chain.at[0, step],
            self.s.at[2, step],
            self.s.at[3, step],
            self.p.right,
        )

    def leftward(self, t):
        return remote(
            self.parts.at[2 * t + self.p.lane],
            self.chain.at[1, t],
            self.s.at[4, t],
            self.s.at[5, t],
            self.p.left,
        )

    def add(self, at, other):
        self.parts[at] = (self.parts[at].astype(f32) + other.astype(f32)).astype(bf16)

    def start(self):
        for turn in range(min(2, self.p.lines)):
            self.across(turn).start()

    def turn(self, turn):
        p = self.p
        t = self.order(turn)
        at = 2 * t + p.lane
        self.across(turn).wait_recv()
        if turn + 2 < p.lines:
            self.across(turn + 2).start()
        self.add(at, self.side[t])

        @pl.when(t > p.line)
        def _():
            @pl.when(p.has_left)
            def _():
                self.rightward(t).wait_recv()
                self.add(at, self.chain[0, p.lines - 1 - t])

            self.rightward(t).start()

        @pl.when(t < p.line)
        def _():
            @pl.when(p.has_right)
            def _():
                self.leftward(t).wait_recv()
                self.add(at, self.chain[1, t])

            self.leftward(t).start()

    def turns(self):
        for turn in range(self.p.lines):
            self.turn(turn)

    def total(self):
        p = self.p
        at = 2 * p.line + p.lane

        @pl.when(p.has_left)
        def _():
            self.rightward(p.line).wait_recv()
            self.add(at, self.chain[0, p.lines - 1 - p.line])

        @pl.when(p.has_right)
        def _():
            self.leftward(p.line).wait_recv()
            self.add(at, self.chain[1, p.line])

        return self.parts[at].astype(f32)

    def finish(self):
        p = self.p
        for turn in range(p.lines):
            self.across(turn).wait_send()
        for t in range(p.lines):
            pl.when(t > p.line)(lambda t=t: self.rightward(t).wait_send())
            pl.when(t < p.line)(lambda t=t: self.leftward(t).wait_send())


class GroupSum:
    sems = 6

    def __init__(self, place, parts, near, out, far, sems):
        self.p, self.parts, self.near, self.out, self.far, self.s = place, parts, near, out, far, sems

    def to_twin(self, i, which, cols):
        p = self.p
        block = p.diag_f if which == 0 else p.twin_f
        return remote(
            self.parts.at[block, :, cols],
            self.near.at[which, :, cols],
            self.s.at[which, i],
            self.s.at[2 + which, i],
            p.twin,
        )

    def to_cross(self, i, cols):
        return remote(
            self.out.at[:, cols], self.far.at[:, cols], self.s.at[4, i], self.s.at[5, i], self.p.cross
        )

    def give(self, i, cols):
        self.to_twin(i, 0, cols).start()
        self.to_twin(i, 1, cols).start()

    def pass_on(self, i, cols):
        self.to_twin(i, 0, cols).wait_recv()
        mine = self.parts[self.p.cross_f, :, cols].astype(f32)
        self.out[:, cols] = (mine + self.near[0, :, cols].astype(f32)).astype(bf16)
        self.to_cross(i, cols).start()

    def take(self, i, cols):
        self.to_twin(i, 1, cols).wait_recv()
        near = self.parts[self.p.f, :, cols].astype(f32) + self.near[1, :, cols].astype(f32)
        self.to_cross(i, cols).wait_recv()
        return near + self.far[:, cols].astype(f32)

    def finish(self, i, cols):
        self.to_twin(i, 0, cols).wait_send()
        self.to_twin(i, 1, cols).wait_send()
        self.to_cross(i, cols).wait_send()


class GroupTrade:
    sems = 2

    def __init__(self, place, whole, slots, sems, columns):
        self.p, self.whole, self.slots, self.s, self.n = place, whole, slots, sems, columns

    def block(self, g):
        return self.whole.at[:, pl.ds(pl.multiple_of(g * self.n, 128), self.n)]

    def copy(self, d):
        g = (self.p.f + d) % 4
        return remote(
            self.block(g), self.slots.at[self.p.f], self.s.at[0, d], self.s.at[1, d], {"fsdp": g}
        )

    def arrival(self, d):
        slot = self.slots.at[(self.p.f + 4 - d) % 4]
        return remote(slot, slot, self.s.at[0, d], self.s.at[1, d], {"fsdp": (self.p.f + d) % 4})

    def own(self):
        return pltpu.make_async_copy(
            self.block(self.p.f), self.slots.at[self.p.f], self.s.at[1, 0]
        )

    def start(self):
        for d in (2, 3, 1):
            self.copy(d).start()
        self.own().start()

    def wait(self):
        self.own().wait()
        for d in (1, 2, 3):
            self.arrival(d).wait_recv()

    def finish(self):
        for d in (1, 2, 3):
            self.copy(d).wait_send()


def rotated(v, cosine, sine):
    first = v[:, :128]
    return jnp.concatenate(
        [first * cosine + pltpu.roll(first, 64, 1) * sine, v[:, 128:]], axis=1
    )


class WeightColumns:
    sems = 6

    def __init__(self, place, own, whole, sems, own_sem, pieces):
        self.p, self.own, self.whole, self.s, self.own_sem = place, own, whole, sems, own_sem
        self.pieces, self.n = pieces, own.shape[0] // pieces

    def part(self, ref, i):
        return ref.at[pl.ds(i * self.n, self.n)]

    def slot(self, g, i):
        return self.whole.at[g, pl.ds(i * self.n, self.n)]

    def local(self):
        return pltpu.make_async_copy(self.own, self.whole.at[self.p.f], self.own_sem)

    def to_twin(self, i):
        return remote(
            self.part(self.own, i), self.slot(self.p.f, i), self.s.at[0, i], self.s.at[3, i], self.p.twin
        )

    def to_cross(self, i):
        return remote(
            self.part(self.own, i), self.slot(self.p.f, i), self.s.at[1, i], self.s.at[4, i], self.p.cross
        )

    def forward(self, i):
        slot = self.slot(self.p.cross_f, i)
        return remote(slot, slot, self.s.at[2, i], self.s.at[5, i], self.p.twin)

    def give(self, i):
        self.to_cross(i).start()
        self.to_twin(i).start()

    def pass_on(self, i):
        slot = self.slot(self.p.cross_f, i)
        remote(slot, slot, self.s.at[1, i], self.s.at[4, i], self.p.cross).wait_recv()
        self.forward(i).start()

    def finish(self, i):
        twin, diag = self.slot(self.p.twin_f, i), self.slot(self.p.diag_f, i)
        remote(twin, twin, self.s.at[0, i], self.s.at[3, i], self.p.twin).wait_recv()
        remote(diag, diag, self.s.at[2, i], self.s.at[5, i], self.p.twin).wait_recv()
        self.to_twin(i).wait_send()
        self.to_cross(i).wait_send()
        self.forward(i).wait_send()


class WeightRows:
    sems = 3

    def __init__(self, place, held, whole, sems, own_sem, pieces):
        per_owner = place.lines * 2 // 4
        self.p, self.held, self.whole, self.s, self.own_sem = place, held, whole, sems, own_sem
        self.rows = whole.shape[0]
        self.pieces, self.n = pieces, whole.shape[0] // pieces
        self.first = (place.c % per_owner) * self.rows
        owner = place.c // per_owner
        self.is_owner = place.f == owner
        self.is_cross = place.f == (owner + 2) % 4
        self.is_last = (place.f != owner) & (place.f != (owner + 2) % 4)

    def source(self, i):
        return self.held.at[pl.ds(pl.multiple_of(self.first + i * self.n, 16), self.n)]

    def slot(self, i):
        return self.whole.at[pl.ds(i * self.n, self.n)]

    def local(self):
        return pltpu.make_async_copy(
            self.held.at[pl.ds(pl.multiple_of(self.first, 16), self.rows)], self.whole, self.own_sem
        )

    def to_cross(self, i):
        return remote(self.source(i), self.slot(i), self.s.at[0, i], self.s.at[2, i], self.p.cross)

    def to_twin(self, i):
        return remote(self.source(i), self.slot(i), self.s.at[1, i], self.s.at[2, i], self.p.twin)

    def forward(self, i):
        slot = self.slot(i)
        return remote(slot, slot, self.s.at[1, i], self.s.at[2, i], self.p.twin)

    def start(self):
        @pl.when(self.is_owner)
        def _():
            self.local().start()
            for i in range(self.pieces):
                self.to_cross(i).start()
                self.to_twin(i).start()

    def pass_on(self, i):
        @pl.when(self.is_cross)
        def _():
            self.forward(i).wait_recv()
            self.forward(i).start()

    def finish(self):
        @pl.when(self.is_owner)
        def _():
            self.local().wait()
            for i in range(self.pieces):
                self.to_cross(i).wait_send()
                self.to_twin(i).wait_send()

        @pl.when(self.is_cross)
        def _():
            for i in range(self.pieces):
                self.forward(i).wait_send()

        @pl.when(self.is_last)
        def _():
            for i in range(self.pieces):
                self.forward(i).wait_recv()


def tiles_of(first, count, tile):
    tile = tile if count % tile == 0 else 128

    def loop(body):
        def one(i, carry):
            body(pl.ds(pl.multiple_of(first + i * tile, 128), tile))
            return carry

        lax.fori_loop(0, count // tile, one, 0)

    return loop


def front_kernel(
    lines,
    x_ref,
    gain_one,
    gain_two,
    cosine,
    sine,
    bias,
    w_keyval,
    w_query,
    w_out,
    cot,
    w_columns,
    w_rows,
    normed_out,
    query_out,
    keyval_out,
    probs_out,
    mixed_out,
    middle_out,
    normed_two_out,
    cot_all,
    columns_all,
    rows_all,
    whole,
    slots,
    parts,
    near,
    out,
    far,
    keyval,
    mixed,
    trade_sems,
    sum_sems,
    keyval_sems,
    cot_sems,
    column_sems,
    row_sems,
    own_sems,
):
    p = Place(lines)
    rows, width = x_ref.shape
    heads = query_out.shape[0]
    inner = heads * HD
    kv_width = 2 * HD
    p.barrier()

    columns = WeightColumns(p, w_columns, columns_all, column_sems, own_sems.at[0], column_sems.shape[1])
    down = WeightRows(p, w_rows, rows_all, row_sems, own_sems.at[1], row_sems.shape[1])
    cot_gather = LineGather(p, cot, cot_all, cot_sems)
    cot_local = pltpu.make_async_copy(cot, cot_all.at[p.c], own_sems.at[2])

    source = x_ref[...].astype(f32)
    whole[...] = rms_norm(source, gain_one[...]).astype(bf16)
    trade = GroupTrade(p, whole, slots.at[0], trade_sems.at[0], slots.shape[3])
    trade.start()
    columns.local().start()
    cot_local.start()
    cot_gather.start()
    trade.wait()
    normed_out[...] = slots[0]

    half = (heads // 2) * HD
    chunks = [(0, kv_width), (kv_width, half), (kv_width + half, inner - half)]
    group = GroupSum(p, parts, near, out, far, sum_sems.at[0])

    def project(lhs, weight, first, count, to):
        @tiles_of(first, count, 256)
        def _(cols):
            left = lhs[...].reshape(4 * rows, lhs.shape[-1])
            product = jnp.dot(left, weight[:, cols], preferred_element_type=f32)
            if to:
                cols = pl.ds(pl.multiple_of(cols.start + to, 128), cols.size)
            parts[:, :, cols] = product.astype(bf16).reshape(4, rows, cols.size)

    spans = [pl.ds(first, count) for first, count in chunks]
    project(slots.at[0], w_keyval, 0, kv_width, 0)
    group.give(0, spans[0])
    project(slots.at[0], w_query, 0, half, kv_width)
    group.give(1, spans[1])
    group.pass_on(0, spans[0])
    project(slots.at[0], w_query, half, inner - half, kv_width)
    group.give(2, spans[2])
    group.pass_on(1, spans[1])
    group.pass_on(2, spans[2])

    linear = group.take(0, spans[0])
    keyval[p.c] = jnp.concatenate(
        [rotated(linear[:, :HD], cosine[...], sine[...]), linear[:, HD:]], axis=1
    ).astype(bf16)
    kv_gather = LineGather(p, keyval.at[p.c], keyval, keyval_sems)
    kv_gather.start()
    for i in (1, 2):
        linear = group.take(i, spans[i])
        for h in range(linear.shape[1] // HD):
            turned = rotated(linear[:, h * HD : (h + 1) * HD], cosine[...], sine[...])
            at = h if i == 1 else h + heads // 2
            query_out[at] = (turned * HD**-0.5).astype(bf16)
        if i == 1:
            kv_gather.step(0)
    for i in range(columns.pieces):
        columns.give(i)
    for step in range(1, lines - 1):
        kv_gather.step(step)
    kv_gather.finish()
    keyval_out[...] = keyval[...]

    length = bias.shape[1]

    def two_heads(i, carry):
        keys = keyval[:, :, :HD].reshape(length, HD)
        values = keyval[:, :, HD:].reshape(length, HD)
        two = query_out[pl.ds(2 * i, 2)].reshape(2 * rows, HD)
        scores = contract_rows(two, keys).reshape(2, rows, length) + bias[...][None]
        scores = scores.reshape(2 * rows, length)
        weights = jnp.exp(scores - jnp.max(scores, axis=-1, keepdims=True))
        total = jnp.sum(weights, axis=-1, keepdims=True)
        weights = (weights / total).astype(bf16)
        probs_out[pl.ds(2 * i, 2)] = weights.reshape(2, rows, length)
        product = jnp.dot(weights, values, preferred_element_type=f32).astype(bf16)
        at = pl.multiple_of(i * 2 * HD, 128)
        mixed[:, pl.ds(at, HD)] = product[:rows]
        mixed[:, pl.ds(at + HD, HD)] = product[rows:]
        return carry

    lax.fori_loop(0, heads // 2, two_heads, 0)
    trade_two = GroupTrade(p, mixed, slots.at[1], trade_sems.at[1], slots.shape[3])
    trade_two.start()
    for step in range(lines - 1):
        cot_gather.step(step)
    for i in range(len(chunks)):
        group.finish(i, spans[i])
    trade_two.wait()
    mixed_out[...] = slots[1]

    half = width // 2
    spans_two = [pl.ds(0, half), pl.ds(half, half)]
    group_two = GroupSum(p, parts, near, out, far, sum_sems.at[1])
    for i in range(2):
        project(slots.at[1], w_out, i * half, half, 0)
        group_two.give(i, spans_two[i])
    for i in range(2):
        group_two.pass_on(i, spans_two[i])
    for i in range(2):
        middle_out[:, spans_two[i]] = x_ref[:, spans_two[i]].astype(f32) + group_two.take(
            i, spans_two[i]
        )
    normed_two_out[...] = rms_norm(middle_out[...], gain_two[...]).astype(bf16)

    down.start()
    for i in range(columns.pieces):
        columns.pass_on(i)
    for i in range(down.pieces):
        down.pass_on(i)
    for i in range(2):
        group_two.finish(i, spans_two[i])
    trade.finish()
    trade_two.finish()
    columns.local().wait()
    cot_local.wait()
    for i in range(columns.pieces):
        columns.finish(i)
    down.finish()
    cot_gather.finish()


def front(lines, operands, part_width, heads):
    x = operands[0]
    rows, width = x.shape
    places = 2 * lines
    length = places * rows
    inner = heads * HD
    shard = width // 4
    parts_width = inner + 2 * HD
    in_vmem = pl.BlockSpec(memory_space=VMEM)
    anywhere = pl.BlockSpec(memory_space=pl.ANY)
    shape = jax.ShapeDtypeStruct
    pieces = 4
    assert inner == width
    return pl.pallas_call(
        functools.partial(front_kernel, lines),
        out_shape=(
            shape((4, rows, shard), bf16),
            shape((heads, rows, HD), bf16),
            shape((places, rows, 2 * HD), bf16),
            shape((heads, rows, length), bf16),
            shape((4, rows, shard), bf16),
            shape((rows, width), f32),
            shape((rows, width), bf16),
            shape((places, rows, width), bf16),
            shape((4,) + operands[10].shape, bf16),
            shape((part_width, width), bf16),
        ),
        in_specs=[in_vmem] * 9 + [anywhere] * 3,
        out_specs=[in_vmem] * 7 + [anywhere] * 3,
        scratch_shapes=[
            VMEM((rows, width), bf16),
            VMEM((2, 4, rows, shard), bf16),
            VMEM((4, rows, parts_width), bf16),
            VMEM((2, rows, parts_width), bf16),
            VMEM((rows, parts_width), bf16),
            VMEM((rows, parts_width), bf16),
            VMEM((places, rows, 2 * HD), bf16),
            VMEM((rows, inner), bf16),
            DMA((2, GroupTrade.sems, 4)),
            DMA((2, GroupSum.sems, 3)),
            DMA((LineGather.sems, lines)),
            DMA((LineGather.sems, lines)),
            DMA((WeightColumns.sems, pieces)),
            DMA((WeightRows.sems, 3)),
            DMA((3,)),
        ],
        compiler_params=pltpu.CompilerParams(
            collective_id=0, has_side_effects=True, vmem_limit_bytes=vmem_bytes
        ),
        name="front",
    )(*operands)


def per_device(
    tokens,
    doc_bounds,
    cotangent,
    norm_one,
    query_weight,
    keyval_weight,
    out_weight,
    norm_two,
    gate_up_weight,
    down_weight,
):
    ctx_size = lax.axis_size("ctx")
    fsdp_size = lax.axis_size("fsdp")
    lines = ctx_size // 2
    rows = tokens.shape[1]
    width = tokens.shape[2]
    length = rows * ctx_size
    inner_width = query_weight.shape[1]
    head_count = inner_width // HD
    hidden_width = gate_up_weight.shape[1] // 2
    part_width = hidden_width // ctx_size
    padded = -(-part_width // 128) * 128
    ctx_place = lax.axis_index("ctx")
    source = tokens[0].astype(jnp.float32)
    bounds = doc_bounds[0]
    query_index = ctx_place * rows + jnp.arange(rows, dtype=jnp.int32)
    key_index = jnp.arange(length, dtype=jnp.int32)
    allowed = visible(query_index, key_index, bounds)
    bias = jnp.where(allowed, 0.0, -1e30).astype(jnp.float32)
    angles = rotary_angles(query_index, bounds)
    cosine = jnp.cos(angles)
    sine = jnp.sin(angles)
    cosine = jnp.concatenate([cosine, cosine], axis=1)
    sine = jnp.concatenate([-sine, sine], axis=1)

    def own_columns(first):
        cols = lax.dynamic_slice_in_dim(
            gate_up_weight, first + ctx_place * part_width, part_width, 1
        )
        return jnp.pad(cols, ((0, 0), (0, padded - part_width)))

    w_columns = jnp.concatenate([own_columns(0), own_columns(hidden_width)], axis=1)
    cot_rows = cotangent[0]
    (
        normed,
        queries,
        window,
        weights,
        mixed,
        middle,
        normed_two,
        cot_all,
        w_gate_up,
        w_down,
    ) = front(
        lines,
        (
            tokens[0],
            norm_one[None],
            norm_two[None],
            cosine,
            sine,
            bias,
            keyval_weight,
            query_weight,
            out_weight,
            cot_rows,
            w_columns,
            down_weight,
        ),
        part_width,
        head_count,
    )
    normed = normed.reshape(fsdp_size * rows, -1)
    mixed = mixed.reshape(fsdp_size * rows, -1)
    window = window.reshape(length, -1)
    cot_all = cot_all.reshape(length, width)
    w_gate_up = w_gate_up.reshape(width, 2 * padded)
    key_rows = window[:, :HD]
    value_rows = window[:, HD:]
    w_qkv = jnp.concatenate([query_weight, keyval_weight], axis=1)

    def collect(value):
        return lax.all_to_all(value, "fsdp", split_axis=0, concat_axis=1, tiled=True)

    _, norm_back_one = jax.vjp(rms_norm, source, norm_one)
    _, norm_back_two = jax.vjp(rms_norm, middle, norm_two)
    normed_two = lax.all_gather(normed_two, "ctx", axis=0, tiled=True)
    projected = jnp.dot(normed_two, w_gate_up, preferred_element_type=jnp.float32)
    hidden_full, gelu_back = jax.vjp(gelu_product, projected[:, :padded], projected[:, padded:])
    hidden = hidden_full.astype(jnp.bfloat16)[:, :part_width]
    grad_hidden = contract_rows(cot_all, w_down)
    grad_gate, grad_up = gelu_back(jnp.pad(grad_hidden, ((0, 0), (0, padded - part_width))))
    grad_gate_up = jnp.concatenate([grad_gate, grad_up], axis=1).astype(jnp.bfloat16)
    grad_normed_two = lax.psum_scatter(
        contract_rows(grad_gate_up, w_gate_up).astype(jnp.bfloat16),
        "ctx",
        scatter_dimension=0,
        tiled=True,
    ).astype(jnp.float32)
    branch_two = lax.psum_scatter(
        jnp.dot(hidden, w_down, preferred_element_type=jnp.float32).astype(jnp.bfloat16),
        "ctx",
        scatter_dimension=0,
        tiled=True,
    ).astype(jnp.float32)
    result = (middle + branch_two).astype(jnp.bfloat16)

    down_grad = lax.psum_scatter(
        contract_tokens(hidden, cot_all).astype(jnp.bfloat16),
        "fsdp",
        scatter_dimension=1,
        tiled=True,
    ).astype(jnp.float32)
    gate_up_part = lax.psum_scatter(
        contract_tokens(normed_two, grad_gate_up).astype(jnp.bfloat16),
        "fsdp",
        scatter_dimension=1,
        tiled=True,
    )
    gate_up_part = lax.all_to_all(
        gate_up_part.reshape(ctx_size, width // ctx_size, -1), "ctx", 0, 0, tiled=True
    )
    core = lax.axis_index("fsdp") % 2
    gate_up_part = gate_up_part.reshape((2, ctx_size // 2) + gate_up_part.shape[1:])
    kept = lax.dynamic_index_in_dim(gate_up_part, core, 0, keepdims=False)
    given = lax.dynamic_index_in_dim(gate_up_part, 1 - core, 0, keepdims=False)
    taken = lax.ppermute(given, "fsdp", [(i, i ^ 1) for i in range(fsdp_size)])
    halves = jnp.where(core == 0, jnp.stack([kept, taken], 2), jnp.stack([taken, kept], 2))
    halves = halves.reshape(halves.shape[:2] + (-1,))[:, :, :part_width]
    gate_up_grad = (
        halves.transpose(1, 0, 2).reshape(width // ctx_size, -1).astype(jnp.float32)
    )

    grad_middle_norm, gain_two_term = norm_back_two(grad_normed_two)
    grad_middle = cot_rows.astype(jnp.float32) + grad_middle_norm
    grad_branch = lax.all_gather(grad_middle.astype(jnp.bfloat16), "fsdp", axis=0, tiled=True)
    grad_mixed = collect(contract_rows(grad_branch, out_weight).astype(jnp.bfloat16))
    grad_mixed = grad_mixed.reshape(rows, head_count, HD)

    grad_weights = jnp.einsum(
        "thd,kd->htk", grad_mixed, value_rows, preferred_element_type=jnp.float32
    )
    row_delta = jnp.sum(weights * grad_weights, axis=-1, keepdims=True)
    grad_scores = (weights * (grad_weights - row_delta)).astype(jnp.bfloat16)
    grad_queries = jnp.einsum(
        "htk,kd->htd", grad_scores, key_rows, preferred_element_type=jnp.float32
    )
    grad_keys = jnp.einsum("htk,htd->kd", grad_scores, queries, preferred_element_type=jnp.float32)
    grad_values = jnp.einsum(
        "htk,thd->kd", weights, grad_mixed, preferred_element_type=jnp.float32
    )
    own_grad = lax.psum_scatter(
        jnp.concatenate([grad_keys, grad_values], axis=1).astype(jnp.bfloat16),
        "ctx",
        scatter_dimension=0,
        tiled=True,
    ).astype(jnp.float32)

    def turned_back(part):
        first = part[..., :128]
        swapped = jnp.concatenate([first[..., 64:], first[..., :64]], axis=-1)
        return jnp.concatenate([first * cosine - swapped * sine, part[..., 128:]], axis=-1)

    grad_linear = jnp.concatenate(
        [
            (turned_back(grad_queries) * HD**-0.5).transpose(1, 0, 2).reshape(rows, inner_width),
            turned_back(own_grad[:, :HD]),
            own_grad[:, HD:],
        ],
        axis=1,
    )
    grad_linear = lax.all_gather(grad_linear.astype(jnp.bfloat16), "fsdp", axis=0, tiled=True)
    grad_normed = collect(contract_rows(grad_linear, w_qkv).astype(jnp.bfloat16))
    grad_source_norm, gain_one_term = norm_back_one(grad_normed.astype(jnp.float32))
    input_grad = (grad_middle + grad_source_norm).astype(jnp.bfloat16)

    per_owner = ctx_size // fsdp_size

    def in_blocks(term):
        tall, wide = term.shape
        term = term.astype(jnp.bfloat16)
        term = term.reshape(per_owner, tall // per_owner, fsdp_size, wide // fsdp_size)
        return term.transpose(0, 2, 1, 3).reshape(ctx_size, tall // per_owner, wide // fsdp_size)

    def summed(blocks):
        block = lax.psum_scatter(blocks, "ctx", scatter_dimension=0, tiled=True)[0]
        pairs = [
            ((r * fsdp_size + g) * fsdp_size + f, (per_owner * f + r) * fsdp_size + g)
            for r in range(per_owner)
            for g in range(fsdp_size)
            for f in range(fsdp_size)
        ]
        return lax.ppermute(block, ("ctx", "fsdp"), pairs).astype(jnp.float32)

    out_grad = summed(in_blocks(contract_tokens(mixed, grad_branch)))
    qkv_term = contract_tokens(normed, grad_linear)
    qkv_block = summed(
        jnp.concatenate(
            [in_blocks(qkv_term[:, :inner_width]), in_blocks(qkv_term[:, inner_width:])], axis=2
        )
    )
    query_grad = qkv_block[:, : inner_width // fsdp_size]
    keyval_grad = qkv_block[:, inner_width // fsdp_size :]
    gains = lax.psum_scatter(
        jnp.stack([gain_one_term, gain_two_term]),
        ("ctx", "fsdp"),
        scatter_dimension=1,
        tiled=True,
    )
    return (
        result[None],
        input_grad[None],
        gains[0],
        query_grad,
        keyval_grad,
        out_grad,
        gains[1],
        gate_up_grad,
        down_grad,
    )


def solution(mesh):
    placed = (
        P("fsdp", "ctx", None),
        P("fsdp", None),
        P("fsdp", "ctx", None),
        P(),
        P("fsdp", None),
        P("fsdp", None),
        P("fsdp", None),
        P(),
        P("fsdp", None),
        P("fsdp", None),
    )
    return jax.shard_map(
        per_device,
        mesh=mesh,
        in_specs=placed,
        out_specs=(
            P("fsdp", "ctx", None),
            P("fsdp", "ctx", None),
            P(("ctx", "fsdp")),
            P("ctx", "fsdp"),
            P("ctx", "fsdp"),
            P("ctx", "fsdp"),
            P(("ctx", "fsdp")),
            P("ctx", "fsdp"),
            P("ctx", "fsdp"),
        ),
        check_vma=False,
    )
```

time: 1400 us -> 1320 us (0.943)
  Pallas kernels: 0 us -> 276 us
  waiting for transfers between devices: 1030 us -> 764 us
  local copies, waits for them, and re-layouts: 111 us -> 74.4 us
  matrix products: 128 us -> 107 us
  starting transfers between devices: 31.7 us -> 15.7 us
    pallas_call x0 -> x1, Pallas kernels: none -> 276 us  [front(): pl.pallas_call(functools.partial(front_kernel, lines), out_shape=(shape((...]
    ppermute x2 -> x0, waiting for transfers between devices: 102 us -> none  [the longest x1 102 us: owner_block(): moved = lax.ppermute(part, ('ctx', 'fsdp'), over)]
    all_gather x4 -> x1, waiting for transfers between devices: 144 us -> 74.7 us  [per_device(): normed_two = lax.all_gather(normed_two, 'ctx', axis=0, tiled=True)]
    reduce_scatter x2 -> x0, waiting for transfers between devices: 63.4 us -> none  [the longest x1 35.9 us: per_device(): lax.psum_scatter(jnp.dot(normed, w_qkv, preferred_element_type=jnp.float3...]
    reduce_scatter x1, waiting for transfers between devices: 120 us -> 95.9 us  [per_device(): lax.psum_scatter(jnp.dot(hidden, w_down, preferred_element_type=jnp.float...]
    unnamed x91 -> x43, local copies, waits for them, and re-layouts: 36.6 us -> 19.9 us
    dot_general x7 -> x3, matrix products: 22.1 us -> 6.13 us  [the longest x1 2.65 us: per_device(): jnp.einsum('htk,thd->kd', weights, grad_mixed, preferred_element_type=jnp...]
    reduce_scatter x2, waiting for transfers between devices: 194 us -> 208 us  [summed(): block = lax.psum_scatter(blocks, 'ctx', scatter_dimension=0, tiled=True)[0]]
  transfers between devices with their start and end apart: 25 -> 16, of which waited for: 17 -> 11; matrix products, arithmetic and copies ran while one was open for 14% -> 11% of each run, Pallas kernels for 0% -> 0%
where the time goes in v2:
time: 1320 us; the launch traced here: 1310 us
  waiting for transfers between devices  764 us (58%)
  Pallas kernels  276 us (21%)
  matrix products  107 us (8%)
  local copies, waits for them, and re-layouts  74.4 us (6%)
  other arithmetic  44.2 us (3%)
  starting transfers between devices  15.7 us (1%)
  between operations  14.8 us (1%)
    pallas_call x1, Pallas kernels, front(): pl.pallas_call(functools.partial(front_kernel, lines), out_shape=(shape((...  276 us
    reduce_scatter x2, waiting for transfers between devices, summed(): block = lax.psum_scatter(blocks, 'ctx', scatter_dimension=0, tiled=True)[0]  208 us
    unnamed x13, waiting for transfers between devices  175 us
    reduce_scatter x1, waiting for transfers between devices, per_device(): lax.psum_scatter(contract_rows(grad_gate_up, w_gate_up).astype(jnp.bfloat...  100 us
    reduce_scatter x1, waiting for transfers between devices, per_device(): lax.psum_scatter(jnp.dot(hidden, w_down, preferred_element_type=jnp.float...  95.9 us
    all_gather x1, waiting for transfers between devices, per_device(): normed_two = lax.all_gather(normed_two, 'ctx', axis=0, tiled=True)  74.7 us
    reduce_scatter x1, waiting for transfers between devices, per_device(): lax.psum_scatter(jnp.concatenate([grad_keys, grad_values], axis=1).astype...  59.2 us
    dot_general x4, matrix products, contract_tokens(): lax.dot_general(left, right, (((0,), (0,)), ((), ())), preferred_element_...  37.7 us
  transfers between devices with their start and end apart: 16, of which 11 were waited for; matrix products, arithmetic and copies ran while one was open for 11% of the time, Pallas kernels for 0%

profile of v2, /device:TPU:4, one launch (start us, length us, event | category | flops | bytes accessed | tf_op | source)
XLA Modules:
  0.0 1308.8 jit_solution(16929676469471232126)
XLA Ops:
  14.8 3.2 constant_dynamic-slice_fusion.1
  21.7 275.6 %front.1 = (bf16[4,128,640]{2,1,0:T(8,128)(2,1)}, bf16[10,128,256]{2,1,0:T(8,128)(2,1)}, bf16[8,128,512]{2,1,0:T(8,128)(2,1)}, bf16[10,128,1024]{2,1,0:T(8,128)(...) custom-call(bf16[128,2560]{1,0:T(8,128)(2,1)} %bitcast.111, ...), custom_call_target="tpu_custom_call" | custom-call | tf_op jit(solution)/shard_map/front/pallas_call | solution.py:700
  297.6 10.4 fusion.63
  308.0 74.7 %all-gather.4.cloned.1.call-done = bf16[1024,2560]{1,0:T(8,128)(2,1)} async-done(((bf16[128,2560]{1,0:T(8,128)(2,1)}), bf16[1024,2560]{1,0:T(8,128)(2,1)}) %all-gather.4.cloned.1.call-update) | async-done | bytes 5242896 | tf_op jit(solution)/shard_map/all_gather | solution.py:828
  382.6 15.4 %fusion.62 = f32[1024,2048]{1,0:T(8,128)S(1)} fusion(bf16[1024,2560]{1,0:T(8,128)(2,1)} %all-gather.4.cloned.1.call-done, bf16[2560,2048]{1,0:T(8,128)(2,1)} %bitcast.128), kind=kOutput, calls=%fused_computation.126 | convolution fusion | flops 10737418240 | bytes 24117248 | tf_op jit(solution)/shard_map/dot_general | solution.py:829
  398.0 5.3 fusion.10
  405.3 15.3 %convolution_convert_fusion.1 = bf16[1024,2560]{1,0:T(8,128)(2,1)} fusion(bf16[2560,2048]{1,0:T(8,128)(2,1)} %bitcast.129, bf16[1024,1024]{1,0:T(8,128)(2,1)S(1)} %get-tuple-element.36, bf16[1024,1024]{1,0:T(8,128)(2,1)S(1)} %get-tuple-element.35), kind=kOutput, calls=%fused_computation.5 | convolution fusion | flops 10748428288 | bytes 19922944 | tf_op jit(solution)/shard_map/dot_general | solution.py:47
  422.1 100.3 %reduce-scatter.15.cloned.1.call-done = bf16[128,2560]{1,0:T(8,128)(2,1)} async-done(((bf16[1024,2560]{1,0:T(8,128)(2,1)}), bf16[128,2560]{1,0:T(8,128)(2,1)}) %reduce-scatter.15.cloned.1.call-update) | async-done | bytes 655376 | tf_op jit(solution)/shard_map/reduce_scatter | solution.py:835
  524.1 2.4 fusion.57
  526.6 25.4 %all-gather.6.cloned.1.call-done = bf16[512,2560]{1,0:T(8,128)(2,1)} async-done(((bf16[128,2560]{1,0:T(8,128)(2,1)}), bf16[512,2560]{1,0:T(8,128)(2,1)}) %all-gather.6.cloned.1.call-update) | async-done | bytes 2621456 | tf_op jit(solution)/shard_map/all_gather | solution.py:877
  552.0 4.9 convolution_convert_fusion.6
  557.3 12.9 all_to_all.34
  570.2 2.7 fusion.34
  577.8 2.6 fusion.39
  581.3 59.2 %reduce-scatter.17.cloned.1.call-done = bf16[128,512]{1,0:T(8,128)(2,1)} async-done(((bf16[1024,512]{1,0:T(8,128)(2,1)}), bf16[128,512]{1,0:T(8,128)(2,1)}) %reduce-scatter.17.cloned.1.call-update) | async-done | bytes 131088 | tf_op jit(solution)/shard_map/reduce_scatter | solution.py:893
  644.9 16.7 %convolution_convert_fusion = bf16[2560,2048]{1,0:T(8,128)(2,1)} fusion(bf16[1024,2560]{1,0:T(8,128)(2,1)} %all-gather.4.cloned.1.call-done, bf16[1024,1024]{1,0:T(8,128)(2,1)} %copy-done.8, bf16[1024,1024]{1,0:T(8,128)(2,1)} %copy-done.7), kind=kOutput, calls=%fused_computation | convolution fusion | flops 10751049728 | bytes 19922944 | tf_op jit(solution)/shard_map/dot_general | solution.py:53
  662.7 5.4 convolution_convert_fusion.4
  668.1 6.7 reshape.180
  674.8 4.0 copy.87
  678.9 5.0 fusion.11
  684.0 11.1 convolution_convert_fusion.3
  695.1 7.9 copy.100
  703.3 9.7 convolution_convert_fusion.2
  714.3 6.4 fusion.20
  720.7 4.2 all-to-all-start.1
  725.0 4.4 convolution_convert_fusion.5
  729.4 2.1 slice.123
  732.4 6.7 reshape.175
  739.2 4.2 copy.85
  747.9 4.4 pad_maximum_fusion.1
  752.3 15.7 %reduce-scatter.23.cloned.1.call-done = bf16[2560,512]{1,0:T(8,128)(2,1)} async-done(((bf16[2560,2048]{1,0:T(8,128)(2,1)}), bf16[2560,512]{1,0:T(8,128)(2,1)}) %reduce-scatter.23.cloned.1.call-update) | async-done | bytes 2621456 | tf_op jit(solution)/shard_map/reduce_scatter | solution.py:855
  768.0 6.1 all-to-all-start.2
  774.1 116.2 %reduce-scatter.21.cloned.1.call-done = bf16[1,320,640]{2,1,0:T(8,128)(2,1)} async-done(((bf16[8,320,640]{2,1,0:T(8,128)(2,1)}), bf16[1,320,640]{2,1,0:T(8,128)(2,1)}) %reduce-scatter.21.cloned.1.call-update) | async-done | bytes 409616 | tf_op jit(solution)/shard_map/reduce_scatter | solution.py:927
  890.3 2.2 collective-permute-start.1
  892.4 51.0 %reduce-scatter.27.cloned.1.call-done = bf16[640,960]{1,0:T(8,128)(2,1)} async-done(((bf16[2560,960]{1,0:T(8,128)(2,1)}), bf16[640,960]{1,0:T(8,128)(2,1)}) %reduce-scatter.27.cloned.1.call-update) | async-done | bytes 1228816
  943.4 2.4 copy.101
  945.9 2.9 convert_element_type.166
  948.8 1.9 convert_element_type.160
  950.7 3.4 dynamic-slice_bitcast_fusion.1
  954.1 95.9 %reduce-scatter.13.cloned.1.call-done = bf16[128,2560]{1,0:T(8,128)(2,1)} async-done(((bf16[1024,2560]{1,0:T(8,128)(2,1)}), bf16[128,2560]{1,0:T(8,128)(2,1)}) %reduce-scatter.13.cloned.1.call-update) | async-done | bytes 655376 | tf_op jit(solution)/shard_map/reduce_scatter | solution.py:841
  1050.0 3.6 fusion.37
  1053.6 124.1 %reduce-scatter.25.cloned.1.call-done = f32[80,2]{1,0:T(8,128)} async-done(((f32[2560,2]{1,0:T(8,128)}), f32[80,2]{1,0:T(8,128)}) %reduce-scatter.25.cloned.1.call-update) | async-done | bytes 656
  1179.7 92.2 %reduce-scatter.19.cloned.1.call-done = bf16[1,320,768]{2,1,0:T(8,128)(2,1)} async-done(((bf16[8,320,768]{2,1,0:T(8,128)(2,1)}), bf16[1,320,768]{2,1,0:T(8,128)(2,1)}) %reduce-scatter.19.cloned.1.call-update) | async-done | bytes 491536 | tf_op jit(solution)/shard_map/reduce_scatter | solution.py:927
  1272.0 1.9 collective-permute-start
  1273.9 2.9 fusion.17
  1277.8 5.7 copy.89
  1283.5 7.4 reshape.185
  1290.9 9.3 collective-permute-done
  (119 shorter events, 40.0 us)
Async XLA Ops:
  7.2 375.5 %all-gather.4.cloned.1.call-start = ((), (), s32[]{:S(2)}) async-start(), calls=%async_computation.11 | async-start | bytes 5898240 | tf_op jit(solution)/shard_map/all_gather | solution.py:828
  297.3 225.1 %reduce-scatter.15.cloned.1.call-start = ((), (), s32[]{:S(2)}) async-start(), calls=%async_computation.13 | async-start | bytes 5898240 | tf_op jit(solution)/shard_map/reduce_scatter | solution.py:835
  382.6 15.4 %copy-start.4 = (f32[1024,960]{1,0:T(8,128)S(1)}, f32[1024,960]{1,0:T(8,128)}, u32[]{:S(2)}) copy-start(f32[1024,960]{1,0:T(8,128)} %fusion.63) | copy-start | bytes 11796484
  403.3 1.4 copy-start.7
  403.3 2.0 copy-start.8
  420.6 1.3 copy-start
  420.6 101.8 %copy-start.14 = (f32[2560]{0:T(1024)S(1)}, f32[2560]{0:T(1024)}, u32[]{:S(2)}) copy-start(f32[2560]{0:T(1024)} %param.17) | copy-start | bytes 30724
  420.6 103.5 %copy-start.3 = (bf16[1,128,2560]{2,1,0:T(8,128)(2,1)S(1)}, bf16[1,128,2560]{2,1,0:T(8,128)(2,1)}, u32[]{:S(2)}) copy-start(bf16[1,128,2560]{2,1,0:T(8,128)(2,1)} %param.12) | copy-start | bytes 1966084
  420.6 131.4 %all-gather.6.cloned.1.call-start = ((), (), s32[]{:S(2)}) async-start(), calls=%async_computation.14 | async-start | bytes 3276800 | tf_op jit(solution)/shard_map/all_gather | solution.py:877
  526.6 114.0 %reduce-scatter.17.cloned.1.call-start = ((), (), s32[]{:S(2)}) async-start(), calls=%async_computation.15 | async-start | bytes 1179648 | tf_op jit(solution)/shard_map/reduce_scatter | solution.py:893
  557.3 15.6 %copy-start.1 = (bf16[10,128,1024]{2,1,0:T(8,128)(2,1)S(1)}, bf16[10,128,1024]{2,1,0:T(8,128)(2,1)}, u32[]{:S(2)}) copy-start(bf16[10,128,1024]{2,1,0:T(8,128)(2,1)} %get-tuple-element.24) | copy-start | bytes 7864324
  557.3 15.6 %copy-start.12 = (bf16[8,128,512]{2,1,0:T(8,128)(2,1)S(1)}, bf16[8,128,512]{2,1,0:T(8,128)(2,1)}, u32[]{:S(2)}) copy-start(bf16[8,128,512]{2,1,0:T(8,128)(2,1)} %get-tuple-element.25) | copy-start | bytes 3145732
  574.0 1.1 copy-start.18
  574.7 1.5 copy-start.6
  576.2 1.6 copy-start.13
  577.3 3.4 copy-start.10
  577.3 3.4 copy-start.11
  577.3 137.0 %all-gather.8.cloned.1.call-start = ((), (), s32[]{:S(2)}) async-start(), calls=%async_computation.16 | async-start | bytes 3932160 | tf_op jit(solution)/shard_map/all_gather | solution.py:913
  644.6 123.4 %reduce-scatter.23.cloned.1.call-start = ((), (), s32[]{:S(2)}) async-start(), calls=%async_computation.19 | async-start | bytes 13107200 | tf_op jit(solution)/shard_map/reduce_scatter | solution.py:855
  661.6 1.1 copy-start.17
  661.6 228.6 %reduce-scatter.21.cloned.1.call-start = ((), (), s32[]{:S(2)}) async-start(), calls=%async_computation.18 | async-start | bytes 3686400 | tf_op jit(solution)/shard_map/reduce_scatter | solution.py:927
  678.9 264.6 %reduce-scatter.27.cloned.1.call-start = ((), (), s32[]{:S(2)}) async-start(), calls=%async_computation.21 | async-start | bytes 6553600
  703.0 347.0 %reduce-scatter.13.cloned.1.call-start = ((), (), s32[]{:S(2)}) async-start(), calls=%async_computation.12 | async-start | bytes 5898240 | tf_op jit(solution)/shard_map/reduce_scatter | solution.py:841
  713.0 1.1 copy-start.2
  713.0 1.4 copy-start.9
  714.3 10.7 copy-start.16
  720.7 23.7 %all-to-all-start.1 = ((bf16[4,128,640]{2,1,0:T(8,128)(2,1)}), bf16[4,128,640]{2,1,0:T(8,128)(2,1)}, u32[]{:S(2)}, u32[]{:S(2)}) async-start(bf16[4,128,640]{2,1,0:T(8,128)(2,1)} %bitcast.19), calls=%async_computation.4 | async-start | bytes 1310720 | tf_op jit(solution)/shard_map/all_to_all | solution.py:824
  724.9 452.7 %reduce-scatter.25.cloned.1.call-start = ((), (), s32[]{:S(2)}) async-start(), calls=%async_computation.20 | async-start | bytes 1351680
  729.4 3.0 copy-start.5
  739.2 4.2 slice-start
  743.5 2.3 copy-start.15
  747.9 524.1 %reduce-scatter.19.cloned.1.call-start = ((), (), s32[]{:S(2)}) async-start(), calls=%async_computation.17 | async-start | bytes 4423680 | tf_op jit(solution)/shard_map/reduce_scatter | solution.py:927
  768.0 182.7 %all-to-all-start.2 = ((bf16[8,320,512]{2,1,0:T(8,128)(2,1)}), bf16[8,320,512]{2,1,0:T(8,128)(2,1)}, u32[]{:S(2)}, u32[]{:S(2)}) async-start(bf16[8,320,512]{2,1,0:T(8,128)(2,1)} %bitcast.117), calls=%async_computation.8 | async-start | bytes 5242880 | tf_op jit(solution)/shard_map/all_to_all | solution.py:861
  890.3 58.5 %collective-permute-start.1 = (bf16[320,640]{1,0:T(8,128)(2,1)}, bf16[320,640]{1,0:T(8,128)(2,1)}, u32[]{:S(2)}, u32[]{:S(2)}) collective-permute-start(bf16[320,640]{1,0:T(8,128)(2,1)} %bitcast.135), channel_id=1, source_target_pairs={{0,0},{1,8},{2,16},{3,24},{4,1},{5,9},{6,17},{7,25},{8,2},{9,10},{... | collective-permute-start | bytes 1228808 | tf_op jit(solution)/shard_map/ppermute | solution.py:934
  954.1 319.8 %collective-permute-start.2 = (bf16[4,320,512]{2,1,0:T(8,128)(2,1)}, bf16[4,320,512]{2,1,0:T(8,128)(2,1)}, u32[]{:S(2)}, u32[]{:S(2)}) collective-permute-start(bf16[4,320,512]{2,1,0:T(8,128)(2,1)} %get-tuple-element.40), channel_id=1, source_target_pairs={{0,1},{1,0},{2,3},{3,2},{4,5},{5,4},{6,7},{7,6},{8,9},{9,8},{10,11... | collective-permute-start | bytes 3932168 | tf_op jit(solution)/shard_map/ppermute | solution.py:868
  1272.0 28.2 %collective-permute-start = (bf16[320,768]{1,0:T(8,128)(2,1)}, bf16[320,768]{1,0:T(8,128)(2,1)S(1)}, u32[]{:S(2)}, u32[]{:S(2)}) collective-permute-start(bf16[320,768]{1,0:T(8,128)(2,1)} %bitcast.134), channel_id=1, source_target_pairs={{0,0},{1,8},{2,16},{3,24},{4,1},{5,9},{6,17},{7,25},{8,2},{9,10},{... | collective-permute-start | bytes 1474568 | tf_op jit(solution)/shard_map/ppermute | solution.py:934
Sparse Core Ops, SparseCore 0:
  297.4 85.1 all-gather.3
  420.8 101.6 reduce-scatter.14
  526.7 25.3 all-gather.5
  577.4 63.1 reduce-scatter.16
  644.8 28.2 all-gather.7
  675.6 92.3 reduce-scatter.22
  772.0 118.1 reduce-scatter.20
  892.8 50.5 reduce-scatter.26
  947.4 102.5 reduce-scatter.12
  1052.2 125.4 reduce-scatter.24
  1181.9 90.0 reduce-scatter.18

commit v3 on v2

--- a/solution.py
+++ b/solution.py
@@ -16,7 +16,7 @@
 bf16 = jnp.bfloat16
 VMEM = pltpu.VMEM
 DMA = pltpu.SemaphoreType.DMA
-vmem_bytes = 58 * 1024 * 1024
+vmem_bytes = 62 * 1024 * 1024
 
 
 def rms_norm(values, gain):
@@ -243,13 +243,13 @@
         for turn in range(min(2, self.p.lines)):
             self.across(turn).start()
 
-    def turn(self, turn):
+    def turn(self, turn, ahead=2):
         p = self.p
         t = self.order(turn)
         at = 2 * t + p.lane
         self.across(turn).wait_recv()
-        if turn + 2 < p.lines:
-            self.across(turn + 2).start()
+        if ahead and turn + ahead < p.lines:
+            self.across(turn + ahead).start()
         self.add(at, self.side[t])
 
         @pl.when(t > p.line)
@@ -331,16 +331,23 @@
         self.out[:, cols] = (mine + self.near[0, :, cols].astype(f32)).astype(bf16)
         self.to_cross(i, cols).start()
 
-    def take(self, i, cols):
+    def take(self, i, cols, own=None):
         self.to_twin(i, 1, cols).wait_recv()
-        near = self.parts[self.p.f, :, cols].astype(f32) + self.near[1, :, cols].astype(f32)
+        own = self.parts[self.p.f, :, cols] if own is None else own
+        near = own.astype(f32) + self.near[1, :, cols].astype(f32)
         self.to_cross(i, cols).wait_recv()
         return near + self.far[:, cols].astype(f32)
 
-    def finish(self, i, cols):
+    def given(self, i, cols):
         self.to_twin(i, 0, cols).wait_send()
         self.to_twin(i, 1, cols).wait_send()
+
+    def passed(self, i, cols):
         self.to_cross(i, cols).wait_send()
+
+    def finish(self, i, cols):
+        self.given(i, cols)
+        self.passed(i, cols)
 
 
 class GroupTrade:
@@ -389,7 +396,7 @@
     )
 
 
-class WeightColumns:
+class GroupGather:
     sems = 6
 
     def __init__(self, place, own, whole, sems, own_sem, pieces):
@@ -435,74 +442,6 @@
         self.to_twin(i).wait_send()
         self.to_cross(i).wait_send()
         self.forward(i).wait_send()
-
-
-class WeightRows:
-    sems = 3
-
-    def __init__(self, place, held, whole, sems, own_sem, pieces):
-        per_owner = place.lines * 2 // 4
-        self.p, self.held, self.whole, self.s, self.own_sem = place, held, whole, sems, own_sem
-        self.rows = whole.shape[0]
-        self.pieces, self.n = pieces, whole.shape[0] // pieces
-        self.first = (place.c % per_owner) * self.rows
-        owner = place.c // per_owner
-        self.is_owner = place.f == owner
-        self.is_cross = place.f == (owner + 2) % 4
-        self.is_last = (place.f != owner) & (place.f != (owner + 2) % 4)
-
-    def source(self, i):
-        return self.held.at[pl.ds(pl.multiple_of(self.first + i * self.n, 16), self.n)]
-
-    def slot(self, i):
-        return self.whole.at[pl.ds(i * self.n, self.n)]
-
-    def local(self):
-        return pltpu.make_async_copy(
-            self.held.at[pl.ds(pl.multiple_of(self.first, 16), self.rows)], self.whole, self.own_sem
-        )
-
-    def to_cross(self, i):
-        return remote(self.source(i), self.slot(i), self.s.at[0, i], self.s.at[2, i], self.p.cross)
-
-    def to_twin(self, i):
-        return remote(self.source(i), self.slot(i), self.s.at[1, i], self.s.at[2, i], self.p.twin)
-
-    def forward(self, i):
-        slot = self.slot(i)
-        return remote(slot, slot, self.s.at[1, i], self.s.at[2, i], self.p.twin)
-
-    def start(self):
-        @pl.when(self.is_owner)
-        def _():
-            self.local().start()
-            for i in range(self.pieces):
-                self.to_cross(i).start()
-                self.to_twin(i).start()
-
-    def pass_on(self, i):
-        @pl.when(self.is_cross)
-        def _():
-            self.forward(i).wait_recv()
-            self.forward(i).start()
-
-    def finish(self):
-        @pl.when(self.is_owner)
-        def _():
-            self.local().wait()
-            for i in range(self.pieces):
-                self.to_cross(i).wait_send()
-                self.to_twin(i).wait_send()
-
-        @pl.when(self.is_cross)
-        def _():
-            for i in range(self.pieces):
-                self.forward(i).wait_send()
-
-        @pl.when(self.is_last)
-        def _():
-            for i in range(self.pieces):
-                self.forward(i).wait_recv()
 
 
 def tiles_of(first, count, tile):
@@ -530,7 +469,6 @@
     w_query,
     w_out,
     cot,
-    w_columns,
     w_rows,
     normed_out,
     query_out,
@@ -540,7 +478,6 @@
     middle_out,
     normed_two_out,
     cot_all,
-    columns_all,
     rows_all,
     whole,
     slots,
@@ -554,7 +491,6 @@
     sum_sems,
     keyval_sems,
     cot_sems,
-    column_sems,
     row_sems,
     own_sems,
 ):
@@ -565,16 +501,15 @@
     kv_width = 2 * HD
     p.barrier()
 
-    columns = WeightColumns(p, w_columns, columns_all, column_sems, own_sems.at[0], column_sems.shape[1])
-    down = WeightRows(p, w_rows, rows_all, row_sems, own_sems.at[1], row_sems.shape[1])
+    down = GroupGather(p, w_rows, rows_all, row_sems, own_sems.at[0], row_sems.shape[1])
     cot_gather = LineGather(p, cot, cot_all, cot_sems)
-    cot_local = pltpu.make_async_copy(cot, cot_all.at[p.c], own_sems.at[2])
+    cot_local = pltpu.make_async_copy(cot, cot_all.at[p.c], own_sems.at[1])
 
     source = x_ref[...].astype(f32)
     whole[...] = rms_norm(source, gain_one[...]).astype(bf16)
     trade = GroupTrade(p, whole, slots.at[0], trade_sems.at[0], slots.shape[3])
     trade.start()
-    columns.local().start()
+    down.local().start()
     cot_local.start()
     cot_gather.start()
     trade.wait()
@@ -603,6 +538,7 @@
     group.give(2, spans[2])
     group.pass_on(1, spans[1])
     group.pass_on(2, spans[2])
+    cot_gather.step(0)
 
     linear = group.take(0, spans[0])
     keyval[p.c] = jnp.concatenate(
@@ -618,11 +554,13 @@
             query_out[at] = (turned * HD**-0.5).astype(bf16)
         if i == 1:
             kv_gather.step(0)
-    for i in range(columns.pieces):
-        columns.give(i)
+    for i in range(down.pieces):
+        down.give(i)
     for step in range(1, lines - 1):
         kv_gather.step(step)
     kv_gather.finish()
+    if lines > 2:
+        cot_gather.step(1)
     keyval_out[...] = keyval[...]
 
     length = bias.shape[1]
@@ -646,7 +584,7 @@
     lax.fori_loop(0, heads // 2, two_heads, 0)
     trade_two = GroupTrade(p, mixed, slots.at[1], trade_sems.at[1], slots.shape[3])
     trade_two.start()
-    for step in range(lines - 1):
+    for step in range(2, lines - 1):
         cot_gather.step(step)
     for i in range(len(chunks)):
         group.finish(i, spans[i])
@@ -667,24 +605,20 @@
         )
     normed_two_out[...] = rms_norm(middle_out[...], gain_two[...]).astype(bf16)
 
-    down.start()
-    for i in range(columns.pieces):
-        columns.pass_on(i)
     for i in range(down.pieces):
         down.pass_on(i)
     for i in range(2):
         group_two.finish(i, spans_two[i])
     trade.finish()
     trade_two.finish()
-    columns.local().wait()
+    down.local().wait()
     cot_local.wait()
-    for i in range(columns.pieces):
-        columns.finish(i)
-    down.finish()
+    for i in range(down.pieces):
+        down.finish(i)
     cot_gather.finish()
 
 
-def front(lines, operands, part_width, heads):
+def front(lines, operands, heads):
     x = operands[0]
     rows, width = x.shape
     places = 2 * lines
@@ -695,7 +629,7 @@
     in_vmem = pl.BlockSpec(memory_space=VMEM)
     anywhere = pl.BlockSpec(memory_space=pl.ANY)
     shape = jax.ShapeDtypeStruct
-    pieces = 4
+    pieces = 2
     assert inner == width
     return pl.pallas_call(
         functools.partial(front_kernel, lines),
@@ -709,10 +643,9 @@
             shape((rows, width), bf16),
             shape((places, rows, width), bf16),
             shape((4,) + operands[10].shape, bf16),
-            shape((part_width, width), bf16),
         ),
-        in_specs=[in_vmem] * 9 + [anywhere] * 3,
-        out_specs=[in_vmem] * 7 + [anywhere] * 3,
+        in_specs=[in_vmem] * 9 + [anywhere] * 2,
+        out_specs=[in_vmem] * 7 + [anywhere] * 2,
         scratch_shapes=[
             VMEM((rows, width), bf16),
             VMEM((2, 4, rows, shard), bf16),
@@ -726,14 +659,268 @@
             DMA((2, GroupSum.sems, 3)),
             DMA((LineGather.sems, lines)),
             DMA((LineGather.sems, lines)),
-            DMA((WeightColumns.sems, pieces)),
-            DMA((WeightRows.sems, 3)),
-            DMA((3,)),
+            DMA((GroupGather.sems, pieces)),
+            DMA((2,)),
         ],
         compiler_params=pltpu.CompilerParams(
             collective_id=0, has_side_effects=True, vmem_limit_bytes=vmem_bytes
         ),
         name="front",
+    )(*operands)
+
+
+def gelu_parts(v):
+    k = 0.7978845608028654
+    square = v * v
+    inner = jnp.tanh(k * v * (1.0 + 0.044715 * square))
+    half = 0.5 * (1.0 + inner)
+    slope = half + 0.5 * v * (1.0 - inner * inner) * (k * (1.0 + 3 * 0.044715 * square))
+    return v * half, slope
+
+
+def norm_back(values, gain, grad):
+    r = lax.rsqrt(jnp.mean(values * values, axis=-1, keepdims=True) + epsilon)
+    scaled = values * r
+    inner = grad * gain
+    grad_values = r * (inner - scaled * jnp.mean(inner * scaled, axis=-1, keepdims=True))
+    return grad_values, jnp.sum(grad * scaled, axis=0, keepdims=True)
+
+
+def middle_kernel(
+    lines,
+    cot_all,
+    w_rows,
+    gain_two,
+    own,
+    middle,
+    w_columns,
+    grad_middle_out,
+    gain_out,
+    grads_out,
+    down_out,
+    normed_all_out,
+    result_parts,
+    normed_all,
+    weights,
+    grad_hidden,
+    hidden,
+    parts,
+    side,
+    chain,
+    down_near,
+    down_stage,
+    down_far,
+    gather_sems,
+    column_sems,
+    sum_sems,
+    down_sems,
+    own_sems,
+):
+    p = Place(lines)
+    rows, width = own.shape
+    two = 2 * rows
+    padded = hidden.shape[2]
+    shard = width // 4
+    tile = 256 if padded % 256 == 0 else 128
+    p.barrier()
+
+    columns = GroupGather(p, w_columns, weights, column_sems, own_sems.at[0], column_sems.shape[1])
+    gather = LineGather(p, own, normed_all, gather_sems)
+    gather.start()
+    for i in range(columns.pieces):
+        columns.give(i)
+    columns.local().start()
+    own_local = pltpu.make_async_copy(own, normed_all.at[p.c], own_sems.at[2 + lines])
+    own_local.start()
+    middle_local = pltpu.make_async_copy(middle, grad_middle_out, own_sems.at[3 + lines])
+    middle_local.start()
+
+    def hidden_grad(line):
+        def one(i, carry):
+            cols = pl.ds(pl.multiple_of(i * tile, 128), tile)
+            left = cot_all[pl.ds(2 * line, 2)].reshape(two, width)
+            right = w_rows[pl.ds(pl.multiple_of(i * tile, 16), tile)]
+            grad_hidden[line, :, cols] = contract_rows(left, right)
+            return carry
+
+        lax.fori_loop(0, padded // tile, one, 0)
+
+    done = 0
+    for step in range(lines - 1):
+        hidden_grad(done)
+        done += 1
+        gather.step(step)
+        if step < columns.pieces:
+            columns.pass_on(step)
+    for i in range(lines - 1, columns.pieces):
+        columns.pass_on(i)
+    while done < lines:
+        hidden_grad(done)
+        done += 1
+    gather.finish()
+    own_local.wait()
+    columns.local().wait()
+    for i in range(columns.pieces):
+        columns.finish(i)
+    normed_local = pltpu.make_async_copy(normed_all, normed_all_out, own_sems.at[1])
+    normed_local.start()
+
+    line_sum = LineSum(p, parts, side, chain, sum_sems)
+
+    def feed_forward(line):
+        def one(i, carry):
+            cols = pl.ds(pl.multiple_of(i * tile, 128), tile)
+            up_cols = pl.ds(pl.multiple_of(i * tile + padded, 128), tile)
+            left = normed_all[pl.ds(2 * line, 2)].reshape(two, width)
+            gate = jnp.dot(
+                left, weights[:, :, cols].reshape(width, tile), preferred_element_type=f32
+            )
+            up = jnp.dot(
+                left, weights[:, :, up_cols].reshape(width, tile), preferred_element_type=f32
+            )
+            gelu, slope = gelu_parts(gate)
+            grad = grad_hidden[line, :, cols]
+            hidden[line, :, cols] = (gelu * up).astype(bf16)
+            grads_out[line, :, cols] = (grad * up * slope).astype(bf16)
+            grads_out[line, :, up_cols] = (grad * gelu).astype(bf16)
+            return carry
+
+        lax.fori_loop(0, padded // tile, one, 0)
+
+        def back(g, carry):
+            product = contract_rows(grads_out[line], weights[g]).astype(bf16)
+            cols = pl.ds(pl.multiple_of(g * shard, 128), shard)
+            parts[pl.ds(2 * line, 2), :, cols] = product.reshape(2, rows, shard)
+            return carry
+
+        lax.fori_loop(0, 4, back, 0)
+
+    result_stage = normed_all
+
+    def result_copy(line):
+        blocks = pl.ds(2 * line, 2)
+        return pltpu.make_async_copy(
+            result_stage.at[blocks], result_parts.at[blocks], own_sems.at[2 + line]
+        )
+
+    def result_part(line):
+        def one(i, carry):
+            cols = pl.ds(pl.multiple_of(i * shard, 128), shard)
+            product = jnp.dot(
+                hidden[line], w_rows[:, cols], preferred_element_type=f32
+            ).astype(bf16)
+            result_stage[pl.ds(2 * line, 2), :, cols] = product.reshape(2, rows, shard)
+            return carry
+
+        lax.fori_loop(0, 4, one, 0)
+        result_copy(line).start()
+
+    quarter = padded // 4
+    every = slice(None)
+    down_parts = weights.at[:, pl.ds(0, quarter), pl.ds(0, shard)]
+
+    def down_group(i):
+        return GroupSum(p, down_parts, down_near.at[i], down_stage.at[i % 2], down_far.at[i], down_sems)
+
+    def down_chunk(i):
+        def one(g, carry):
+            cols = pl.ds(pl.multiple_of(g * shard, 128), shard)
+            left = hidden[:, :, i * quarter : (i + 1) * quarter].reshape(lines * two, quarter)
+            right = cot_all[:, :, cols].reshape(lines * two, shard)
+            down_parts[g] = contract_tokens(left, right).astype(bf16)
+            return carry
+
+        lax.fori_loop(0, 4, one, 0)
+        down_out[i] = down_parts[p.f]
+        down_group(i).give(i, every)
+
+    for turn in range(lines):
+        feed_forward(line_sum.order(turn))
+        line_sum.across(turn).start()
+        if turn > 0:
+            line_sum.turn(turn - 1, 0)
+    normed_local.wait()
+
+    for i in range(4):
+        if i >= 1:
+            down_group(i - 1).given(i - 1, every)
+        if i >= 2:
+            down_out[i - 2] = down_group(i - 2).take(i - 2, every, down_out[i - 2]).astype(bf16)
+            down_group(i - 2).passed(i - 2, every)
+        down_chunk(i)
+        if i < lines:
+            result_part(i)
+        down_group(i).pass_on(i, every)
+    for line in range(4, lines):
+        result_part(line)
+    line_sum.turn(lines - 1, 0)
+    grad = line_sum.total()
+    middle_local.wait()
+    grad_values, gain = norm_back(grad_middle_out[...], gain_two[...], grad)
+    grad_middle_out[...] = cot_all[p.c].astype(f32) + grad_values
+    gain_out[...] = gain
+    for i in (2, 3):
+        down_out[i] = down_group(i).take(i, every, down_out[i]).astype(bf16)
+        down_group(i).passed(i, every)
+    down_group(3).given(3, every)
+    for line in range(lines):
+        result_copy(line).wait()
+    line_sum.finish()
+
+
+def middle_bytes(lines, rows, width, padded):
+    length = 2 * lines * rows
+    return (
+        14 * rows * width
+        + 9 * length * width
+        + 9 * padded * width
+        + 10 * length * padded
+    )
+
+
+def middle_part(lines, operands, padded):
+    own = operands[3]
+    rows, width = own.shape
+    places = 2 * lines
+    shard = width // 4
+    quarter = padded // 4
+    pieces = 4
+    in_vmem = pl.BlockSpec(memory_space=VMEM)
+    anywhere = pl.BlockSpec(memory_space=pl.ANY)
+    shape = jax.ShapeDtypeStruct
+    return pl.pallas_call(
+        functools.partial(middle_kernel, lines),
+        out_shape=(
+            shape((rows, width), f32),
+            shape((1, width), f32),
+            shape((lines, 2 * rows, 2 * padded), bf16),
+            shape((4, quarter, shard), bf16),
+            shape((places, rows, width), bf16),
+            shape((places, rows, width), bf16),
+        ),
+        in_specs=[in_vmem] * 3 + [anywhere] * 3,
+        out_specs=[in_vmem] * 4 + [anywhere] * 2,
+        scratch_shapes=[
+            VMEM((places, rows, width), bf16),
+            VMEM((4, shard, 2 * padded), bf16),
+            VMEM((lines, 2 * rows, padded), f32),
+            VMEM((lines, 2 * rows, padded), bf16),
+            VMEM((places, rows, width), bf16),
+            VMEM((lines, rows, width), bf16),
+            VMEM((2, lines - 1, rows, width), bf16),
+            VMEM((4, 2, quarter, shard), bf16),
+            VMEM((2, quarter, shard), bf16),
+            VMEM((4, quarter, shard), bf16),
+            DMA((LineGather.sems, lines)),
+            DMA((GroupGather.sems, pieces)),
+            DMA((LineSum.sems, lines)),
+            DMA((GroupSum.sems, 4)),
+            DMA((4 + lines,)),
+        ],
+        compiler_params=pltpu.CompilerParams(
+            collective_id=1, has_side_effects=True, vmem_limit_bytes=vmem_bytes
+        ),
+        name="middle",
     )(*operands)
 
 
@@ -758,8 +945,9 @@
     inner_width = query_weight.shape[1]
     head_count = inner_width // HD
     hidden_width = gate_up_weight.shape[1] // 2
-    part_width = hidden_width // ctx_size
-    padded = -(-part_width // 128) * 128
+    piece = hidden_width // (ctx_size * fsdp_size)
+    padded_piece = -(-piece // 32) * 32
+    padded = padded_piece * fsdp_size
     ctx_place = lax.axis_index("ctx")
     source = tokens[0].astype(jnp.float32)
     bounds = doc_bounds[0]
@@ -773,13 +961,25 @@
     cosine = jnp.concatenate([cosine, cosine], axis=1)
     sine = jnp.concatenate([-sine, sine], axis=1)
 
-    def own_columns(first):
-        cols = lax.dynamic_slice_in_dim(
-            gate_up_weight, first + ctx_place * part_width, part_width, 1
-        )
-        return jnp.pad(cols, ((0, 0), (0, padded - part_width)))
-
-    w_columns = jnp.concatenate([own_columns(0), own_columns(hidden_width)], axis=1)
+    def padded_to(value, axis):
+        pads = [(0, 0)] * value.ndim
+        pads[axis] = (0, padded_piece - piece)
+        return jnp.pad(value, pads)
+
+    shard_width = hidden_width // fsdp_size
+    w_columns = jnp.concatenate(
+        [
+            padded_to(
+                lax.dynamic_slice_in_dim(
+                    gate_up_weight, q * shard_width + ctx_place * piece, piece, 1
+                ),
+                1,
+            )
+            for q in range(2 * fsdp_size)
+        ],
+        axis=1,
+    )
+    w_rows = padded_to(lax.dynamic_slice_in_dim(down_weight, ctx_place * piece, piece, 0), 0)
     cot_rows = cotangent[0]
     (
         normed,
@@ -790,7 +990,6 @@
         middle,
         normed_two,
         cot_all,
-        w_gate_up,
         w_down,
     ) = front(
         lines,
@@ -805,17 +1004,13 @@
             query_weight,
             out_weight,
             cot_rows,
-            w_columns,
-            down_weight,
+            w_rows,
         ),
-        part_width,
         head_count,
     )
     normed = normed.reshape(fsdp_size * rows, -1)
     mixed = mixed.reshape(fsdp_size * rows, -1)
     window = window.reshape(length, -1)
-    cot_all = cot_all.reshape(length, width)
-    w_gate_up = w_gate_up.reshape(width, 2 * padded)
     key_rows = window[:, :HD]
     value_rows = window[:, HD:]
     w_qkv = jnp.concatenate([query_weight, keyval_weight], axis=1)
@@ -824,56 +1019,66 @@
         return lax.all_to_all(value, "fsdp", split_axis=0, concat_axis=1, tiled=True)
 
     _, norm_back_one = jax.vjp(rms_norm, source, norm_one)
-    _, norm_back_two = jax.vjp(rms_norm, middle, norm_two)
-    normed_two = lax.all_gather(normed_two, "ctx", axis=0, tiled=True)
-    projected = jnp.dot(normed_two, w_gate_up, preferred_element_type=jnp.float32)
-    hidden_full, gelu_back = jax.vjp(gelu_product, projected[:, :padded], projected[:, padded:])
-    hidden = hidden_full.astype(jnp.bfloat16)[:, :part_width]
-    grad_hidden = contract_rows(cot_all, w_down)
-    grad_gate, grad_up = gelu_back(jnp.pad(grad_hidden, ((0, 0), (0, padded - part_width))))
-    grad_gate_up = jnp.concatenate([grad_gate, grad_up], axis=1).astype(jnp.bfloat16)
-    grad_normed_two = lax.psum_scatter(
-        contract_rows(grad_gate_up, w_gate_up).astype(jnp.bfloat16),
-        "ctx",
-        scatter_dimension=0,
-        tiled=True,
-    ).astype(jnp.float32)
-    branch_two = lax.psum_scatter(
-        jnp.dot(hidden, w_down, preferred_element_type=jnp.float32).astype(jnp.bfloat16),
-        "ctx",
-        scatter_dimension=0,
-        tiled=True,
-    ).astype(jnp.float32)
-    result = (middle + branch_two).astype(jnp.bfloat16)
-
-    down_grad = lax.psum_scatter(
-        contract_tokens(hidden, cot_all).astype(jnp.bfloat16),
+    w_down = w_down.reshape(padded, width)
+    if middle_bytes(lines, rows, width, padded) <= vmem_bytes:
+        grad_middle, gain_two_term, grad_gate_up, down_part, normed_two, result_parts = middle_part(
+            lines, (cot_all, w_down, norm_two[None], normed_two, middle, w_columns), padded
+        )
+        gain_two_term = gain_two_term[0]
+        normed_two = normed_two.reshape(length, width)
+        grad_gate_up = grad_gate_up.reshape(length, 2 * padded)
+        result_parts = result_parts.reshape(length, width)
+    else:
+        cot_all = cot_all.reshape(length, width)
+        normed_two = lax.all_gather(normed_two, "ctx", axis=0, tiled=True)
+        w_gate_up = lax.all_gather(w_columns, "fsdp", axis=0, tiled=True)
+        projected = jnp.dot(normed_two, w_gate_up, preferred_element_type=f32)
+        gelu, slope = gelu_parts(projected[:, :padded])
+        up_part = projected[:, padded:]
+        hidden = (gelu * up_part).astype(bf16)
+        grad_hidden = contract_rows(cot_all, w_down)
+        grad_gate_up = jnp.concatenate(
+            [grad_hidden * up_part * slope, grad_hidden * gelu], axis=1
+        ).astype(bf16)
+        grad_normed_two = lax.psum_scatter(
+            contract_rows(grad_gate_up, w_gate_up).astype(bf16),
+            "ctx",
+            scatter_dimension=0,
+            tiled=True,
+        ).astype(f32)
+        grad_middle_norm, gain_two_term = norm_back(middle, norm_two[None], grad_normed_two)
+        gain_two_term = gain_two_term[0]
+        grad_middle = cot_rows.astype(f32) + grad_middle_norm
+        result_parts = jnp.dot(hidden, w_down, preferred_element_type=f32).astype(bf16)
+        down_part = lax.psum_scatter(
+            contract_tokens(hidden, cot_all).astype(bf16),
+            "fsdp",
+            scatter_dimension=1,
+            tiled=True,
+        ).reshape(fsdp_size, padded_piece, -1)
+    branch_two = lax.psum_scatter(result_parts, "ctx", scatter_dimension=0, tiled=True)
+    result = (middle + branch_two.astype(f32)).astype(bf16)
+
+    per_owner = ctx_size // fsdp_size
+    down_grad = lax.all_to_all(jnp.repeat(down_part, per_owner, axis=0), "ctx", 0, 0, tiled=True)
+    first = (ctx_place % per_owner) * fsdp_size
+    down_grad = lax.dynamic_slice_in_dim(down_grad, first, fsdp_size, 0)
+    down_grad = down_grad[:, :piece].reshape(fsdp_size * piece, -1).astype(f32)
+
+    gate_up_part = lax.psum_scatter(
+        contract_tokens(normed_two, grad_gate_up).astype(bf16),
         "fsdp",
         scatter_dimension=1,
         tiled=True,
-    ).astype(jnp.float32)
-    gate_up_part = lax.psum_scatter(
-        contract_tokens(normed_two, grad_gate_up).astype(jnp.bfloat16),
-        "fsdp",
-        scatter_dimension=1,
-        tiled=True,
     )
     gate_up_part = lax.all_to_all(
         gate_up_part.reshape(ctx_size, width // ctx_size, -1), "ctx", 0, 0, tiled=True
     )
-    core = lax.axis_index("fsdp") % 2
-    gate_up_part = gate_up_part.reshape((2, ctx_size // 2) + gate_up_part.shape[1:])
-    kept = lax.dynamic_index_in_dim(gate_up_part, core, 0, keepdims=False)
-    given = lax.dynamic_index_in_dim(gate_up_part, 1 - core, 0, keepdims=False)
-    taken = lax.ppermute(given, "fsdp", [(i, i ^ 1) for i in range(fsdp_size)])
-    halves = jnp.where(core == 0, jnp.stack([kept, taken], 2), jnp.stack([taken, kept], 2))
-    halves = halves.reshape(halves.shape[:2] + (-1,))[:, :, :part_width]
+    gate_up_part = gate_up_part.reshape(ctx_size, width // ctx_size, 2, padded_piece)[..., :piece]
     gate_up_grad = (
-        halves.transpose(1, 0, 2).reshape(width // ctx_size, -1).astype(jnp.float32)
-    )
-
-    grad_middle_norm, gain_two_term = norm_back_two(grad_normed_two)
-    grad_middle = cot_rows.astype(jnp.float32) + grad_middle_norm
+        gate_up_part.transpose(1, 2, 0, 3).reshape(width // ctx_size, -1).astype(f32)
+    )
+
     grad_branch = lax.all_gather(grad_middle.astype(jnp.bfloat16), "fsdp", axis=0, tiled=True)
     grad_mixed = collect(contract_rows(grad_branch, out_weight).astype(jnp.bfloat16))
     grad_mixed = grad_mixed.reshape(rows, head_count, HD)
@@ -915,7 +1120,6 @@
     grad_source_norm, gain_one_term = norm_back_one(grad_normed.astype(jnp.float32))
     input_grad = (grad_middle + grad_source_norm).astype(jnp.bfloat16)
 
-    per_owner = ctx_size // fsdp_size
 
     def in_blocks(term):
         tall, wide = term.shape

time: 1320 us -> 1050 us (0.80)
  waiting for transfers between devices: 764 us -> 567 us
  matrix products: 107 us -> 41.9 us
  blocking collectives: 12.9 us -> 33.7 us
  other arithmetic: 44.2 us -> 26.2 us
    pallas_call x1, Pallas kernels: 276 us -> 105 us  [front(): pl.pallas_call(functools.partial(front_kernel, lines), out_shape=(shape((...]
    pallas_call x0 -> x1, Pallas kernels: none -> 159 us  [middle_part(): pl.pallas_call(functools.partial(middle_kernel, lines), out_shape=(shape(...]
    reduce_scatter x3 -> x2, waiting for transfers between devices: 212 us -> 121 us  [the longest x1 115 us: per_device(): lax.psum_scatter(result_parts, 'ctx', scatter_dimension=0, tiled=True)]
    all_gather x1 -> x0, waiting for transfers between devices: 74.7 us -> none  [per_device(): normed_two = lax.all_gather(normed_two, 'ctx', axis=0, tiled=True)]
    unnamed x13 -> x9, waiting for transfers between devices: 175 us -> 125 us
    all_to_all x1, waiting for transfers between devices: 0.01 us -> 31.8 us  [per_device(): lax.all_to_all(jnp.repeat(down_part, per_owner, axis=0), 'ctx', 0, 0, til...]
    dot_general x4 -> x2, matrix products: 37 us -> 11.3 us  [contract_rows(): lax.dot_general(left, right, (((1,), (1,)), ((), ())), preferred_element_...]
    dot_general x2 -> x0, matrix products: 25 us -> none  [the longest x1 15.4 us: per_device(): jnp.dot(normed_two, w_gate_up, preferred_element_type=jnp.float32)]
  transfers between devices with their start and end apart: 16 -> 12, of which waited for: 11 -> 8; matrix products, arithmetic and copies ran while one was open for 11% -> 7% of each run, Pallas kernels for 0% -> 0%
where the time goes in v3:
time: 1050 us; the launch traced here: 1030 us
  waiting for transfers between devices  567 us (54%)
  Pallas kernels  264 us (25%)
  local copies, waits for them, and re-layouts  64.2 us (6%)
  matrix products  41.9 us (4%)
  blocking collectives  33.7 us (3%)
  other arithmetic  26.2 us (2%)
  starting transfers between devices  16.3 us (2%)
  between operations  14.7 us (1%)
    reduce_scatter x2, waiting for transfers between devices, summed(): block = lax.psum_scatter(blocks, 'ctx', scatter_dimension=0, tiled=True)[0]  195 us
    pallas_call x1, Pallas kernels, middle_part(): pl.pallas_call(functools.partial(middle_kernel, lines), out_shape=(shape(...  159 us
    unnamed x9, waiting for transfers between devices  125 us
    reduce_scatter x1, waiting for transfers between devices, per_device(): lax.psum_scatter(result_parts, 'ctx', scatter_dimension=0, tiled=True)  115 us
    pallas_call x1, Pallas kernels, front(): pl.pallas_call(functools.partial(front_kernel, lines), out_shape=(shape((...  105 us
    reduce_scatter x1, waiting for transfers between devices, per_device(): lax.psum_scatter(jnp.concatenate([grad_keys, grad_values], axis=1).astype...  59.2 us
    all_gather x1, waiting for transfers between devices, per_device(): lax.all_gather(grad_middle.astype(jnp.bfloat16), 'fsdp', axis=0, tiled=True)  34.2 us
    all_to_all x2, blocking collectives, collect(): lax.all_to_all(value, 'fsdp', split_axis=0, concat_axis=1, tiled=True)  33.7 us
  transfers between devices with their start and end apart: 12, of which 8 were waited for; matrix products, arithmetic and copies ran while one was open for 7% of the time, Pallas kernels for 0%

profile of v3, /device:TPU:4, one launch (start us, length us, event | category | flops | bytes accessed | tf_op | source)
XLA Modules:
  0.0 1027.9 jit_solution(6160031845271027280)
XLA Ops:
  7.2 1.3 fusion.40
  8.6 1.3 fusion.32
  9.9 1.3 convert_add_fusion
  11.2 3.5 constant_dynamic-slice_fusion.1
  23.1 1.4 constant_dynamic-slice_fusion.9
  27.4 105.0 %front.1 = (bf16[4,128,640]{2,1,0:T(8,128)(2,1)}, bf16[10,128,256]{2,1,0:T(8,128)(2,1)}, bf16[8,128,512]{2,1,0:T(8,128)(2,1)}, bf16[10,128,1024]{2,1,0:T(8,128)(...) custom-call(bf16[128,2560]{1,0:T(8,128)(2,1)} %bitcast.95, ...), custom_call_target="tpu_custom_call" | custom-call | tf_op jit(solution)/shard_map/front/pallas_call | solution.py:634
  132.3 158.8 %middle.1 = (f32[128,2560]{1,0:T(8,128)}, f32[1,2560]{1,0:T(1,128)}, bf16[4,256,2048]{2,1,0:T(8,128)(2,1)}, bf16[4,256,640]{2,1,0:T(8,128)(2,1)}, bf16[8,128,256...) custom-call(bf16[8,128,2560]{2,1,0:T(8,128)(2,1)} %get-tuple-element.25.cot_all, bf16[1024,2560]{1,0:T(8,128)(2,1)} %bitcast.97, ...), custom_call_target="tpu_custom_call" | custom-call | tf_op jit(solution)/shard_map/middle/pallas_call | solution.py:891
  291.1 2.2 convert_element_type.133
  293.4 34.2 %all-gather.3.cloned.1.call-done = bf16[512,2560]{1,0:T(8,128)(2,1)} async-done(((bf16[128,2560]{1,0:T(8,128)(2,1)}), bf16[512,2560]{1,0:T(8,128)(2,1)}) %all-gather.3.cloned.1.call-update) | async-done | bytes 2621456 | tf_op jit(solution)/shard_map/all_gather | solution.py:1082
  327.6 5.8 convolution_convert_fusion.3
  333.4 1.6 copy.43
  335.0 12.7 %all_to_all.39 = bf16[4,128,640]{1,2,0:T(8,128)(2,1)S(1)} all-to-all(bf16[4,128,640]{1,2,0:T(8,128)(2,1)S(1)} %copy.43), channel_id=1, replica_groups=mesh['ctx'=8,'fsdp'=4] {'fsdp'}, dimensions={0} | all-to-all | bytes 1310720 | tf_op jit(solution)/shard_map/all_to_all | solution.py:1019
  353.7 2.6 fusion.22
  357.3 59.2 %reduce-scatter.11.cloned.1.call-done = bf16[128,512]{1,0:T(8,128)(2,1)} async-done(((bf16[1024,512]{1,0:T(8,128)(2,1)}), bf16[128,512]{1,0:T(8,128)(2,1)}) %reduce-scatter.11.cloned.1.call-update) | async-done | bytes 131088 | tf_op jit(solution)/shard_map/reduce_scatter | solution.py:1098
  420.6 16.7 %convolution_convert_fusion = bf16[2560,2048]{1,0:T(8,128)(2,1)} fusion(bf16[1024,2560]{1,0:T(8,128)(2,1)} %bitcast.114, bf16[1024,2048]{1,0:T(8,128)(2,1)} %bitcast.115), kind=kOutput, calls=%fused_computation | convolution fusion | flops 10742661120 | bytes 19922944 | tf_op jit(solution)/shard_map/dot_general | solution.py:53
  437.3 1.7 copy-done.14
  439.1 3.6 convolution_convert_fusion.1
  442.7 5.6 reshape.163
  448.3 2.1 copy.55
  451.8 1.8 broadcast_in_dim.52
  453.6 5.3 all-to-all-start.3
  459.4 4.9 convolution_convert_fusion.2
  465.4 3.0 reshape.158
  468.4 2.6 copy.53
  470.9 2.3 reshape.160
  474.4 2.2 pad_maximum_fusion
  476.7 2.7 copy-done.4
  479.4 5.5 fusion.6
  484.9 31.8 %all-to-all-done.3 = bf16[8,256,640]{2,1,0:T(8,128)(2,1)} async-done(((bf16[8,256,640]{2,1,0:T(8,128)(2,1)}), bf16[8,256,640]{2,1,0:T(8,128)(2,1)}, u32[]{:S(2)}, u32[]{:S(2)}) %all-to-all-start.3) | async-done | bytes 2621472 | tf_op jit(solution)/shard_map/all_to_all | solution.py:1063
  516.6 21.0 %all_to_all.40 = bf16[4,128,640]{2,1,0:T(8,128)(2,1)S(1)} all-to-all(bf16[4,128,640]{2,1,0:T(8,128)(2,1)} %bitcast.107), channel_id=1, replica_groups=mesh['ctx'=8,'fsdp'=4] {'fsdp'}, dimensions={0} | all-to-all | bytes 1310720 | tf_op jit(solution)/shard_map/all_to_all | solution.py:1019
  537.7 6.2 reduce-scatter.17.cloned.1.call-done
  543.9 6.2 all-to-all-start.2
  550.3 1.5 constant_dynamic-slice_fusion
  551.8 1.7 bitcast_convert_fusion
  553.5 112.6 %reduce-scatter.15.cloned.1.call-done = bf16[1,320,640]{2,1,0:T(8,128)(2,1)} async-done(((bf16[8,320,640]{2,1,0:T(8,128)(2,1)}), bf16[1,320,640]{2,1,0:T(8,128)(2,1)}) %reduce-scatter.15.cloned.1.call-update) | async-done | bytes 409616 | tf_op jit(solution)/shard_map/reduce_scatter | solution.py:1131
  666.1 1.9 collective-permute-start.1
  668.0 115.2 %reduce-scatter.9.cloned.1.call-done = bf16[128,2560]{1,0:T(8,128)(2,1)} async-done(((bf16[1024,2560]{1,0:T(8,128)(2,1)}), bf16[128,2560]{1,0:T(8,128)(2,1)}) %reduce-scatter.9.cloned.1.call-update) | async-done | bytes 655376 | tf_op jit(solution)/shard_map/reduce_scatter | solution.py:1059
  783.2 2.0 fusion.18
  787.0 1.6 copy.64
  788.6 82.9 %reduce-scatter.13.cloned.1.call-done = bf16[1,320,768]{2,1,0:T(8,128)(2,1)} async-done(((bf16[8,320,768]{2,1,0:T(8,128)(2,1)}), bf16[1,320,768]{2,1,0:T(8,128)(2,1)}) %reduce-scatter.13.cloned.1.call-update) | async-done | bytes 491536 | tf_op jit(solution)/shard_map/reduce_scatter | solution.py:1131
  871.5 2.1 collective-permute-start
  873.6 1.3 fusion.20
  874.9 124.4 %reduce-scatter.19.cloned.1.call-done = f32[80,2]{1,0:T(8,128)} async-done(((f32[2560,2]{1,0:T(8,128)}), f32[80,2]{1,0:T(8,128)}) %reduce-scatter.19.cloned.1.call-update) | async-done | bytes 656
  1001.5 1.9 slice.113
  1003.4 1.6 slice.114
  1005.0 3.5 reshape.168
  1008.5 5.4 convert_bitcast_fusion
  1013.9 6.9 reshape.171
  (102 shorter events, 30.8 us)
Async XLA Ops:
  7.2 320.5 %all-gather.3.cloned.1.call-start = ((), (), s32[]{:S(2)}) async-start(), calls=%async_computation.11 | async-start | bytes 3276800 | tf_op jit(solution)/shard_map/all_gather | solution.py:1082
  11.2 5.3 copy-start.12
  11.2 5.9 copy-start.11
  293.4 123.0 %reduce-scatter.11.cloned.1.call-start = ((), (), s32[]{:S(2)}) async-start(), calls=%async_computation.12 | async-start | bytes 1179648 | tf_op jit(solution)/shard_map/reduce_scatter | solution.py:1098
  333.4 14.2 %copy-start = (bf16[10,128,1024]{2,1,0:T(8,128)(2,1)S(1)}, bf16[10,128,1024]{2,1,0:T(8,128)(2,1)}, u32[]{:S(2)}) copy-start(bf16[10,128,1024]{2,1,0:T(8,128)(2,1)} %get-tuple-element.30) | copy-start | bytes 7864324
  347.6 1.2 copy-start.9
  349.9 1.1 copy-start.17
  350.6 1.5 copy-start.5
  352.1 1.6 copy-start.10
  353.2 3.4 copy-start.7
  353.2 3.4 copy-start.8
  353.2 106.2 %all-gather.5.cloned.1.call-start = ((), (), s32[]{:S(2)}) async-start(), calls=%async_computation.13 | async-start | bytes 3932160 | tf_op jit(solution)/shard_map/all_gather | solution.py:1118
  420.5 123.4 %reduce-scatter.17.cloned.1.call-start = ((), (), s32[]{:S(2)}) async-start(), calls=%async_computation.16 | async-start | bytes 13107200 | tf_op jit(solution)/shard_map/reduce_scatter | solution.py:1068
  437.3 1.7 copy-start.14
  437.3 1.9 copy-start.16
  437.3 228.8 %reduce-scatter.15.cloned.1.call-start = ((), (), s32[]{:S(2)}) async-start(), calls=%async_computation.15 | async-start | bytes 3686400 | tf_op jit(solution)/shard_map/reduce_scatter | solution.py:1131
  450.5 332.7 %reduce-scatter.9.cloned.1.call-start = ((), (), s32[]{:S(2)}) async-start(), calls=%async_computation.10 | async-start | bytes 5898240 | tf_op jit(solution)/shard_map/reduce_scatter | solution.py:1059
  450.5 1.3 copy-start.6
  453.6 5.7 copy-start.15
  453.6 63.0 %all-to-all-start.3 = ((bf16[8,256,640]{2,1,0:T(8,128)(2,1)}), bf16[8,256,640]{2,1,0:T(8,128)(2,1)}, u32[]{:S(2)}, u32[]{:S(2)}) async-start(bf16[8,256,640]{2,1,0:T(8,128)(2,1)} %bitcast.38), calls=%async_computation.8 | async-start | bytes 5242880 | tf_op jit(solution)/shard_map/all_to_all | solution.py:1063
  458.9 412.6 %reduce-scatter.13.cloned.1.call-start = ((), (), s32[]{:S(2)}) async-start(), calls=%async_computation.14 | async-start | bytes 4423680 | tf_op jit(solution)/shard_map/reduce_scatter | solution.py:1131
  476.7 2.7 copy-start.4
  543.9 6.2 copy-start.1
  543.9 461.1 %all-to-all-start.2 = ((bf16[8,320,512]{2,1,0:T(8,128)(2,1)}), bf16[8,320,512]{2,1,0:T(8,128)(2,1)}, u32[]{:S(2)}, u32[]{:S(2)}) async-start(bf16[8,320,512]{2,1,0:T(8,128)(2,1)} %bitcast.102), calls=%async_computation.7 | async-start | bytes 5242880 | tf_op jit(solution)/shard_map/all_to_all | solution.py:1074
  550.1 449.3 %reduce-scatter.19.cloned.1.call-start = ((), (), s32[]{:S(2)}) async-start(), calls=%async_computation.17 | async-start | bytes 1351680
  550.3 232.9 %copy-start.2 = (f32[128,2560]{1,0:T(8,128)S(1)}, f32[128,2560]{1,0:T(8,128)}, u32[]{:S(2)}) copy-start(f32[128,2560]{1,0:T(8,128)} %get-tuple-element.24.middle) | copy-start | bytes 3932164
  666.1 119.2 %collective-permute-start.1 = (bf16[320,640]{1,0:T(8,128)(2,1)}, bf16[320,640]{1,0:T(8,128)(2,1)S(1)}, u32[]{:S(2)}, u32[]{:S(2)}) collective-permute-start(bf16[320,640]{1,0:T(8,128)(2,1)} %bitcast.119), channel_id=1, source_target_pairs={{0,0},{1,8},{2,16},{3,24},{4,1},{5,9},{6,17},{7,25},{8,2},{9,10},{... | collective-permute-start | bytes 1228808 | tf_op jit(solution)/shard_map/ppermute | solution.py:1138
  786.3 0.7 copy-start.13
  786.4 87.2 %copy-start.3 = (f32[128,2560]{1,0:T(8,128)S(1)}, f32[128,2560]{1,0:T(8,128)}, u32[]{:S(2)}) copy-start(f32[128,2560]{1,0:T(8,128)} %get-tuple-element.29) | copy-start | bytes 3932164
  871.5 129.9 %collective-permute-start = (bf16[320,768]{1,0:T(8,128)(2,1)}, bf16[320,768]{1,0:T(8,128)(2,1)}, u32[]{:S(2)}, u32[]{:S(2)}) collective-permute-start(bf16[320,768]{1,0:T(8,128)(2,1)} %bitcast.118), channel_id=1, source_target_pairs={{0,0},{1,8},{2,16},{3,24},{4,1},{5,9},{6,17},{7,25},{8,2},{9,10},{... | collective-permute-start | bytes 1474568 | tf_op jit(solution)/shard_map/ppermute | solution.py:1138
Sparse Core Ops, SparseCore 0:
  293.5 34.0 all-gather.2
  353.3 63.0 reduce-scatter.10
  420.6 28.1 all-gather.4
  451.5 92.3 reduce-scatter.16
  547.7 118.2 reduce-scatter.14
  669.5 113.6 reduce-scatter.8
  787.4 84.0 reduce-scatter.12
  873.9 125.4 reduce-scatter.18

commit v4 on v3

--- a/solution.py
+++ b/solution.py
@@ -91,7 +91,7 @@
         self.has_right = self.line < lines - 1
         self.has_left = self.line > 0
 
-    def barrier(self, ctx=True, fsdp=True):
+    def barrier(self, ctx=True, fsdp=True, also=()):
         sem = pltpu.get_barrier_semaphore()
 
         def greet(device):
@@ -109,6 +109,9 @@
             count = (
                 count + 1 + self.has_right.astype(jnp.int32) + self.has_left.astype(jnp.int32)
             )
+        for needed, device in also:
+            pl.when(needed)(lambda device=device: greet(device))
+            count = count + needed.astype(jnp.int32)
         pl.semaphore_wait(sem, count)
 
 
@@ -239,11 +242,11 @@
     def add(self, at, other):
         self.parts[at] = (self.parts[at].astype(f32) + other.astype(f32)).astype(bf16)
 
-    def start(self):
-        for turn in range(min(2, self.p.lines)):
+    def start(self, ahead=2):
+        for turn in range(min(ahead, self.p.lines)):
             self.across(turn).start()
 
-    def turn(self, turn, ahead=2):
+    def near(self, turn, ahead=2):
         p = self.p
         t = self.order(turn)
         at = 2 * t + p.lane
@@ -251,28 +254,32 @@
         if ahead and turn + ahead < p.lines:
             self.across(turn + ahead).start()
         self.add(at, self.side[t])
-
-        @pl.when(t > p.line)
+        pl.when((t > p.line) & (p.line == 0))(lambda: self.rightward(t).start())
+        pl.when((t < p.line) & (p.line == p.lines - 1))(lambda: self.leftward(t).start())
+
+    def far(self, turn):
+        p = self.p
+        t = self.order(turn)
+        at = 2 * t + p.lane
+
+        @pl.when((t > p.line) & p.has_left)
         def _():
-            @pl.when(p.has_left)
-            def _():
-                self.rightward(t).wait_recv()
-                self.add(at, self.chain[0, p.lines - 1 - t])
-
+            self.rightward(t).wait_recv()
+            self.add(at, self.chain[0, p.lines - 1 - t])
             self.rightward(t).start()
 
-        @pl.when(t < p.line)
+        @pl.when((t < p.line) & p.has_right)
         def _():
-            @pl.when(p.has_right)
-            def _():
-                self.leftward(t).wait_recv()
-                self.add(at, self.chain[1, t])
-
+            self.leftward(t).wait_recv()
+            self.add(at, self.chain[1, t])
             self.leftward(t).start()
 
-    def turns(self):
+    def turns(self, ahead=2):
         for turn in range(self.p.lines):
-            self.turn(turn)
+            self.near(turn, ahead)
+            if turn > 0:
+                self.far(turn - 1)
+        self.far(self.p.lines - 1)
 
     def total(self):
         p = self.p
@@ -359,6 +366,9 @@
     def block(self, g):
         return self.whole.at[:, pl.ds(pl.multiple_of(g * self.n, 128), self.n)]
 
+    def send(self, d):
+        self.copy(d).start()
+
     def copy(self, d):
         g = (self.p.f + d) % 4
         return remote(
@@ -387,6 +397,14 @@
     def finish(self):
         for d in (1, 2, 3):
             self.copy(d).wait_send()
+
+
+class GroupReturn(GroupTrade):
+    def __init__(self, place, whole, slots, sems):
+        super().__init__(place, whole, slots, sems, 0)
+
+    def block(self, g):
+        return self.whole.at[g]
 
 
 def rotated(v, cosine, sine):
@@ -399,27 +417,30 @@
 class GroupGather:
     sems = 6
 
-    def __init__(self, place, own, whole, sems, own_sem, pieces):
+    def __init__(self, place, own, whole, sems, own_sem, pieces, cuts=None):
         self.p, self.own, self.whole, self.s, self.own_sem = place, own, whole, sems, own_sem
-        self.pieces, self.n = pieces, own.shape[0] // pieces
-
-    def part(self, ref, i):
-        return ref.at[pl.ds(i * self.n, self.n)]
+        self.pieces, self.n, self.cuts = pieces, own.shape[0] // pieces, cuts
+
+    def span(self, i):
+        return (slice(None), self.cuts[i]) if self.cuts else (pl.ds(i * self.n, self.n),)
+
+    def part(self, i):
+        return self.own.at[self.span(i)]
 
     def slot(self, g, i):
-        return self.whole.at[g, pl.ds(i * self.n, self.n)]
+        return self.whole.at[(g,) + self.span(i)]
 
     def local(self):
         return pltpu.make_async_copy(self.own, self.whole.at[self.p.f], self.own_sem)
 
     def to_twin(self, i):
         return remote(
-            self.part(self.own, i), self.slot(self.p.f, i), self.s.at[0, i], self.s.at[3, i], self.p.twin
+            self.part(i), self.slot(self.p.f, i), self.s.at[0, i], self.s.at[3, i], self.p.twin
         )
 
     def to_cross(self, i):
         return remote(
-            self.part(self.own, i), self.slot(self.p.f, i), self.s.at[1, i], self.s.at[4, i], self.p.cross
+            self.part(i), self.slot(self.p.f, i), self.s.at[1, i], self.s.at[4, i], self.p.cross
         )
 
     def forward(self, i):
@@ -429,19 +450,29 @@
     def give(self, i):
         self.to_cross(i).start()
         self.to_twin(i).start()
+
+    def near(self, i):
+        twin = self.slot(self.p.twin_f, i)
+        remote(twin, twin, self.s.at[0, i], self.s.at[3, i], self.p.twin).wait_recv()
 
     def pass_on(self, i):
         slot = self.slot(self.p.cross_f, i)
         remote(slot, slot, self.s.at[1, i], self.s.at[4, i], self.p.cross).wait_recv()
         self.forward(i).start()
 
-    def finish(self, i):
-        twin, diag = self.slot(self.p.twin_f, i), self.slot(self.p.diag_f, i)
-        remote(twin, twin, self.s.at[0, i], self.s.at[3, i], self.p.twin).wait_recv()
+    def last(self, i):
+        diag = self.slot(self.p.diag_f, i)
         remote(diag, diag, self.s.at[2, i], self.s.at[5, i], self.p.twin).wait_recv()
+
+    def sent(self, i):
         self.to_twin(i).wait_send()
         self.to_cross(i).wait_send()
         self.forward(i).wait_send()
+
+    def finish(self, i):
+        self.near(i)
+        self.last(i)
+        self.sent(i)
 
 
 def tiles_of(first, count, tile):
@@ -838,7 +869,9 @@
         feed_forward(line_sum.order(turn))
         line_sum.across(turn).start()
         if turn > 0:
-            line_sum.turn(turn - 1, 0)
+            line_sum.near(turn - 1, 0)
+        if turn > 1:
+            line_sum.far(turn - 2)
     normed_local.wait()
 
     for i in range(4):
@@ -851,9 +884,12 @@
         if i < lines:
             result_part(i)
         down_group(i).pass_on(i, every)
+        if i == 1:
+            line_sum.far(lines - 2)
     for line in range(4, lines):
         result_part(line)
-    line_sum.turn(lines - 1, 0)
+    line_sum.near(lines - 1, 0)
+    line_sum.far(lines - 1)
     grad = line_sum.total()
     middle_local.wait()
     grad_values, gain = norm_back(grad_middle_out[...], gain_two[...], grad)
@@ -924,6 +960,503 @@
     )(*operands)
 
 
+def back_kernel(
+    lines,
+    with_result,
+    grad_middle,
+    probs,
+    keyval,
+    queries,
+    tokens,
+    gain_one,
+    cosine,
+    sine,
+    w_out,
+    w_query,
+    w_keyval,
+    *rest,
+):
+    if with_result:
+        middle, result_in, result_out, *rest = rest
+    (
+        input_grad_out,
+        gain_out,
+        branch_out,
+        linear_out,
+        branch_all,
+        linear_all,
+        branch,
+        linear,
+        trade_parts,
+        trade_slots,
+        grad_mixed,
+        kv_total,
+        kv_parts,
+        kv_side,
+        kv_chain,
+        branch_sems,
+        linear_sems,
+        trade_sems,
+        kv_sems,
+        own_sems,
+        *rest,
+    ) = rest
+    p = Place(lines)
+    rows, width = grad_middle.shape
+    heads = queries.shape[0]
+    length = probs.shape[2]
+    shard = w_out.shape[0]
+    kv_width = 2 * HD
+    p.barrier()
+    if with_result:
+        result_parts, result_side, result_chain, result_sems = rest
+        result_sum = LineSum(p, result_parts, result_side, result_chain, result_sems)
+        result_copy = pltpu.make_async_copy(result_in, result_parts, own_sems.at[2])
+        result_copy.start()
+
+    branch[...] = grad_middle[...].astype(bf16)
+    group = GroupGather(p, branch, branch_all, branch_sems, own_sems.at[0], 1)
+    group.give(0)
+    group.local().start()
+    if with_result:
+        result_copy.wait()
+        result_sum.start(1)
+    back_trade = GroupReturn(p, trade_parts.at[0], trade_slots.at[0], trade_sems.at[0])
+
+    def mixed_back(g):
+        trade_parts[0, g] = contract_rows(branch_all[g], w_out[...]).astype(bf16)
+
+    group.local().wait()
+    mixed_back(p.f)
+    back_trade.own().start()
+    group.near(0)
+    mixed_back(p.twin_f)
+    group.pass_on(0)
+    mixed_back(p.cross_f)
+    back_trade.send(2)
+    group.last(0)
+    mixed_back(p.diag_f)
+    back_trade.send(1)
+    back_trade.send(3)
+    branch_copy = pltpu.make_async_copy(branch_all, branch_out, own_sems.at[3])
+    branch_copy.start()
+    if with_result:
+        result_sum.near(0, 1)
+    back_trade.wait()
+    for g in range(4):
+        grad_mixed[:, g * shard : (g + 1) * shard] = trade_slots[0, g]
+
+    kv_total[...] = jnp.zeros_like(kv_total)
+    kv_at, q_at = pl.ds(0, kv_width), pl.ds(kv_width, heads * HD)
+
+    batch = 2 if length <= 2048 else 1
+
+    def some_heads(i, carry):
+        keys = keyval[:, :, :HD].reshape(length, HD)
+        values = keyval[:, :, HD:].reshape(length, HD)
+        at = [pl.multiple_of((i * batch + h) * HD, 128) for h in range(batch)]
+        outer = jnp.concatenate([grad_mixed[:, pl.ds(a, HD)] for a in at], axis=0)
+        weights = probs[pl.ds(batch * i, batch)].reshape(batch * rows, length)
+        wide = weights.astype(f32)
+        grad_weights = contract_rows(outer, values)
+        delta = jnp.sum(wide * grad_weights, axis=-1, keepdims=True)
+        grad_scores = (wide * (grad_weights - delta)).astype(bf16)
+        product = jnp.dot(grad_scores, keys, preferred_element_type=f32) * HD**-0.5
+        for h in range(batch):
+            turned = rotated(product[h * rows : (h + 1) * rows], cosine[...], -sine[...])
+            linear[:, pl.ds(kv_width + at[h], HD)] = turned.astype(bf16)
+        two = queries[pl.ds(batch * i, batch)].reshape(batch * rows, HD)
+        kv_total[:, :HD] += contract_tokens(grad_scores, two)
+        kv_total[:, HD:] += contract_tokens(weights, outer)
+        return carry
+
+    lax.fori_loop(0, heads // batch, some_heads, 0)
+    linear_group = GroupGather(
+        p, linear, linear_all, linear_sems, own_sems.at[1], 2, (q_at, kv_at)
+    )
+    linear_group.give(0)
+    if with_result:
+        result_sum.far(0)
+        result_sum.near(1, 0)
+    kv_parts[...] = kv_total[...].astype(bf16).reshape(kv_parts.shape)
+    kv_sum = LineSum(p, kv_parts, kv_side, kv_chain, kv_sems)
+    kv_sum.start(lines)
+    kv_sum.turns(0)
+    own = kv_sum.total()
+    linear[:, :HD] = rotated(own[:, :HD], cosine[...], -sine[...]).astype(bf16)
+    linear[:, pl.ds(HD, HD)] = own[:, HD:].astype(bf16)
+    linear_group.give(1)
+    linear_group.local().start()
+    if with_result:
+        for turn in range(2, lines):
+            result_sum.across(turn).start()
+        result_sum.far(1)
+    linear_group.pass_on(0)
+    linear_group.pass_on(1)
+    linear_group.local().wait()
+    for i in range(2):
+        linear_group.near(i)
+        linear_group.last(i)
+
+    linear_copy = pltpu.make_async_copy(linear_all, linear_out, own_sems.at[4])
+    linear_copy.start()
+
+    last_trade = GroupReturn(p, trade_parts.at[1], trade_slots.at[1], trade_sems.at[1])
+
+    def normed_back(g):
+        product = contract_rows(linear_all[g, :, kv_at], w_keyval[...])
+        product += contract_rows(linear_all[g, :, q_at], w_query[...])
+        trade_parts[1, g] = product.astype(bf16)
+
+    normed_back(p.cross_f)
+    last_trade.send(2)
+    normed_back(p.diag_f)
+    normed_back(p.twin_f)
+    last_trade.send(1)
+    last_trade.send(3)
+    normed_back(p.f)
+    last_trade.own().start()
+    if with_result:
+        for turn in range(2, lines):
+            result_sum.near(turn, 0)
+            result_sum.far(turn)
+    last_trade.wait()
+    for g in range(4):
+        grad_mixed[:, g * shard : (g + 1) * shard] = trade_slots[1, g]
+    source = tokens[...].astype(f32)
+    grad_values, gain = norm_back(source, gain_one[...], grad_mixed[...].astype(f32))
+    input_grad_out[...] = (grad_middle[...] + grad_values).astype(bf16)
+    gain_out[...] = gain
+    if with_result:
+        result_out[...] = (middle[...] + result_sum.total()).astype(bf16)
+        result_sum.finish()
+    back_trade.finish()
+    last_trade.finish()
+    group.sent(0)
+    linear_group.sent(0)
+    linear_group.sent(1)
+    kv_sum.finish()
+    branch_copy.wait()
+    linear_copy.wait()
+
+
+def back(lines, operands, result_operands):
+    rows, width = operands[0].shape
+    heads = operands[3].shape[0]
+    places = 2 * lines
+    length = places * rows
+    shard = width // 4
+    linear_width = width + 2 * HD
+    in_vmem = pl.BlockSpec(memory_space=VMEM)
+    anywhere = pl.BlockSpec(memory_space=pl.ANY)
+    shape = jax.ShapeDtypeStruct
+    with_result = bool(result_operands)
+    result_scratch = [
+        VMEM((places, rows, width), bf16),
+        VMEM((lines, rows, width), bf16),
+        VMEM((2, lines - 1, rows, width), bf16),
+        DMA((LineSum.sems, lines)),
+    ]
+    return pl.pallas_call(
+        functools.partial(back_kernel, lines, with_result),
+        out_shape=((shape((rows, width), bf16),) if with_result else ())
+        + (
+            shape((rows, width), bf16),
+            shape((1, width), f32),
+            shape((4, rows, width), bf16),
+            shape((4, rows, linear_width), bf16),
+        ),
+        in_specs=[in_vmem] * 11 + ([in_vmem, anywhere] if with_result else []),
+        out_specs=[in_vmem] * (3 if with_result else 2) + [anywhere] * 2,
+        scratch_shapes=[
+            VMEM((4, rows, width), bf16),
+            VMEM((4, rows, linear_width), bf16),
+            VMEM((rows, width), bf16),
+            VMEM((rows, linear_width), bf16),
+            VMEM((2, 4, rows, shard), bf16),
+            VMEM((2, 4, rows, shard), bf16),
+            VMEM((rows, width), bf16),
+            VMEM((length, 2 * HD), f32),
+            VMEM((places, rows, 2 * HD), bf16),
+            VMEM((lines, rows, 2 * HD), bf16),
+            VMEM((2, lines - 1, rows, 2 * HD), bf16),
+            DMA((GroupGather.sems, 1)),
+            DMA((GroupGather.sems, 2)),
+            DMA((2, GroupTrade.sems, 4)),
+            DMA((LineSum.sems, lines)),
+            DMA((5,)),
+        ]
+        + (result_scratch if with_result else []),
+        compiler_params=pltpu.CompilerParams(
+            collective_id=2, has_side_effects=True, vmem_limit_bytes=vmem_bytes
+        ),
+        name="back",
+    )(*operands, *result_operands)
+
+
+def grads_kernel(lines, with_columns, normed, mixed, branch_all, linear_all, down_in, *rest):
+    if with_columns:
+        normed_two, hidden_grads, *rest = rest
+    projection_out, out_out, down_out, *rest = rest
+    if with_columns:
+        columns_out, *rest = rest
+    (
+        parts,
+        side,
+        chain,
+        out_parts,
+        out_side,
+        out_chain,
+        sums,
+        projection_sems,
+        out_sems,
+        down_sems,
+        place_sems,
+        *rest,
+    ) = rest
+    if with_columns:
+        chunk_parts, near, stage, far, chunks, group_sems, trade_sems, *rest = rest
+    p = Place(lines)
+    places = 2 * lines
+    shard = normed.shape[2]
+    tokens = 4 * normed.shape[1]
+    per_owner = places // 4
+    tall = shard // per_owner
+    kv_share = 2 * HD // 4
+
+    to_ctx, to_f = per_owner * p.f + p.c // 4, p.c % 4
+    from_ctx, from_f = 4 * (p.c % per_owner) + p.f, p.c // per_owner
+    moves = (to_ctx != p.c) | (to_f != p.f)
+    others = [
+        (jnp.full((), True), {"ctx": (p.c + d) % places}) for d in range(1, places)
+    ] + [
+        (moves, {"ctx": to_ctx, "fsdp": to_f}),
+        (moves, {"ctx": from_ctx, "fsdp": from_f}),
+    ]
+    p.barrier(ctx=False, also=others)
+
+    def down_copy(q):
+        dest = per_owner * q + p.c // 4
+        return remote(
+            down_in.at[q], down_out.at[p.c % 4], down_sems.at[0, q], down_sems.at[1, p.c % 4], {"ctx": dest}
+        )
+
+    def down_own(q):
+        return pltpu.make_async_copy(down_in.at[q], down_out.at[p.c % 4], down_sems.at[2, 0])
+
+    def down_arrival(i):
+        slot = down_out.at[i]
+        return remote(slot, slot, down_sems.at[0, 0], down_sems.at[1, i], p.beside)
+
+    for q in range(4):
+        stays = per_owner * q + p.c // 4 == p.c
+        pl.when(~stays)(lambda q=q: down_copy(q).start())
+        pl.when(stays)(lambda q=q: down_own(q).start())
+
+    projection_sum = LineSum(p, parts, side, chain, projection_sems)
+    out_sum = LineSum(p, out_parts, out_side, out_chain, out_sems)
+
+    def out_blocks(g, carry):
+        left = mixed[...].reshape(tokens, shard)
+        right = branch_all[:, :, pl.ds(pl.multiple_of(g * shard, 128), shard)]
+        product = contract_tokens(left, right.reshape(tokens, shard))
+        for r in range(per_owner):
+            out_parts[4 * r + g] = product[r * tall : (r + 1) * tall].astype(bf16)
+        return carry
+
+    def projection_blocks(g, carry):
+        left = normed[...].reshape(tokens, shard)
+        right = linear_all[:, :, pl.ds(pl.multiple_of(2 * HD + g * shard, 128), shard)]
+        product = contract_tokens(left, right.reshape(tokens, shard))
+        right = linear_all[:, :, pl.ds(pl.multiple_of(g * kv_share, 128), kv_share)]
+        kv_product = contract_tokens(left, right.reshape(tokens, kv_share))
+        for r in range(per_owner):
+            rows = slice(r * tall, (r + 1) * tall)
+            parts[4 * r + g, :, :shard] = product[rows].astype(bf16)
+            parts[4 * r + g, :, shard:] = kv_product[rows].astype(bf16)
+        return carry
+
+    lax.fori_loop(0, 4, out_blocks, 0)
+    out_sum.start(2)
+    lax.fori_loop(0, 4, projection_blocks, 0)
+
+    if with_columns:
+        block = columns_out.shape[2]
+        every = slice(None)
+
+        def chunk_of(k):
+            return (p.line + k) % lines
+
+        def group(k):
+            return GroupSum(p, chunk_parts, near.at[k], stage.at[k % 2], far.at[k], group_sems)
+
+        def compute(k):
+            cols = pl.ds(pl.multiple_of(chunk_of(k) * chunk_parts.shape[1], 128), chunk_parts.shape[1])
+
+            def one(g, carry):
+                left = normed_two[:, :, cols].reshape(-1, chunk_parts.shape[1])
+                right = hidden_grads[:, :, pl.ds(pl.multiple_of(g * block, 128), block)]
+                chunk_parts[g] = contract_tokens(left, right.reshape(-1, block)).astype(bf16)
+                return carry
+
+            lax.fori_loop(0, 4, one, 0)
+            chunks[k] = chunk_parts[p.f]
+            group(k).give(k, every)
+
+        def halves(k):
+            half = chunk_parts.shape[1] // 2
+            for lane in range(2):
+                yield lane, 2 * chunk_of(k) + lane, chunks.at[k, pl.ds(lane * half, half)]
+
+        def place_copy(k, lane, dest, src):
+            return remote(
+                src,
+                columns_out.at[p.c],
+                trade_sems.at[0, 2 * k + lane],
+                trade_sems.at[1, p.c],
+                {"ctx": dest},
+            )
+
+        def place_own(src):
+            return pltpu.make_async_copy(src, columns_out.at[p.c], trade_sems.at[2, 0])
+
+        def arrival(i):
+            slot = columns_out.at[i]
+            return remote(slot, slot, trade_sems.at[0, 0], trade_sems.at[1, i], p.beside)
+
+        def complete(k):
+            chunks[k] = group(k).take(k, every, chunks[k]).astype(bf16)
+            for lane, dest, src in halves(k):
+                pl.when(dest != p.c)(
+                    lambda k=k, lane=lane, dest=dest, src=src: place_copy(k, lane, dest, src).start()
+                )
+                pl.when(dest == p.c)(lambda src=src: place_own(src).start())
+
+        for k in range(lines):
+            if k >= 1:
+                group(k - 1).given(k - 1, every)
+            if k >= 2:
+                complete(k - 2)
+                group(k - 2).passed(k - 2, every)
+            compute(k)
+            group(k).pass_on(k, every)
+            out_sum.near(k, 2)
+            if k > 0:
+                out_sum.far(k - 1)
+        out_sum.far(lines - 1)
+    else:
+        out_sum.turns(2)
+
+    def to_place(i, src, dst):
+        return remote(
+            src, dst, place_sems.at[0, i], place_sems.at[1, i], {"ctx": to_ctx, "fsdp": to_f}
+        )
+
+    def hand_over(i, line_sum, at, dst):
+        src = sums.at[pl.ds(0, tall), at]
+        sums[:, at] = line_sum.total().astype(bf16)
+        pl.when(moves)(lambda: to_place(i, src, dst).start())
+        pl.when(~moves)(lambda: pltpu.make_async_copy(src, dst, place_sems.at[2, i]).start())
+
+    def handed(i, at, dst):
+        src = sums.at[pl.ds(0, tall), at]
+
+        @pl.when(moves)
+        def _():
+            to_place(i, src, dst).wait_send()
+            to_place(i, src, dst).wait_recv()
+
+        pl.when(~moves)(lambda: pltpu.make_async_copy(src, dst, place_sems.at[2, i]).wait())
+
+    projection_sum.start(2)
+    wide = shard + kv_share
+    hand_over(0, out_sum, pl.ds(wide, shard), out_out)
+    if with_columns:
+        for k in (lines - 2, lines - 1):
+            complete(k)
+            group(k).passed(k, every)
+        group(lines - 1).given(lines - 1, every)
+    projection_sum.turns(2)
+    hand_over(1, projection_sum, pl.ds(0, wide), projection_out)
+
+    handed(0, pl.ds(wide, shard), out_out)
+    for q in range(4):
+        stays = per_owner * q + p.c // 4 == p.c
+        pl.when(~stays)(lambda q=q: down_copy(q).wait_send())
+        pl.when(stays)(lambda q=q: down_own(q).wait())
+    for i in range(4):
+        source = 4 * (p.c % per_owner) + i
+        pl.when(source != p.c)(lambda i=i: down_arrival(i).wait_recv())
+    if with_columns:
+        for k in range(lines):
+            for lane, dest, src in halves(k):
+                pl.when(dest != p.c)(
+                    lambda k=k, lane=lane, dest=dest, src=src: place_copy(k, lane, dest, src).wait_send()
+                )
+                pl.when(dest == p.c)(lambda src=src: place_own(src).wait())
+        for i in range(places):
+            pl.when(p.c != i)(lambda i=i: arrival(i).wait_recv())
+    out_sum.finish()
+    projection_sum.finish()
+    handed(1, pl.ds(0, wide), projection_out)
+
+
+def weight_grads(lines, operands, column_operands):
+    rows, shard = operands[0].shape[1:]
+    width = 4 * shard
+    places = 2 * lines
+    tall = 4 * shard // places
+    wide = shard + 2 * HD // 4
+    quarter = operands[4].shape[1]
+    in_vmem = pl.BlockSpec(memory_space=VMEM)
+    anywhere = pl.BlockSpec(memory_space=pl.ANY)
+    shape = jax.ShapeDtypeStruct
+    with_columns = bool(column_operands)
+    column_shapes, column_scratch = (), []
+    if with_columns:
+        block = column_operands[1].shape[2] // 4
+        chunk = width // lines
+        column_shapes = (shape((places, chunk // 2, block), bf16),)
+        column_scratch = [
+            VMEM((4, chunk, block), bf16),
+            VMEM((lines, 2, chunk, block), bf16),
+            VMEM((2, chunk, block), bf16),
+            VMEM((lines, chunk, block), bf16),
+            VMEM((lines, chunk, block), bf16),
+            DMA((GroupSum.sems, lines)),
+            DMA((3, places)),
+        ]
+    return pl.pallas_call(
+        functools.partial(grads_kernel, lines, with_columns),
+        out_shape=(
+            shape((tall, wide), bf16),
+            shape((tall, shard), bf16),
+            shape((4, quarter, shard), bf16),
+        )
+        + column_shapes,
+        in_specs=[in_vmem] * 4 + [anywhere] + [in_vmem] * len(column_operands),
+        out_specs=[anywhere] * (3 + len(column_shapes)),
+        scratch_shapes=[
+            VMEM((places, tall, wide), bf16),
+            VMEM((lines, tall, wide), bf16),
+            VMEM((2, lines - 1, tall, wide), bf16),
+            VMEM((places, tall, shard), bf16),
+            VMEM((lines, tall, shard), bf16),
+            VMEM((2, lines - 1, tall, shard), bf16),
+            VMEM((tall, wide + shard), bf16),
+            DMA((LineSum.sems, lines)),
+            DMA((LineSum.sems, lines)),
+            DMA((3, 4)),
+            DMA((3, 2)),
+        ]
+        + column_scratch,
+        compiler_params=pltpu.CompilerParams(
+            collective_id=3, has_side_effects=True, vmem_limit_bytes=vmem_bytes
+        ),
+        name="grads",
+    )(*operands, *column_operands)
+
+
 def per_device(
     tokens,
     doc_bounds,
@@ -949,7 +1482,6 @@
     padded_piece = -(-piece // 32) * 32
     padded = padded_piece * fsdp_size
     ctx_place = lax.axis_index("ctx")
-    source = tokens[0].astype(jnp.float32)
     bounds = doc_bounds[0]
     query_index = ctx_place * rows + jnp.arange(rows, dtype=jnp.int32)
     key_index = jnp.arange(length, dtype=jnp.int32)
@@ -1008,26 +1540,13 @@
         ),
         head_count,
     )
-    normed = normed.reshape(fsdp_size * rows, -1)
-    mixed = mixed.reshape(fsdp_size * rows, -1)
-    window = window.reshape(length, -1)
-    key_rows = window[:, :HD]
-    value_rows = window[:, HD:]
-    w_qkv = jnp.concatenate([query_weight, keyval_weight], axis=1)
-
-    def collect(value):
-        return lax.all_to_all(value, "fsdp", split_axis=0, concat_axis=1, tiled=True)
-
-    _, norm_back_one = jax.vjp(rms_norm, source, norm_one)
     w_down = w_down.reshape(padded, width)
-    if middle_bytes(lines, rows, width, padded) <= vmem_bytes:
+    fits = middle_bytes(lines, rows, width, padded) <= vmem_bytes
+    if fits:
         grad_middle, gain_two_term, grad_gate_up, down_part, normed_two, result_parts = middle_part(
             lines, (cot_all, w_down, norm_two[None], normed_two, middle, w_columns), padded
         )
         gain_two_term = gain_two_term[0]
-        normed_two = normed_two.reshape(length, width)
-        grad_gate_up = grad_gate_up.reshape(length, 2 * padded)
-        result_parts = result_parts.reshape(length, width)
     else:
         cot_all = cot_all.reshape(length, width)
         normed_two = lax.all_gather(normed_two, "ctx", axis=0, tiled=True)
@@ -1056,96 +1575,51 @@
             scatter_dimension=1,
             tiled=True,
         ).reshape(fsdp_size, padded_piece, -1)
-    branch_two = lax.psum_scatter(result_parts, "ctx", scatter_dimension=0, tiled=True)
-    result = (middle + branch_two.astype(f32)).astype(bf16)
-
-    per_owner = ctx_size // fsdp_size
-    down_grad = lax.all_to_all(jnp.repeat(down_part, per_owner, axis=0), "ctx", 0, 0, tiled=True)
-    first = (ctx_place % per_owner) * fsdp_size
-    down_grad = lax.dynamic_slice_in_dim(down_grad, first, fsdp_size, 0)
+    operands = (
+        grad_middle,
+        weights,
+        window,
+        queries,
+        tokens[0],
+        norm_one[None],
+        cosine,
+        sine,
+        out_weight,
+        query_weight,
+        keyval_weight,
+    )
+    if fits:
+        result, input_grad, gain_one_term, grad_branch, grad_linear = back(
+            lines, operands, (middle, result_parts.reshape(ctx_size, rows, width))
+        )
+    else:
+        input_grad, gain_one_term, grad_branch, grad_linear = back(lines, operands, ())
+        branch_two = lax.psum_scatter(result_parts, "ctx", scatter_dimension=0, tiled=True)
+        result = (middle + branch_two.astype(f32)).astype(bf16)
+    gain_one_term = gain_one_term[0]
+
+    operands = (normed, mixed, grad_branch, grad_linear, down_part)
+    if fits:
+        projection_grad, out_grad, down_grad, gate_up_part = weight_grads(
+            lines, operands, (normed_two, grad_gate_up)
+        )
+    else:
+        projection_grad, out_grad, down_grad = weight_grads(lines, operands, ())
+        gate_up_part = lax.psum_scatter(
+            contract_tokens(normed_two, grad_gate_up).astype(bf16),
+            "fsdp",
+            scatter_dimension=1,
+            tiled=True,
+        )
+        gate_up_part = lax.all_to_all(
+            gate_up_part.reshape(ctx_size, width // ctx_size, -1), "ctx", 0, 0, tiled=True
+        )
+    query_grad = projection_grad[:, : inner_width // fsdp_size].astype(f32)
+    keyval_grad = projection_grad[:, inner_width // fsdp_size :].astype(f32)
+    out_grad = out_grad.astype(f32)
     down_grad = down_grad[:, :piece].reshape(fsdp_size * piece, -1).astype(f32)
-
-    gate_up_part = lax.psum_scatter(
-        contract_tokens(normed_two, grad_gate_up).astype(bf16),
-        "fsdp",
-        scatter_dimension=1,
-        tiled=True,
-    )
-    gate_up_part = lax.all_to_all(
-        gate_up_part.reshape(ctx_size, width // ctx_size, -1), "ctx", 0, 0, tiled=True
-    )
     gate_up_part = gate_up_part.reshape(ctx_size, width // ctx_size, 2, padded_piece)[..., :piece]
-    gate_up_grad = (
-        gate_up_part.transpose(1, 2, 0, 3).reshape(width // ctx_size, -1).astype(f32)
-    )
-
-    grad_branch = lax.all_gather(grad_middle.astype(jnp.bfloat16), "fsdp", axis=0, tiled=True)
-    grad_mixed = collect(contract_rows(grad_branch, out_weight).astype(jnp.bfloat16))
-    grad_mixed = grad_mixed.reshape(rows, head_count, HD)
-
-    grad_weights = jnp.einsum(
-        "thd,kd->htk", grad_mixed, value_rows, preferred_element_type=jnp.float32
-    )
-    row_delta = jnp.sum(weights * grad_weights, axis=-1, keepdims=True)
-    grad_scores = (weights * (grad_weights - row_delta)).astype(jnp.bfloat16)
-    grad_queries = jnp.einsum(
-        "htk,kd->htd", grad_scores, key_rows, preferred_element_type=jnp.float32
-    )
-    grad_keys = jnp.einsum("htk,htd->kd", grad_scores, queries, preferred_element_type=jnp.float32)
-    grad_values = jnp.einsum(
-        "htk,thd->kd", weights, grad_mixed, preferred_element_type=jnp.float32
-    )
-    own_grad = lax.psum_scatter(
-        jnp.concatenate([grad_keys, grad_values], axis=1).astype(jnp.bfloat16),
-        "ctx",
-        scatter_dimension=0,
-        tiled=True,
-    ).astype(jnp.float32)
-
-    def turned_back(part):
-        first = part[..., :128]
-        swapped = jnp.concatenate([first[..., 64:], first[..., :64]], axis=-1)
-        return jnp.concatenate([first * cosine - swapped * sine, part[..., 128:]], axis=-1)
-
-    grad_linear = jnp.concatenate(
-        [
-            (turned_back(grad_queries) * HD**-0.5).transpose(1, 0, 2).reshape(rows, inner_width),
-            turned_back(own_grad[:, :HD]),
-            own_grad[:, HD:],
-        ],
-        axis=1,
-    )
-    grad_linear = lax.all_gather(grad_linear.astype(jnp.bfloat16), "fsdp", axis=0, tiled=True)
-    grad_normed = collect(contract_rows(grad_linear, w_qkv).astype(jnp.bfloat16))
-    grad_source_norm, gain_one_term = norm_back_one(grad_normed.astype(jnp.float32))
-    input_grad = (grad_middle + grad_source_norm).astype(jnp.bfloat16)
-
-
-    def in_blocks(term):
-        tall, wide = term.shape
-        term = term.astype(jnp.bfloat16)
-        term = term.reshape(per_owner, tall // per_owner, fsdp_size, wide // fsdp_size)
-        return term.transpose(0, 2, 1, 3).reshape(ctx_size, tall // per_owner, wide // fsdp_size)
-
-    def summed(blocks):
-        block = lax.psum_scatter(blocks, "ctx", scatter_dimension=0, tiled=True)[0]
-        pairs = [
-            ((r * fsdp_size + g) * fsdp_size + f, (per_owner * f + r) * fsdp_size + g)
-            for r in range(per_owner)
-            for g in range(fsdp_size)
-            for f in range(fsdp_size)
-        ]
-        return lax.ppermute(block, ("ctx", "fsdp"), pairs).astype(jnp.float32)
-
-    out_grad = summed(in_blocks(contract_tokens(mixed, grad_branch)))
-    qkv_term = contract_tokens(normed, grad_linear)
-    qkv_block = summed(
-        jnp.concatenate(
-            [in_blocks(qkv_term[:, :inner_width]), in_blocks(qkv_term[:, inner_width:])], axis=2
-        )
-    )
-    query_grad = qkv_block[:, : inner_width // fsdp_size]
-    keyval_grad = qkv_block[:, inner_width // fsdp_size :]
+    gate_up_grad = gate_up_part.transpose(1, 2, 0, 3).reshape(width // ctx_size, -1).astype(f32)
     gains = lax.psum_scatter(
         jnp.stack([gain_one_term, gain_two_term]),
         ("ctx", "fsdp"),

time: 1050 us -> 628 us (0.60); the launches traced: 1030 us -> 619 us
  waiting for transfers between devices: 567 us -> 0.02 us
  Pallas kernels: 264 us -> 551 us
  matrix products: 41.9 us -> 0 us
  blocking collectives: 33.7 us -> 0 us
  local copies, waits for them, and re-layouts: 64.2 us -> 38.7 us
  starting transfers between devices: 16.3 us -> 0.04 us
  other arithmetic: 26.2 us -> 14.1 us
    reduce_scatter x5 -> x0, waiting for transfers between devices: 376 us -> none  [the longest x2 195 us: summed(): block = lax.psum_scatter(blocks, 'ctx', scatter_dimension=0, tiled=True)[0]]
    pallas_call x0 -> x2, Pallas kernels: none -> 288 us  [the longest x1 187 us: weight_grads(): pl.pallas_call(functools.partial(grads_kernel, lines, with_columns), out_...]
    unnamed x9 -> x2, waiting for transfers between devices: 125 us -> 0.02 us
    dot_general x9 -> x0, matrix products: 41.9 us -> none  [the longest x3 25.2 us: contract_tokens(): lax.dot_general(left, right, (((0,), (0,)), ((), ())), preferred_element_...]
    all_gather x2 -> x0, waiting for transfers between devices: 34.2 us -> none  [the longest x1 34.2 us: per_device(): lax.all_gather(grad_middle.astype(jnp.bfloat16), 'fsdp', axis=0, tiled=True)]
    all_to_all x2 -> x0, blocking collectives: 33.7 us -> none  [collect(): lax.all_to_all(value, 'fsdp', split_axis=0, concat_axis=1, tiled=True)]
    all_to_all x2 -> x0, waiting for transfers between devices: 31.8 us -> none  [the longest x1 31.8 us: per_device(): lax.all_to_all(jnp.repeat(down_part, per_owner, axis=0), 'ctx', 0, 0, til...]
    all_to_all x2 -> x0, starting transfers between devices: 11.5 us -> none  [the longest x1 6.19 us: per_device(): lax.all_to_all(gate_up_part.reshape(ctx_size, width // ctx_size, -1), 'ct...]
  transfers between devices with their start and end apart: 12 -> 1, of which waited for: 8 -> 0; matrix products, arithmetic and copies ran while one was open for 7% -> 4% of each run, Pallas kernels for 0% -> 30%
where the time goes in v4:
time: 628 us; the launch traced here: 619 us
  Pallas kernels  551 us (88%)
  local copies, waits for them, and re-layouts  38.7 us (6%)
  between operations  14.6 us (2%)
  other arithmetic  14.1 us (2%)
    pallas_call x1, Pallas kernels, weight_grads(): pl.pallas_call(functools.partial(grads_kernel, lines, with_columns), out_...  187 us
    pallas_call x1, Pallas kernels, middle_part(): pl.pallas_call(functools.partial(middle_kernel, lines), out_shape=(shape(...  159 us
    pallas_call x1, Pallas kernels, front(): pl.pallas_call(functools.partial(front_kernel, lines), out_shape=(shape((...  105 us
    pallas_call x1, Pallas kernels, back(): pl.pallas_call(functools.partial(back_kernel, lines, with_result), out_sh...  100 us
  transfers between devices with their start and end apart: 1, of which 0 were waited for; matrix products, arithmetic and copies ran while one was open for 4% of the time, Pallas kernels for 30%

profile of v4, /device:TPU:4, one launch (start us, length us, event | category | flops | bytes accessed | tf_op | source)
XLA Modules:
  0.0 618.7 jit_solution(7350599263569681145)
XLA Ops:
  7.2 0.0 reduce-scatter.4.cloned.1.call-start
  7.3 1.3 fusion.10
  8.6 1.3 fusion.6
  9.9 1.3 convert_add_fusion
  11.2 1.3 broadcast_in_dim.22.gain_one
  12.5 1.3 broadcast_in_dim.36.gain_two
  13.8 0.3 fusion.5
  14.1 0.7 pad_maximum_fusion.cosine
  14.8 3.4 constant_dynamic-slice_fusion
  18.3 0.8 pad_dynamic-update-slice_fusion.7
  19.1 0.7 pad_maximum_fusion.1.sine
  19.8 1.4 constant_dynamic-slice_fusion.8
  21.2 1.1 pad.29.w_rows
  22.3 0.8 pad_dynamic-update-slice_fusion.6
  23.1 0.8 pad_dynamic-update-slice_fusion.5
  23.8 0.8 pad_dynamic-update-slice_fusion.4
  24.6 0.8 pad_dynamic-update-slice_fusion.3
  25.4 0.8 pad_dynamic-update-slice_fusion.2
  26.2 0.8 pad_dynamic-update-slice_fusion.1
  26.9 0.8 pad_dynamic-update-slice_fusion.w_columns
  27.7 1.0 fusion.4.bias
  28.7 104.9 %front.1 = (bf16[4,128,640]{2,1,0:T(8,128)(2,1)}, bf16[10,128,256]{2,1,0:T(8,128)(2,1)}, bf16[8,128,512]{2,1,0:T(8,128)(2,1)}, bf16[10,128,1024]{2,1,0:T(8,128)(...) custom-call(bf16[128,2560]{1,0:T(8,128)(2,1)} %bitcast.20, ...), custom_call_target="tpu_custom_call" | custom-call | tf_op jit(solution)/shard_map/front/pallas_call | solution.py:665
  133.6 158.6 %middle.1 = (f32[128,2560]{1,0:T(8,128)}, f32[1,2560]{1,0:T(1,128)}, bf16[4,256,2048]{2,1,0:T(8,128)(2,1)}, bf16[4,256,640]{2,1,0:T(8,128)(2,1)}, bf16[8,128,256...) custom-call(bf16[8,128,2560]{2,1,0:T(8,128)(2,1)} %get-tuple-element.33.cot_all, bf16[1024,2560]{1,0:T(8,128)(2,1)} %bitcast.18, ...), custom_call_target="tpu_custom_call" | custom-call | tf_op jit(solution)/shard_map/middle/pallas_call | solution.py:927
  292.2 0.0 copy-start.3
  292.2 100.4 %back.1 = (bf16[128,2560]{1,0:T(8,128)(2,1)}, bf16[128,2560]{1,0:T(8,128)(2,1)}, f32[1,2560]{1,0:T(1,128)}, bf16[4,128,2560]{2,1,0:T(8,128)(2,1)}, bf16[4,128,3072]{2,1,0:T(8,128)(2,1)}) custom-call(f32[128,2560]{1,0:T(8,128)} %get-tuple-element.37.grad_middle, bf16[10,128,1024]{2,1,0:T(8,128)(2,1)} %get-tuple-element.38.probs, ...), custom_call_target="tpu_custom_call" | custom-call | tf_op jit(solution)/shard_map/back/pallas_call | solution.py:1160
  392.6 0.0 copy-done.3
  392.6 0.7 pad_maximum_fusion.2
  393.3 1.5 copy.21
  394.8 0.0 reduce-scatter.4.cloned.1.call-update
  394.8 187.4 %grads.1 = (bf16[320,768]{1,0:T(8,128)(2,1)}, bf16[320,640]{1,0:T(8,128)(2,1)}, bf16[4,256,640]{2,1,0:T(8,128)(2,1)}, bf16[8,320,512]{2,1,0:T(8,128)(2,1)}) custom-call(bf16[4,128,640]{2,1,0:T(8,128)(2,1)} %get-tuple-element.46.normed, bf16[4,128,640]{2,1,0:T(8,128)(2,1)} %get-tuple-element.47.mixed, bf16[4,128,2560]{2,1,0:T(8,128)(2,1)} %get-tuple-element.48.branch_all, ...), custom_call_target="tpu_custom_call" | custom-call | tf_op jit(solution)/shard_map/grads/pallas_call | solution.py:1429
  582.3 1.9 slice_convert_fusion
  584.2 1.4 slice.39
  585.6 1.7 bitcast_convert_fusion
  587.3 3.5 reshape.69
  590.9 0.0 copy-start.2
  590.9 1.8 convert_bitcast_fusion
  592.7 1.6 slice_convert_fusion.1
  594.2 0.0 copy-done.2
  594.2 0.9 convert_element_type.85
  595.2 5.3 copy.20
  600.5 7.1 %reshape.70 = f32[320,3840]{1,0:T(8,128)} reshape(f32[320,2,8,240]{3,2,1,0:T(8,128)} %copy.20) | data formatting | bytes 9830400 | tf_op jit(solution)/shard_map/convert_element_type | solution.py:1622
  607.6 0.9 fusion.9
  608.5 0.6 copy.24
  609.1 0.6 copy.23
  609.7 0.0 copy-done.1
  609.7 0.8 copy.34
  610.5 0.0 copy-done
  610.5 0.8 copy.35
  (5 shorter events, 0.0 us)
Async XLA Ops:
  7.2 600.4 %reduce-scatter.4.cloned.1.call-start = ((), (), s32[]{:S(2)}) async-start(), calls=%async_computation.1 | async-start | bytes 1351680
  292.2 100.4 %copy-start.3 = (f32[1,2560]{1,0:T(1,128)S(1)}, f32[1,2560]{1,0:T(1,128)}, u32[]{:S(2)}) copy-start(f32[1,2560]{1,0:T(1,128)} %get-tuple-element.45) | copy-start | bytes 30724
  590.9 3.4 copy-start.2
  600.5 9.2 %copy-start.1 = (bf16[128,2560]{1,0:T(8,128)(2,1)S(1)}, bf16[128,2560]{1,0:T(8,128)(2,1)}, u32[]{:S(2)}) copy-start(bf16[128,2560]{1,0:T(8,128)(2,1)} %get-tuple-element.42) | copy-start | bytes 1966084
  600.5 10.0 %copy-start = (bf16[128,2560]{1,0:T(8,128)(2,1)S(1)}, bf16[128,2560]{1,0:T(8,128)(2,1)}, u32[]{:S(2)}) copy-start(bf16[128,2560]{1,0:T(8,128)(2,1)} %get-tuple-element.43) | copy-start | bytes 1966084
Sparse Core Ops, SparseCore 0:
  395.0 132.7 reduce-scatter.3

commit v5 on v4

--- a/solution.py
+++ b/solution.py
@@ -1,4 +1,5 @@
 import functools
+import math
 
 import jax
 import jax.numpy as jnp
@@ -23,24 +24,8 @@
     return values * lax.rsqrt(jnp.mean(values * values, axis=-1, keepdims=True) + epsilon) * gain
 
 
-def frequencies(quarter):
-    return 10000.0 ** (-jnp.arange(quarter, dtype=jnp.float32) / quarter)
-
-
 def documents(index, bounds):
     return (index >= bounds[0]).astype(jnp.int32) + (index >= bounds[1]).astype(jnp.int32)
-
-
-def rotary_angles(index, bounds):
-    member = documents(index, bounds)
-    opening = jnp.where(member == 0, 0, jnp.where(member == 1, bounds[0], bounds[1]))
-    return (index - opening).astype(jnp.float32)[:, None] * frequencies(HD // 4)[None, :]
-
-
-def visible(query_index, key_index, bounds):
-    apart = query_index[:, None] - key_index[None, :]
-    same_doc = documents(query_index, bounds)[:, None] == documents(key_index, bounds)[None, :]
-    return (apart >= 0) & (apart < WINDOW) & (key_index[None, :] >= 0) & same_doc
 
 
 def contract_rows(left, right):
@@ -53,10 +38,6 @@
     return lax.dot_general(
         left, right, (((0,), (0,)), ((), ())), preferred_element_type=jnp.float32
     )
-
-
-def gelu_product(gate_part, up_part):
-    return jax.nn.gelu(gate_part, approximate=True) * up_part
 
 
 def remote(src, dst, send_sem, recv_sem, device):
@@ -240,7 +221,7 @@
         )
 
     def add(self, at, other):
-        self.parts[at] = (self.parts[at].astype(f32) + other.astype(f32)).astype(bf16)
+        self.parts[at] = (self.parts[at].astype(f32) + other.astype(f32)).astype(self.parts.dtype)
 
     def start(self, ahead=2):
         for turn in range(min(ahead, self.p.lines)):
@@ -399,12 +380,106 @@
             self.copy(d).wait_send()
 
 
+class BlockMove:
+    def __init__(self, place, per_owner, src, dst, sems):
+        p = place
+        self.src, self.dst, self.s = src, dst, sems
+        self.to_ctx, self.to_f = per_owner * p.f + p.c // 4, p.c % 4
+        self.from_ctx, self.from_f = 4 * (p.c % per_owner) + p.f, p.c // per_owner
+        self.moves = (self.to_ctx != p.c) | (self.to_f != p.f)
+
+    def greets(self):
+        return [
+            (self.moves, {"ctx": self.to_ctx, "fsdp": self.to_f}),
+            (self.moves, {"ctx": self.from_ctx, "fsdp": self.from_f}),
+        ]
+
+    def copy(self):
+        device = {"ctx": self.to_ctx, "fsdp": self.to_f}
+        return remote(self.src, self.dst, self.s.at[0], self.s.at[1], device)
+
+    def stay(self):
+        return pltpu.make_async_copy(self.src, self.dst, self.s.at[2])
+
+    def start(self):
+        pl.when(self.moves)(lambda: self.copy().start())
+        pl.when(~self.moves)(lambda: self.stay().start())
+
+    def finish(self):
+        @pl.when(self.moves)
+        def _():
+            self.copy().wait_send()
+            self.copy().wait_recv()
+
+        pl.when(~self.moves)(lambda: self.stay().wait())
+
+
+class PieceMove:
+    def __init__(self, place, per_owner, pieces, slots, sems):
+        p = place
+        self.p, self.n, self.pieces, self.slots, self.s = p, per_owner, pieces, slots, sems
+        self.at = hidden_piece(p.c, p.lines)
+
+    def dest(self, q):
+        return self.n * q + self.at // 4
+
+    def copy(self, q):
+        return remote(
+            self.pieces.at[q],
+            self.slots.at[self.at % 4],
+            self.s.at[0, q],
+            self.s.at[1, self.at % 4],
+            {"ctx": self.dest(q)},
+        )
+
+    def stay(self, q):
+        return pltpu.make_async_copy(self.pieces.at[q], self.slots.at[self.at % 4], self.s.at[2, 0])
+
+    def start(self):
+        for q in range(4):
+            here = self.dest(q) == self.p.c
+            pl.when(~here)(lambda q=q: self.copy(q).start())
+            pl.when(here)(lambda q=q: self.stay(q).start())
+
+    def finish(self):
+        p = self.p
+        for q in range(4):
+            here = self.dest(q) == p.c
+            pl.when(~here)(lambda q=q: self.copy(q).wait_send())
+            pl.when(here)(lambda q=q: self.stay(q).wait())
+        for i in range(4):
+            source = place_of_piece(4 * (p.c % self.n) + i, p.lines)
+            slot = self.slots.at[i]
+            arrival = remote(slot, slot, self.s.at[0, 0], self.s.at[1, i], p.beside)
+            pl.when(source != p.c)(lambda arrival=arrival: arrival.wait_recv())
+
+
+def hidden_piece(c, lines):
+    return (c % 2) * lines + c // 2
+
+
+def place_of_piece(piece, lines):
+    return (piece % lines) * 2 + piece // lines
+
+
 class GroupReturn(GroupTrade):
     def __init__(self, place, whole, slots, sems):
         super().__init__(place, whole, slots, sems, 0)
 
     def block(self, g):
         return self.whole.at[g]
+
+
+def rotary_tables(first, rows, bounds):
+    index = first + lax.broadcasted_iota(jnp.int32, (rows, 128), 0)
+    lane = lax.broadcasted_iota(jnp.int32, (rows, 128), 1)
+    quarter = HD // 4
+    member = documents(index, bounds)
+    opening = jnp.where(member == 0, 0, jnp.where(member == 1, bounds[0], bounds[1]))
+    frequency = jnp.exp((lane % quarter).astype(f32) * (-math.log(10000.0) / quarter))
+    angles = (index - opening).astype(f32) * frequency
+    sine = jnp.sin(angles)
+    return jnp.cos(angles), jnp.where(lane < quarter, -sine, sine)
 
 
 def rotated(v, cosine, sine):
@@ -490,17 +565,15 @@
 
 def front_kernel(
     lines,
+    bounds_ref,
     x_ref,
-    gain_one,
-    gain_two,
-    cosine,
-    sine,
-    bias,
+    gains,
     w_keyval,
     w_query,
     w_out,
     cot,
-    w_rows,
+    w_down,
+    w_gate_up,
     normed_out,
     query_out,
     keyval_out,
@@ -508,6 +581,9 @@
     mixed_out,
     middle_out,
     normed_two_out,
+    cosine,
+    sine,
+    columns_out,
     cot_all,
     rows_all,
     whole,
@@ -518,6 +594,9 @@
     far,
     keyval,
     mixed,
+    bias,
+    w_rows,
+    windows,
     trade_sems,
     sum_sems,
     keyval_sems,
@@ -527,22 +606,86 @@
 ):
     p = Place(lines)
     rows, width = x_ref.shape
+    length = bias.shape[1]
     heads = query_out.shape[0]
     inner = heads * HD
     kv_width = 2 * HD
     p.barrier()
 
+    units = w_gate_up.shape[1] // 2
+    piece = units // (4 * 2 * lines)
+    padded_piece = w_rows.shape[0]
+    own_piece = hidden_piece(p.c, lines)
+    if w_down.shape[0] == padded_piece:
+        rows_copy = pltpu.make_async_copy(w_down, w_rows, own_sems.at[2])
+    else:
+        rows_copy = pltpu.make_async_copy(
+            w_down.at[pl.ds(pl.multiple_of(own_piece * piece, 16), piece)],
+            w_rows.at[pl.ds(0, piece)],
+            own_sems.at[2],
+        )
+    rows_copy.start()
+    span = windows.shape[2]
+    shard = w_gate_up.shape[0]
+
+    def window_first(q):
+        first = q * (units // 4) + own_piece * piece
+        return jnp.minimum(first // 128 * 128, 2 * units - span), first
+
+    def window(q):
+        return pltpu.make_async_copy(
+            w_gate_up.at[:, pl.ds(pl.multiple_of(window_first(q)[0], 128), span)],
+            windows.at[q % 2],
+            own_sems.at[3 + q % 2],
+        )
+
+    def pack_columns(q):
+        window(q).wait()
+        start, first = window_first(q)
+        by = first - start
+        lane = lax.broadcasted_iota(jnp.int32, (shard, 128), 1)
+        tiles = [
+            pltpu.roll(windows[q % 2, :, t * 128 : (t + 1) * 128].astype(f32), (128 - by % 128) % 128, 1)
+            for t in range(span // 128)
+        ]
+        late = by >= 128
+        turned = []
+        for t in range(span // 128 - 1):
+            turned.append(jnp.where(lane < 128 - by % 128, tiles[t], tiles[t + 1]))
+        turned.append(jnp.where(lane < 128 - by % 128, tiles[-1], 0.0))
+        turned = [
+            jnp.where(late, turned[t + 1], turned[t]) for t in range(span // 128 - 1)
+        ]
+        turned = jnp.concatenate(turned, axis=1)[:, :padded_piece]
+        lane = lax.broadcasted_iota(jnp.int32, (shard, padded_piece), 1)
+        columns_out[:, q * padded_piece : (q + 1) * padded_piece] = jnp.where(
+            lane < piece, turned, 0.0
+        ).astype(bf16)
+        if q + 2 < 8:
+            window(q + 2).start()
+
+    window(0).start()
+    window(1).start()
     down = GroupGather(p, w_rows, rows_all, row_sems, own_sems.at[0], row_sems.shape[1])
     cot_gather = LineGather(p, cot, cot_all, cot_sems)
     cot_local = pltpu.make_async_copy(cot, cot_all.at[p.c], own_sems.at[1])
 
     source = x_ref[...].astype(f32)
-    whole[...] = rms_norm(source, gain_one[...]).astype(bf16)
+    whole[...] = rms_norm(source, gains[0:1]).astype(bf16)
     trade = GroupTrade(p, whole, slots.at[0], trade_sems.at[0], slots.shape[3])
     trade.start()
-    down.local().start()
     cot_local.start()
     cot_gather.start()
+    bounds = (bounds_ref[0, 0], bounds_ref[0, 1])
+    cosine[...], sine[...] = rotary_tables(p.c * rows, rows, bounds)
+    query_at = p.c * rows + lax.broadcasted_iota(jnp.int32, (rows, length), 0)
+    key_at = lax.broadcasted_iota(jnp.int32, (rows, length), 1)
+    allowed = (
+        (query_at >= key_at)
+        & (query_at - key_at < WINDOW)
+        & (documents(query_at, bounds) == documents(key_at, bounds))
+    )
+    bias[...] = jnp.where(allowed, 0.0, -1e30)
     trade.wait()
     normed_out[...] = slots[0]
 
@@ -585,6 +728,12 @@
             query_out[at] = (turned * HD**-0.5).astype(bf16)
         if i == 1:
             kv_gather.step(0)
+    rows_copy.wait()
+    if w_down.shape[0] != padded_piece and piece < padded_piece:
+        w_rows[pl.ds(piece, padded_piece - piece)] = jnp.zeros(
+            (padded_piece - piece, width), bf16
+        )
+    down.local().start()
     for i in range(down.pieces):
         down.give(i)
     for step in range(1, lines - 1):
@@ -594,7 +743,6 @@
         cot_gather.step(1)
     keyval_out[...] = keyval[...]
 
-    length = bias.shape[1]
 
     def two_heads(i, carry):
         keys = keyval[:, :, :HD].reshape(length, HD)
@@ -615,6 +763,8 @@
     lax.fori_loop(0, heads // 2, two_heads, 0)
     trade_two = GroupTrade(p, mixed, slots.at[1], trade_sems.at[1], slots.shape[3])
     trade_two.start()
+    for q in range(4):
+        pack_columns(q)
     for step in range(2, lines - 1):
         cot_gather.step(step)
     for i in range(len(chunks)):
@@ -630,11 +780,13 @@
         group_two.give(i, spans_two[i])
     for i in range(2):
         group_two.pass_on(i, spans_two[i])
+    for q in range(4, 8):
+        pack_columns(q)
     for i in range(2):
         middle_out[:, spans_two[i]] = x_ref[:, spans_two[i]].astype(f32) + group_two.take(
             i, spans_two[i]
         )
-    normed_two_out[...] = rms_norm(middle_out[...], gain_two[...]).astype(bf16)
+    normed_two_out[...] = rms_norm(middle_out[...], gains[1:2]).astype(bf16)
 
     for i in range(down.pieces):
         down.pass_on(i)
@@ -649,8 +801,8 @@
     cot_gather.finish()
 
 
-def front(lines, operands, heads):
-    x = operands[0]
+def front(lines, operands, heads, padded_piece):
+    x = operands[1]
     rows, width = x.shape
     places = 2 * lines
     length = places * rows
@@ -672,11 +824,14 @@
             shape((4, rows, shard), bf16),
             shape((rows, width), f32),
             shape((rows, width), bf16),
+            shape((rows, 128), f32),
+            shape((rows, 128), f32),
+            shape((shard, 8 * padded_piece), bf16),
             shape((places, rows, width), bf16),
-            shape((4,) + operands[10].shape, bf16),
+            shape((4, padded_piece, width), bf16),
         ),
-        in_specs=[in_vmem] * 9 + [anywhere] * 2,
-        out_specs=[in_vmem] * 7 + [anywhere] * 2,
+        in_specs=[pl.BlockSpec(memory_space=pltpu.SMEM)] + [in_vmem] * 5 + [anywhere] * 3,
+        out_specs=[in_vmem] * 10 + [anywhere] * 2,
         scratch_shapes=[
             VMEM((rows, width), bf16),
             VMEM((2, 4, rows, shard), bf16),
@@ -686,12 +841,15 @@
             VMEM((rows, parts_width), bf16),
             VMEM((places, rows, 2 * HD), bf16),
             VMEM((rows, inner), bf16),
+            VMEM((rows, length), f32),
+            VMEM((padded_piece, width), bf16),
+            VMEM((2, shard, (padded_piece + 127) // 128 * 128 + 128), bf16),
             DMA((2, GroupTrade.sems, 4)),
             DMA((2, GroupSum.sems, 3)),
             DMA((LineGather.sems, lines)),
             DMA((LineGather.sems, lines)),
             DMA((GroupGather.sems, pieces)),
-            DMA((2,)),
+            DMA((5,)),
         ],
         compiler_params=pltpu.CompilerParams(
             collective_id=0, has_side_effects=True, vmem_limit_bytes=vmem_bytes
@@ -721,7 +879,7 @@
     lines,
     cot_all,
     w_rows,
-    gain_two,
+    gains,
     own,
     middle,
     w_columns,
@@ -892,7 +1050,7 @@
     line_sum.far(lines - 1)
     grad = line_sum.total()
     middle_local.wait()
-    grad_values, gain = norm_back(grad_middle_out[...], gain_two[...], grad)
+    grad_values, gain = norm_back(grad_middle_out[...], gains[1:2], grad)
     grad_middle_out[...] = cot_all[p.c].astype(f32) + grad_values
     gain_out[...] = gain
     for i in (2, 3):
@@ -960,6 +1118,10 @@
     )(*operands)
 
 
+def is_long(length):
+    return length > 2048
+
+
 def back_kernel(
     lines,
     with_result,
@@ -967,13 +1129,15 @@
     probs,
     keyval,
     queries,
+    mixed,
     tokens,
-    gain_one,
+    gains,
     cosine,
     sine,
     w_out,
     w_query,
     w_keyval,
+    down_in,
     *rest,
 ):
     if with_result:
@@ -983,6 +1147,8 @@
         gain_out,
         branch_out,
         linear_out,
+        out_out,
+        down_out,
         branch_all,
         linear_all,
         branch,
@@ -994,10 +1160,18 @@
         kv_parts,
         kv_side,
         kv_chain,
+        out_parts,
+        out_side,
+        out_chain,
+        out_stage,
+        probs_stage,
         branch_sems,
         linear_sems,
         trade_sems,
         kv_sems,
+        out_sems,
+        move_sems,
+        piece_sems,
         own_sems,
         *rest,
     ) = rest
@@ -1007,7 +1181,11 @@
     length = probs.shape[2]
     shard = w_out.shape[0]
     kv_width = 2 * HD
-    p.barrier()
+    per_owner = 2 * lines // 4
+    tall = shard // per_owner
+    out_move = BlockMove(p, per_owner, out_stage, out_out, move_sems)
+    others = [(jnp.full((), True), {"ctx": (p.c + d) % (2 * lines)}) for d in range(1, 2 * lines)]
+    p.barrier(ctx=False, also=others + out_move.greets())
     if with_result:
         result_parts, result_side, result_chain, result_sems = rest
         result_sum = LineSum(p, result_parts, result_side, result_chain, result_sems)
@@ -1018,9 +1196,12 @@
     group = GroupGather(p, branch, branch_all, branch_sems, own_sems.at[0], 1)
     group.give(0)
     group.local().start()
+    down_move = PieceMove(p, per_owner, down_in, down_out, piece_sems)
+    down_move.start()
+    out_sum = LineSum(p, out_parts, out_side, out_chain, out_sems)
     if with_result:
         result_copy.wait()
-        result_sum.start(1)
+        result_sum.start(2)
     back_trade = GroupReturn(p, trade_parts.at[0], trade_slots.at[0], trade_sems.at[0])
 
     def mixed_back(g):
@@ -1040,8 +1221,19 @@
     back_trade.send(3)
     branch_copy = pltpu.make_async_copy(branch_all, branch_out, own_sems.at[3])
     branch_copy.start()
+
+    def out_blocks(g, carry):
+        left = mixed[...].reshape(4 * rows, shard)
+        right = branch_all[:, :, pl.ds(pl.multiple_of(g * shard, 128), shard)]
+        product = contract_tokens(left, right.reshape(4 * rows, shard))
+        for r in range(per_owner):
+            out_parts[4 * r + g] = product[r * tall : (r + 1) * tall].astype(bf16)
+        return carry
+
+    lax.fori_loop(0, 4, out_blocks, 0)
+    out_sum.start(2)
     if with_result:
-        result_sum.near(0, 1)
+        result_sum.near(0, 0)
     back_trade.wait()
     for g in range(4):
         grad_mixed[:, g * shard : (g + 1) * shard] = trade_slots[0, g]
@@ -1049,14 +1241,20 @@
     kv_total[...] = jnp.zeros_like(kv_total)
     kv_at, q_at = pl.ds(0, kv_width), pl.ds(kv_width, heads * HD)
 
-    batch = 2 if length <= 2048 else 1
+    batch = 1 if is_long(length) else 2
 
     def some_heads(i, carry):
         keys = keyval[:, :, :HD].reshape(length, HD)
         values = keyval[:, :, HD:].reshape(length, HD)
         at = [pl.multiple_of((i * batch + h) * HD, 128) for h in range(batch)]
         outer = jnp.concatenate([grad_mixed[:, pl.ds(a, HD)] for a in at], axis=0)
-        weights = probs[pl.ds(batch * i, batch)].reshape(batch * rows, length)
+        if batch == 1:
+            fetch = pltpu.make_async_copy(probs.at[i], probs_stage, own_sems.at[5])
+            fetch.start()
+            fetch.wait()
+            weights = probs_stage[...]
+        else:
+            weights = probs[pl.ds(batch * i, batch)].reshape(batch * rows, length)
         wide = weights.astype(f32)
         grad_weights = contract_rows(outer, values)
         delta = jnp.sum(wide * grad_weights, axis=-1, keepdims=True)
@@ -1078,6 +1276,7 @@
     if with_result:
         result_sum.far(0)
         result_sum.near(1, 0)
+    out_sum.near(0, 0)
     kv_parts[...] = kv_total[...].astype(bf16).reshape(kv_parts.shape)
     kv_sum = LineSum(p, kv_parts, kv_side, kv_chain, kv_sems)
     kv_sum.start(lines)
@@ -1091,6 +1290,11 @@
         for turn in range(2, lines):
             result_sum.across(turn).start()
         result_sum.far(1)
+    for turn in range(2, lines):
+        out_sum.across(turn).start()
+    out_sum.far(0)
+    out_sum.near(1, 0)
+    out_sum.far(1)
     linear_group.pass_on(0)
     linear_group.pass_on(1)
     linear_group.local().wait()
@@ -1124,9 +1328,14 @@
     for g in range(4):
         grad_mixed[:, g * shard : (g + 1) * shard] = trade_slots[1, g]
     source = tokens[...].astype(f32)
-    grad_values, gain = norm_back(source, gain_one[...], grad_mixed[...].astype(f32))
+    grad_values, gain = norm_back(source, gains[0:1], grad_mixed[...].astype(f32))
     input_grad_out[...] = (grad_middle[...] + grad_values).astype(bf16)
     gain_out[...] = gain
+    for turn in range(2, lines):
+        out_sum.near(turn, 0)
+        out_sum.far(turn)
+    out_stage[...] = out_sum.total().astype(bf16)
+    out_move.start()
     if with_result:
         result_out[...] = (middle[...] + result_sum.total()).astype(bf16)
         result_sum.finish()
@@ -1138,6 +1347,9 @@
     kv_sum.finish()
     branch_copy.wait()
     linear_copy.wait()
+    out_sum.finish()
+    down_move.finish()
+    out_move.finish()
 
 
 def back(lines, operands, result_operands):
@@ -1147,10 +1359,13 @@
     length = places * rows
     shard = width // 4
     linear_width = width + 2 * HD
+    tall = width // places
+    pieces = operands[12].shape
     in_vmem = pl.BlockSpec(memory_space=VMEM)
     anywhere = pl.BlockSpec(memory_space=pl.ANY)
     shape = jax.ShapeDtypeStruct
     with_result = bool(result_operands)
+    long = is_long(length)
     result_scratch = [
         VMEM((places, rows, width), bf16),
         VMEM((lines, rows, width), bf16),
@@ -1165,9 +1380,11 @@
             shape((1, width), f32),
             shape((4, rows, width), bf16),
             shape((4, rows, linear_width), bf16),
+            shape((tall, shard), bf16),
+            shape(pieces, bf16),
         ),
-        in_specs=[in_vmem] * 11 + ([in_vmem, anywhere] if with_result else []),
-        out_specs=[in_vmem] * (3 if with_result else 2) + [anywhere] * 2,
+        in_specs=[in_vmem, anywhere if long else in_vmem] + [in_vmem] * 10 + [anywhere] + ([in_vmem, anywhere] if with_result else []),
+        out_specs=[in_vmem] * (3 if with_result else 2) + [anywhere] * 4,
         scratch_shapes=[
             VMEM((4, rows, width), bf16),
             VMEM((4, rows, linear_width), bf16),
@@ -1180,11 +1397,19 @@
             VMEM((places, rows, 2 * HD), bf16),
             VMEM((lines, rows, 2 * HD), bf16),
             VMEM((2, lines - 1, rows, 2 * HD), bf16),
+            VMEM((places, tall, shard), bf16),
+            VMEM((lines, tall, shard), bf16),
+            VMEM((2, lines - 1, tall, shard), bf16),
+            VMEM((tall, shard), bf16),
+            VMEM((rows, length if long else 128), bf16),
             DMA((GroupGather.sems, 1)),
             DMA((GroupGather.sems, 2)),
             DMA((2, GroupTrade.sems, 4)),
             DMA((LineSum.sems, lines)),
-            DMA((5,)),
+            DMA((LineSum.sems, lines)),
+            DMA((3,)),
+            DMA((3, 4)),
+            DMA((6,)),
         ]
         + (result_scratch if with_result else []),
         compiler_params=pltpu.CompilerParams(
@@ -1194,28 +1419,29 @@
     )(*operands, *result_operands)
 
 
-def grads_kernel(lines, with_columns, normed, mixed, branch_all, linear_all, down_in, *rest):
+def grads_kernel(lines, with_columns, normed, linear_all, gain_one, gain_two, *rest):
     if with_columns:
         normed_two, hidden_grads, *rest = rest
-    projection_out, out_out, down_out, *rest = rest
+    projection_out, gains_out, *rest = rest
     if with_columns:
         columns_out, *rest = rest
     (
         parts,
         side,
         chain,
-        out_parts,
-        out_side,
-        out_chain,
-        sums,
+        stage,
+        gain_parts,
+        gain_side,
+        gain_chain,
+        gain_slots,
         projection_sems,
-        out_sems,
-        down_sems,
-        place_sems,
+        gain_sems,
+        slot_sems,
+        move_sems,
         *rest,
     ) = rest
     if with_columns:
-        chunk_parts, near, stage, far, chunks, group_sems, trade_sems, *rest = rest
+        chunk_parts, near, passing, far, chunks, group_sems, trade_sems = rest
     p = Place(lines)
     places = 2 * lines
     shard = normed.shape[2]
@@ -1223,46 +1449,18 @@
     per_owner = places // 4
     tall = shard // per_owner
     kv_share = 2 * HD // 4
-
-    to_ctx, to_f = per_owner * p.f + p.c // 4, p.c % 4
-    from_ctx, from_f = 4 * (p.c % per_owner) + p.f, p.c // per_owner
-    moves = (to_ctx != p.c) | (to_f != p.f)
-    others = [
-        (jnp.full((), True), {"ctx": (p.c + d) % places}) for d in range(1, places)
-    ] + [
-        (moves, {"ctx": to_ctx, "fsdp": to_f}),
-        (moves, {"ctx": from_ctx, "fsdp": from_f}),
-    ]
-    p.barrier(ctx=False, also=others)
-
-    def down_copy(q):
-        dest = per_owner * q + p.c // 4
-        return remote(
-            down_in.at[q], down_out.at[p.c % 4], down_sems.at[0, q], down_sems.at[1, p.c % 4], {"ctx": dest}
-        )
-
-    def down_own(q):
-        return pltpu.make_async_copy(down_in.at[q], down_out.at[p.c % 4], down_sems.at[2, 0])
-
-    def down_arrival(i):
-        slot = down_out.at[i]
-        return remote(slot, slot, down_sems.at[0, 0], down_sems.at[1, i], p.beside)
-
-    for q in range(4):
-        stays = per_owner * q + p.c // 4 == p.c
-        pl.when(~stays)(lambda q=q: down_copy(q).start())
-        pl.when(stays)(lambda q=q: down_own(q).start())
+    move = BlockMove(p, per_owner, stage, projection_out, move_sems)
+    others = [(jnp.full((), True), {"ctx": (p.c + d) % places}) for d in range(1, places)]
+    p.barrier(ctx=False, also=others + move.greets())
+
+    for c in range(places):
+        cols = slice(c * tall, (c + 1) * tall)
+        gain_parts[c, 0:1, :tall] = gain_one[:, cols]
+        gain_parts[c, 1:2, :tall] = gain_two[:, cols]
+    gain_sum = LineSum(p, gain_parts, gain_side, gain_chain, gain_sems)
+    gain_sum.start(lines)
 
     projection_sum = LineSum(p, parts, side, chain, projection_sems)
-    out_sum = LineSum(p, out_parts, out_side, out_chain, out_sems)
-
-    def out_blocks(g, carry):
-        left = mixed[...].reshape(tokens, shard)
-        right = branch_all[:, :, pl.ds(pl.multiple_of(g * shard, 128), shard)]
-        product = contract_tokens(left, right.reshape(tokens, shard))
-        for r in range(per_owner):
-            out_parts[4 * r + g] = product[r * tall : (r + 1) * tall].astype(bf16)
-        return carry
 
     def projection_blocks(g, carry):
         left = normed[...].reshape(tokens, shard)
@@ -1276,25 +1474,25 @@
             parts[4 * r + g, :, shard:] = kv_product[rows].astype(bf16)
         return carry
 
-    lax.fori_loop(0, 4, out_blocks, 0)
-    out_sum.start(2)
     lax.fori_loop(0, 4, projection_blocks, 0)
+    projection_sum.start(2)
 
     if with_columns:
         block = columns_out.shape[2]
+        chunk = chunk_parts.shape[1]
         every = slice(None)
 
         def chunk_of(k):
             return (p.line + k) % lines
 
         def group(k):
-            return GroupSum(p, chunk_parts, near.at[k], stage.at[k % 2], far.at[k], group_sems)
+            return GroupSum(p, chunk_parts, near.at[k], passing.at[k % 2], far.at[k], group_sems)
 
         def compute(k):
-            cols = pl.ds(pl.multiple_of(chunk_of(k) * chunk_parts.shape[1], 128), chunk_parts.shape[1])
+            cols = pl.ds(pl.multiple_of(chunk_of(k) * chunk, 128), chunk)
 
             def one(g, carry):
-                left = normed_two[:, :, cols].reshape(-1, chunk_parts.shape[1])
+                left = normed_two[:, :, cols].reshape(-1, chunk)
                 right = hidden_grads[:, :, pl.ds(pl.multiple_of(g * block, 128), block)]
                 chunk_parts[g] = contract_tokens(left, right.reshape(-1, block)).astype(bf16)
                 return carry
@@ -1304,7 +1502,7 @@
             group(k).give(k, every)
 
         def halves(k):
-            half = chunk_parts.shape[1] // 2
+            half = chunk // 2
             for lane in range(2):
                 yield lane, 2 * chunk_of(k) + lane, chunks.at[k, pl.ds(lane * half, half)]
 
@@ -1340,53 +1538,43 @@
                 group(k - 2).passed(k - 2, every)
             compute(k)
             group(k).pass_on(k, every)
-            out_sum.near(k, 2)
+            if k == 0:
+                gain_sum.turns(0)
+            projection_sum.near(k, 2)
             if k > 0:
-                out_sum.far(k - 1)
-        out_sum.far(lines - 1)
-    else:
-        out_sum.turns(2)
-
-    def to_place(i, src, dst):
-        return remote(
-            src, dst, place_sems.at[0, i], place_sems.at[1, i], {"ctx": to_ctx, "fsdp": to_f}
-        )
-
-    def hand_over(i, line_sum, at, dst):
-        src = sums.at[pl.ds(0, tall), at]
-        sums[:, at] = line_sum.total().astype(bf16)
-        pl.when(moves)(lambda: to_place(i, src, dst).start())
-        pl.when(~moves)(lambda: pltpu.make_async_copy(src, dst, place_sems.at[2, i]).start())
-
-    def handed(i, at, dst):
-        src = sums.at[pl.ds(0, tall), at]
-
-        @pl.when(moves)
-        def _():
-            to_place(i, src, dst).wait_send()
-            to_place(i, src, dst).wait_recv()
-
-        pl.when(~moves)(lambda: pltpu.make_async_copy(src, dst, place_sems.at[2, i]).wait())
-
-    projection_sum.start(2)
-    wide = shard + kv_share
-    hand_over(0, out_sum, pl.ds(wide, shard), out_out)
-    if with_columns:
+                projection_sum.far(k - 1)
         for k in (lines - 2, lines - 1):
             complete(k)
             group(k).passed(k, every)
         group(lines - 1).given(lines - 1, every)
-    projection_sum.turns(2)
-    hand_over(1, projection_sum, pl.ds(0, wide), projection_out)
-
-    handed(0, pl.ds(wide, shard), out_out)
-    for q in range(4):
-        stays = per_owner * q + p.c // 4 == p.c
-        pl.when(~stays)(lambda q=q: down_copy(q).wait_send())
-        pl.when(stays)(lambda q=q: down_own(q).wait())
-    for i in range(4):
-        source = 4 * (p.c % per_owner) + i
-        pl.when(source != p.c)(lambda i=i: down_arrival(i).wait_recv())
+        projection_sum.far(lines - 1)
+    else:
+        gain_sum.turns(0)
+        projection_sum.turns(2)
+
+    own = gain_sum.total()
+    gain_parts[p.c] = own
+
+    def gain_copy(d):
+        return remote(
+            gain_parts.at[p.c],
+            gain_slots.at[d],
+            slot_sems.at[0, d],
+            slot_sems.at[1, d],
+            {"fsdp": (p.f + d) % 4},
+        )
+
+    for d in (1, 2, 3):
+        gain_copy(d).start()
+    stage[...] = projection_sum.total().astype(bf16)
+    move.start()
+    for d in (1, 2, 3):
+        gain_copy(d).wait_recv()
+        own = own + gain_slots[d]
+    gains_out[...] = own
+
+    for d in (1, 2, 3):
+        gain_copy(d).wait_send()
     if with_columns:
         for k in range(lines):
             for lane, dest, src in halves(k):
@@ -1396,18 +1584,18 @@
                 pl.when(dest == p.c)(lambda src=src: place_own(src).wait())
         for i in range(places):
             pl.when(p.c != i)(lambda i=i: arrival(i).wait_recv())
-    out_sum.finish()
+    gain_sum.finish()
     projection_sum.finish()
-    handed(1, pl.ds(0, wide), projection_out)
+    move.finish()
 
 
 def weight_grads(lines, operands, column_operands):
     rows, shard = operands[0].shape[1:]
     width = 4 * shard
     places = 2 * lines
-    tall = 4 * shard // places
+    tall = width // places
     wide = shard + 2 * HD // 4
-    quarter = operands[4].shape[1]
+    gain_wide = -(-tall // 128) * 128
     in_vmem = pl.BlockSpec(memory_space=VMEM)
     anywhere = pl.BlockSpec(memory_space=pl.ANY)
     shape = jax.ShapeDtypeStruct
@@ -1428,26 +1616,22 @@
         ]
     return pl.pallas_call(
         functools.partial(grads_kernel, lines, with_columns),
-        out_shape=(
-            shape((tall, wide), bf16),
-            shape((tall, shard), bf16),
-            shape((4, quarter, shard), bf16),
-        )
-        + column_shapes,
-        in_specs=[in_vmem] * 4 + [anywhere] + [in_vmem] * len(column_operands),
-        out_specs=[anywhere] * (3 + len(column_shapes)),
+        out_shape=(shape((tall, wide), bf16), shape((8, gain_wide), f32)) + column_shapes,
+        in_specs=[in_vmem] * (4 + len(column_operands)),
+        out_specs=[anywhere, in_vmem] + [anywhere] * len(column_shapes),
         scratch_shapes=[
             VMEM((places, tall, wide), bf16),
             VMEM((lines, tall, wide), bf16),
             VMEM((2, lines - 1, tall, wide), bf16),
-            VMEM((places, tall, shard), bf16),
-            VMEM((lines, tall, shard), bf16),
-            VMEM((2, lines - 1, tall, shard), bf16),
-            VMEM((tall, wide + shard), bf16),
+            VMEM((tall, wide), bf16),
+            VMEM((places, 8, gain_wide), f32),
+            VMEM((lines, 8, gain_wide), f32),
+            VMEM((2, lines - 1, 8, gain_wide), f32),
+            VMEM((4, 8, gain_wide), f32),
             DMA((LineSum.sems, lines)),
             DMA((LineSum.sems, lines)),
-            DMA((3, 4)),
-            DMA((3, 2)),
+            DMA((2, 4)),
+            DMA((3,)),
         ]
         + column_scratch,
         compiler_params=pltpu.CompilerParams(
@@ -1455,6 +1639,64 @@
         ),
         name="grads",
     )(*operands, *column_operands)
+
+
+def assemble_kernel(lines, piece, projection, out, down, columns, *outs):
+    query_out, keyval_out, out_out, down_out, columns_out = outs
+    shard = out.shape[1]
+    padded_piece = columns.shape[2] // 2
+    query_out[...] = projection[:, :shard].astype(f32)
+    keyval_out[...] = projection[:, shard:].astype(f32)
+    out_out[...] = out[...].astype(f32)
+    for i in range(down.shape[0]):
+        down_out[i * piece : (i + 1) * piece] = down[i, :piece].astype(f32)
+    pieces = [
+        columns[place_of_piece(n, lines), :, q * padded_piece : q * padded_piece + piece]
+        for q in range(2)
+        for n in range(2 * lines)
+    ]
+    columns_out[...] = jnp.concatenate(pieces, axis=1).astype(f32)
+
+
+def assemble(lines, piece, projection, out, down, columns):
+    tall, wide = projection.shape
+    shard = out.shape[1]
+    places = 2 * lines
+    block = columns.shape[2]
+    steps = 4 if tall % 64 == 0 else 1
+    run = tall // steps
+    full = 2 * places * piece
+
+    def flat(rows, cols):
+        return pl.BlockSpec((rows, cols), lambda i: (i, 0))
+
+    shape = jax.ShapeDtypeStruct
+    return pl.pallas_call(
+        functools.partial(assemble_kernel, lines, piece),
+        grid=(steps,),
+        out_shape=(
+            shape((tall, shard), f32),
+            shape((tall, wide - shard), f32),
+            shape((tall, shard), f32),
+            shape((4 * piece, shard), f32),
+            shape((tall, full), f32),
+        ),
+        in_specs=[
+            flat(run, wide),
+            flat(run, shard),
+            pl.BlockSpec((4 // steps, down.shape[1], shard), lambda i: (i, 0, 0)),
+            pl.BlockSpec((places, run, block), lambda i: (0, i, 0)),
+        ],
+        out_specs=[
+            flat(run, shard),
+            flat(run, wide - shard),
+            flat(run, shard),
+            flat(4 // steps * piece, shard),
+            flat(run, full),
+        ],
+        compiler_params=pltpu.CompilerParams(vmem_limit_bytes=vmem_bytes),
+        name="assemble",
+    )(projection, out, down, columns)
 
 
 def per_device(
@@ -1481,38 +1723,13 @@
     piece = hidden_width // (ctx_size * fsdp_size)
     padded_piece = -(-piece // 32) * 32
     padded = padded_piece * fsdp_size
-    ctx_place = lax.axis_index("ctx")
-    bounds = doc_bounds[0]
-    query_index = ctx_place * rows + jnp.arange(rows, dtype=jnp.int32)
-    key_index = jnp.arange(length, dtype=jnp.int32)
-    allowed = visible(query_index, key_index, bounds)
-    bias = jnp.where(allowed, 0.0, -1e30).astype(jnp.float32)
-    angles = rotary_angles(query_index, bounds)
-    cosine = jnp.cos(angles)
-    sine = jnp.sin(angles)
-    cosine = jnp.concatenate([cosine, cosine], axis=1)
-    sine = jnp.concatenate([-sine, sine], axis=1)
-
-    def padded_to(value, axis):
-        pads = [(0, 0)] * value.ndim
-        pads[axis] = (0, padded_piece - piece)
-        return jnp.pad(value, pads)
-
-    shard_width = hidden_width // fsdp_size
-    w_columns = jnp.concatenate(
-        [
-            padded_to(
-                lax.dynamic_slice_in_dim(
-                    gate_up_weight, q * shard_width + ctx_place * piece, piece, 1
-                ),
-                1,
-            )
-            for q in range(2 * fsdp_size)
-        ],
-        axis=1,
-    )
-    w_rows = padded_to(lax.dynamic_slice_in_dim(down_weight, ctx_place * piece, piece, 0), 0)
+    gains = jnp.stack([norm_one, norm_two])
     cot_rows = cotangent[0]
+    down_rows = down_weight
+    if piece % 16:
+        first = hidden_piece(lax.axis_index("ctx"), lines) * piece
+        down_rows = lax.dynamic_slice_in_dim(down_weight, first, piece, 0)
+        down_rows = jnp.pad(down_rows, ((0, padded_piece - piece), (0, 0)))
     (
         normed,
         queries,
@@ -1521,32 +1738,33 @@
         mixed,
         middle,
         normed_two,
+        cosine,
+        sine,
+        w_columns,
         cot_all,
         w_down,
     ) = front(
         lines,
         (
+            doc_bounds,
             tokens[0],
-            norm_one[None],
-            norm_two[None],
-            cosine,
-            sine,
-            bias,
+            gains,
             keyval_weight,
             query_weight,
             out_weight,
             cot_rows,
-            w_rows,
+            down_rows,
+            gate_up_weight,
         ),
         head_count,
+        padded_piece,
     )
     w_down = w_down.reshape(padded, width)
     fits = middle_bytes(lines, rows, width, padded) <= vmem_bytes
     if fits:
         grad_middle, gain_two_term, grad_gate_up, down_part, normed_two, result_parts = middle_part(
-            lines, (cot_all, w_down, norm_two[None], normed_two, middle, w_columns), padded
-        )
-        gain_two_term = gain_two_term[0]
+            lines, (cot_all, w_down, gains, normed_two, middle, w_columns), padded
+        )
     else:
         cot_all = cot_all.reshape(length, width)
         normed_two = lax.all_gather(normed_two, "ctx", axis=0, tiled=True)
@@ -1566,7 +1784,6 @@
             tiled=True,
         ).astype(f32)
         grad_middle_norm, gain_two_term = norm_back(middle, norm_two[None], grad_normed_two)
-        gain_two_term = gain_two_term[0]
         grad_middle = cot_rows.astype(f32) + grad_middle_norm
         result_parts = jnp.dot(hidden, w_down, preferred_element_type=f32).astype(bf16)
         down_part = lax.psum_scatter(
@@ -1580,31 +1797,32 @@
         weights,
         window,
         queries,
+        mixed,
         tokens[0],
-        norm_one[None],
+        gains,
         cosine,
         sine,
         out_weight,
         query_weight,
         keyval_weight,
+        down_part,
     )
     if fits:
-        result, input_grad, gain_one_term, grad_branch, grad_linear = back(
+        result, input_grad, gain_one_term, _, grad_linear, out_grad, down_grad = back(
             lines, operands, (middle, result_parts.reshape(ctx_size, rows, width))
         )
     else:
-        input_grad, gain_one_term, grad_branch, grad_linear = back(lines, operands, ())
+        input_grad, gain_one_term, _, grad_linear, out_grad, down_grad = back(lines, operands, ())
         branch_two = lax.psum_scatter(result_parts, "ctx", scatter_dimension=0, tiled=True)
         result = (middle + branch_two.astype(f32)).astype(bf16)
-    gain_one_term = gain_one_term[0]
-
-    operands = (normed, mixed, grad_branch, grad_linear, down_part)
+
+    operands = (normed, grad_linear, gain_one_term, gain_two_term)
     if fits:
-        projection_grad, out_grad, down_grad, gate_up_part = weight_grads(
+        projection_grad, gain_grads, gate_up_part = weight_grads(
             lines, operands, (normed_two, grad_gate_up)
         )
     else:
-        projection_grad, out_grad, down_grad = weight_grads(lines, operands, ())
+        projection_grad, gain_grads = weight_grads(lines, operands, ())
         gate_up_part = lax.psum_scatter(
             contract_tokens(normed_two, grad_gate_up).astype(bf16),
             "fsdp",
@@ -1614,18 +1832,11 @@
         gate_up_part = lax.all_to_all(
             gate_up_part.reshape(ctx_size, width // ctx_size, -1), "ctx", 0, 0, tiled=True
         )
-    query_grad = projection_grad[:, : inner_width // fsdp_size].astype(f32)
-    keyval_grad = projection_grad[:, inner_width // fsdp_size :].astype(f32)
-    out_grad = out_grad.astype(f32)
-    down_grad = down_grad[:, :piece].reshape(fsdp_size * piece, -1).astype(f32)
-    gate_up_part = gate_up_part.reshape(ctx_size, width // ctx_size, 2, padded_piece)[..., :piece]
-    gate_up_grad = gate_up_part.transpose(1, 2, 0, 3).reshape(width // ctx_size, -1).astype(f32)
-    gains = lax.psum_scatter(
-        jnp.stack([gain_one_term, gain_two_term]),
-        ("ctx", "fsdp"),
-        scatter_dimension=1,
-        tiled=True,
+    query_grad, keyval_grad, out_grad, down_grad, gate_up_grad = assemble(
+        lines, piece, projection_grad, out_grad, down_grad, gate_up_part
     )
+    share = width // (ctx_size * fsdp_size)
+    gains = lax.dynamic_slice_in_dim(gain_grads, lax.axis_index("fsdp") * share, share, 1)
     return (
         result[None],
         input_grad[None],

time: 628 us -> 583 us (0.928)
  local copies, waits for them, and re-layouts: 38.7 us -> 4.4 us
  Pallas kernels: 551 us -> 569 us
  between operations: 14.6 us -> 0.88 us
  other arithmetic: 14.1 us -> 0.63 us
    pallas_call x1, Pallas kernels: 100 us -> 152 us  [back(): pl.pallas_call(functools.partial(back_kernel, lines, with_result), out_sh...]
    pallas_call x1, Pallas kernels: 187 us -> 148 us  [weight_grads(): pl.pallas_call(functools.partial(grads_kernel, lines, with_columns), out_...]
    convert_element_type x2 -> x0, local copies, waits for them, and re-layouts: 12.4 us -> none  [per_device(): gate_up_part.transpose(1, 2, 0, 3).reshape(width // ctx_size, -1)]
    unnamed x20 -> x6, local copies, waits for them, and re-layouts: 9.78 us -> 1.68 us
    convert_element_type x5 -> x0, other arithmetic: 7.96 us -> none  [the longest x1 1.95 us: per_device(): query_grad = projection_grad[:, :inner_width // fsdp_size].astype(f32)]
    pallas_call x0 -> x1, Pallas kernels: none -> 6.54 us  [assemble(): pl.pallas_call(functools.partial(assemble_kernel, lines, piece), grid=(st...]
  transfers between devices with their start and end apart: 1 -> 0, of which waited for: 0 -> 0; matrix products, arithmetic and copies ran while one was open for 4% -> 0% of each run, Pallas kernels for 30% -> 0%
where the time goes in v5:
time: 583 us; the launch traced here: 575 us
  Pallas kernels  569 us (98%)
    pallas_call x1, Pallas kernels, middle_part(): pl.pallas_call(functools.partial(middle_kernel, lines), out_shape=(shape(...  159 us
    pallas_call x1, Pallas kernels, back(): pl.pallas_call(functools.partial(back_kernel, lines, with_result), out_sh...  152 us
    pallas_call x1, Pallas kernels, weight_grads(): pl.pallas_call(functools.partial(grads_kernel, lines, with_columns), out_...  148 us
    pallas_call x1, Pallas kernels, front(): pl.pallas_call(functools.partial(front_kernel, lines), out_shape=(shape((...  105 us

profile of v5, /device:TPU:4, one launch (start us, length us, event | category | flops | bytes accessed | tf_op | source)
XLA Modules:
  0.0 575.2 jit_solution(8351822959249422778)
XLA Ops:
  0.6 0.7 stack.10
  1.4 0.7 stack.9
  2.1 0.6 pad_maximum_fusion.gains
  2.7 105.0 %front.1 = (bf16[4,128,640]{2,1,0:T(8,128)(2,1)}, bf16[10,128,256]{2,1,0:T(8,128)(2,1)}, bf16[8,128,512]{2,1,0:T(8,128)(2,1)}, bf16[10,128,1024]{2,1,0:T(8,128)(...) custom-call(s32[1,2]{1,0:T(1,128)} %bounds_ref.1, ...), custom_call_target="tpu_custom_call" | custom-call | tf_op jit(solution)/shard_map/front/pallas_call | solution.py:817
  107.7 158.5 %middle.1 = (f32[128,2560]{1,0:T(8,128)}, f32[1,2560]{1,0:T(1,128)}, bf16[4,256,2048]{2,1,0:T(8,128)(2,1)}, bf16[4,256,640]{2,1,0:T(8,128)(2,1)}, bf16[8,128,256...) custom-call(bf16[8,128,2560]{2,1,0:T(8,128)(2,1)} %get-tuple-element.41.cot_all, bf16[1024,2560]{1,0:T(8,128)(2,1)} %bitcast.9, ...), custom_call_target="tpu_custom_call" | custom-call | tf_op jit(solution)/shard_map/middle/pallas_call | solution.py:1085
  266.3 151.7 %back.1 = (bf16[128,2560]{1,0:T(8,128)(2,1)}, bf16[128,2560]{1,0:T(8,128)(2,1)}, f32[1,2560]{1,0:T(1,128)}, bf16[4,128,2560]{2,1,0:T(8,128)(2,1)}, bf16[4,128,30...) custom-call(f32[128,2560]{1,0:T(8,128)} %get-tuple-element.46.grad_middle, ...), custom_call_target="tpu_custom_call" | custom-call | tf_op jit(solution)/shard_map/back/pallas_call | solution.py:1375
  418.0 147.5 %grads.1 = (bf16[320,768]{1,0:T(8,128)(2,1)}, f32[8,384]{1,0:T(8,128)}, bf16[8,320,512]{2,1,0:T(8,128)(2,1)}) custom-call(bf16[4,128,640]{2,1,0:T(8,128)(2,1)} %get-tuple-element.57.normed, bf16[4,128,3072]{2,1,0:T(8,128)(2,1)} %get-tuple-element.58.linear_all, f32[1,2560]{1,0:T(1,128)} %get-tuple-element.59.gain_one, f32[1,2560]{1,0:T(1,128)} %get-tuple-element.60.gain_two, ...), custom_call_target="tpu_custom_call" | custom-call | tf_op jit(solution)/shard_map/grads/pallas_call | solution.py:1617
  565.5 0.0 copy-start.1
  565.5 0.0 copy-start
  565.5 6.5 %assemble.1 = (f32[320,640]{1,0:T(8,128)}, f32[320,128]{1,0:T(8,128)}, f32[320,640]{1,0:T(8,128)}, f32[960,640]{1,0:T(8,128)}, f32[320,3840]{1,0:T(8,128)}) custom-call(bf16[320,768]{1,0:T(8,128)(2,1)} %get-tuple-element.64.projection, bf16[320,640]{1,0:T(8,128)(2,1)} %get-tuple-element.65.out, bf16[4,256,640]{2,1,0:T(8,128)(2,1)} %get-tuple-element.66.down, ...), custom_call_target="tpu_custom_call" | custom-call | tf_op jit(solution)/shard_map/assemble/pallas_call | solution.py:1674
  572.1 0.8 constant_dynamic-slice_fusion
  572.8 0.5 slice_bitcast_fusion
  573.4 0.0 copy-done.1
  573.4 0.8 copy.21
  574.2 0.0 copy-done
  574.2 0.8 copy.22
Async XLA Ops:
  565.5 7.8 %copy-start.1 = (bf16[128,2560]{1,0:T(8,128)(2,1)S(1)}, bf16[128,2560]{1,0:T(8,128)(2,1)}, u32[]{:S(2)}) copy-start(bf16[128,2560]{1,0:T(8,128)(2,1)} %get-tuple-element.55) | copy-start | bytes 1966084
  565.5 8.7 %copy-start = (bf16[128,2560]{1,0:T(8,128)(2,1)S(1)}, bf16[128,2560]{1,0:T(8,128)(2,1)}, u32[]{:S(2)}) copy-start(bf16[128,2560]{1,0:T(8,128)(2,1)} %get-tuple-element.56) | copy-start | bytes 1966084

commit v6 on v5

--- a/solution.py
+++ b/solution.py
@@ -96,6 +96,23 @@
         pl.semaphore_wait(sem, count)
 
 
+class Fetch:
+    def __init__(self, pairs, sems):
+        self.copies = [
+            pltpu.make_async_copy(src, dst, sems.at[i]) for i, (src, dst) in enumerate(pairs)
+        ]
+        for copy in self.copies:
+            copy.start()
+
+    def wait(self, *which):
+        for i in which:
+            self.copies[i].wait()
+
+
+def held(operands):
+    return [VMEM(operand.shape, operand.dtype) for operand in operands]
+
+
 class LineGather:
     sems = 6
 
@@ -568,9 +585,9 @@
     bounds_ref,
     x_ref,
     gains,
-    w_keyval,
-    w_query,
-    w_out,
+    w_keyval_in,
+    w_query_in,
+    w_out_in,
     cot,
     w_down,
     w_gate_up,
@@ -597,6 +614,10 @@
     bias,
     w_rows,
     windows,
+    w_keyval,
+    w_query,
+    w_out,
+    fetch_sems,
     trade_sems,
     sum_sems,
     keyval_sems,
@@ -610,6 +631,9 @@
     heads = query_out.shape[0]
     inner = heads * HD
     kv_width = 2 * HD
+    fetch = Fetch(
+        ((w_keyval_in, w_keyval), (w_query_in, w_query), (w_out_in, w_out)), fetch_sems
+    )
     p.barrier()
 
     units = w_gate_up.shape[1] // 2
@@ -670,6 +694,14 @@
     cot_gather = LineGather(p, cot, cot_all, cot_sems)
     cot_local = pltpu.make_async_copy(cot, cot_all.at[p.c], own_sems.at[1])
 
+    def give(first, last):
+        for i in range(first, min(last, down.pieces)):
+            down.give(i)
+
+    def pass_on(first, last):
+        for i in range(first, min(last, down.pieces)):
+            down.pass_on(i)
+
     source = x_ref[...].astype(f32)
     whole[...] = rms_norm(source, gains[0:1]).astype(bf16)
     trade = GroupTrade(p, whole, slots.at[0], trade_sems.at[0], slots.shape[3])
@@ -686,6 +718,13 @@
         & (documents(query_at, bounds) == documents(key_at, bounds))
     )
     bias[...] = jnp.where(allowed, 0.0, -1e30)
+    rows_copy.wait()
+    if w_down.shape[0] != padded_piece and piece < padded_piece:
+        w_rows[pl.ds(piece, padded_piece - piece)] = jnp.zeros(
+            (padded_piece - piece, width), bf16
+        )
+    down.local().start()
+    give(0, 1)
     trade.wait()
     normed_out[...] = slots[0]
 
@@ -703,6 +742,7 @@
             parts[:, :, cols] = product.astype(bf16).reshape(4, rows, cols.size)
 
     spans = [pl.ds(first, count) for first, count in chunks]
+    fetch.wait(0, 1)
     project(slots.at[0], w_keyval, 0, kv_width, 0)
     group.give(0, spans[0])
     project(slots.at[0], w_query, 0, half, kv_width)
@@ -712,7 +752,6 @@
     group.give(2, spans[2])
     group.pass_on(1, spans[1])
     group.pass_on(2, spans[2])
-    cot_gather.step(0)
 
     linear = group.take(0, spans[0])
     keyval[p.c] = jnp.concatenate(
@@ -720,27 +759,22 @@
     ).astype(bf16)
     kv_gather = LineGather(p, keyval.at[p.c], keyval, keyval_sems)
     kv_gather.start()
-    for i in (1, 2):
+    kv_gather.step(0)
+
+    def take_queries(i):
         linear = group.take(i, spans[i])
         for h in range(linear.shape[1] // HD):
             turned = rotated(linear[:, h * HD : (h + 1) * HD], cosine[...], sine[...])
             at = h if i == 1 else h + heads // 2
             query_out[at] = (turned * HD**-0.5).astype(bf16)
-        if i == 1:
-            kv_gather.step(0)
-    rows_copy.wait()
-    if w_down.shape[0] != padded_piece and piece < padded_piece:
-        w_rows[pl.ds(piece, padded_piece - piece)] = jnp.zeros(
-            (padded_piece - piece, width), bf16
-        )
-    down.local().start()
-    for i in range(down.pieces):
-        down.give(i)
+
+    take_queries(1)
     for step in range(1, lines - 1):
         kv_gather.step(step)
+    cot_gather.step(0)
+    take_queries(2)
+    give(1, 4)
     kv_gather.finish()
-    if lines > 2:
-        cot_gather.step(1)
     keyval_out[...] = keyval[...]
 
 
@@ -765,12 +799,14 @@
     trade_two.start()
     for q in range(4):
         pack_columns(q)
-    for step in range(2, lines - 1):
-        cot_gather.step(step)
     for i in range(len(chunks)):
         group.finish(i, spans[i])
+    give(4, 6)
     trade_two.wait()
     mixed_out[...] = slots[1]
+    if lines > 2:
+        cot_gather.step(1)
+    fetch.wait(2)
 
     half = width // 2
     spans_two = [pl.ds(0, half), pl.ds(half, half)]
@@ -780,16 +816,19 @@
         group_two.give(i, spans_two[i])
     for i in range(2):
         group_two.pass_on(i, spans_two[i])
+    give(6, 8)
     for q in range(4, 8):
         pack_columns(q)
+    pass_on(0, 6)
+    for step in range(2, lines - 1):
+        cot_gather.step(step)
     for i in range(2):
         middle_out[:, spans_two[i]] = x_ref[:, spans_two[i]].astype(f32) + group_two.take(
             i, spans_two[i]
         )
     normed_two_out[...] = rms_norm(middle_out[...], gains[1:2]).astype(bf16)
 
-    for i in range(down.pieces):
-        down.pass_on(i)
+    pass_on(6, 8)
     for i in range(2):
         group_two.finish(i, spans_two[i])
     trade.finish()
@@ -812,7 +851,7 @@
     in_vmem = pl.BlockSpec(memory_space=VMEM)
     anywhere = pl.BlockSpec(memory_space=pl.ANY)
     shape = jax.ShapeDtypeStruct
-    pieces = 2
+    pieces = 8 if padded_piece % 128 == 0 else 1
     assert inner == width
     return pl.pallas_call(
         functools.partial(front_kernel, lines),
@@ -830,7 +869,7 @@
             shape((places, rows, width), bf16),
             shape((4, padded_piece, width), bf16),
         ),
-        in_specs=[pl.BlockSpec(memory_space=pltpu.SMEM)] + [in_vmem] * 5 + [anywhere] * 3,
+        in_specs=[pl.BlockSpec(memory_space=pltpu.SMEM)] + [in_vmem] * 2 + [anywhere] * 6,
         out_specs=[in_vmem] * 10 + [anywhere] * 2,
         scratch_shapes=[
             VMEM((rows, width), bf16),
@@ -844,6 +883,8 @@
             VMEM((rows, length), f32),
             VMEM((padded_piece, width), bf16),
             VMEM((2, shard, (padded_piece + 127) // 128 * 128 + 128), bf16),
+            *held(operands[3:6]),
+            DMA((3,)),
             DMA((2, GroupTrade.sems, 4)),
             DMA((2, GroupSum.sems, 3)),
             DMA((LineGather.sems, lines)),
@@ -877,9 +918,9 @@
 
 def middle_kernel(
     lines,
-    cot_all,
-    w_rows,
     gains,
+    cot_in,
+    w_rows_in,
     own,
     middle,
     w_columns,
@@ -899,6 +940,9 @@
     down_near,
     down_stage,
     down_far,
+    cot_all,
+    w_rows,
+    fetch_sems,
     gather_sems,
     column_sems,
     sum_sems,
@@ -911,6 +955,7 @@
     padded = hidden.shape[2]
     shard = width // 4
     tile = 256 if padded % 256 == 0 else 128
+    fetch = Fetch(((cot_in, cot_all), (w_rows_in, w_rows)), fetch_sems)
     p.barrier()
 
     columns = GroupGather(p, w_columns, weights, column_sems, own_sems.at[0], column_sems.shape[1])
@@ -934,6 +979,7 @@
 
         lax.fori_loop(0, padded // tile, one, 0)
 
+    fetch.wait(0, 1)
     done = 0
     for step in range(lines - 1):
         hidden_grad(done)
@@ -1026,10 +1072,8 @@
     for turn in range(lines):
         feed_forward(line_sum.order(turn))
         line_sum.across(turn).start()
-        if turn > 0:
-            line_sum.near(turn - 1, 0)
-        if turn > 1:
-            line_sum.far(turn - 2)
+        if turn == lines - 2:
+            line_sum.near(0, 0)
     normed_local.wait()
 
     for i in range(4):
@@ -1039,11 +1083,17 @@
             down_out[i - 2] = down_group(i - 2).take(i - 2, every, down_out[i - 2]).astype(bf16)
             down_group(i - 2).passed(i - 2, every)
         down_chunk(i)
+        down_group(i).pass_on(i, every)
+        if i < 2:
+            if i + 1 < lines - 1:
+                line_sum.near(i + 1, 0)
+            line_sum.far(i)
         if i < lines:
             result_part(i)
-        down_group(i).pass_on(i, every)
-        if i == 1:
-            line_sum.far(lines - 2)
+    for turn in range(2, lines - 1):
+        if turn > 2:
+            line_sum.near(turn, 0)
+        line_sum.far(turn)
     for line in range(4, lines):
         result_part(line)
     line_sum.near(lines - 1, 0)
@@ -1092,7 +1142,7 @@
             shape((places, rows, width), bf16),
             shape((places, rows, width), bf16),
         ),
-        in_specs=[in_vmem] * 3 + [anywhere] * 3,
+        in_specs=[in_vmem] + [anywhere] * 5,
         out_specs=[in_vmem] * 4 + [anywhere] * 2,
         scratch_shapes=[
             VMEM((places, rows, width), bf16),
@@ -1105,6 +1155,8 @@
             VMEM((4, 2, quarter, shard), bf16),
             VMEM((2, quarter, shard), bf16),
             VMEM((4, quarter, shard), bf16),
+            *held(operands[1:3]),
+            DMA((2,)),
             DMA((LineGather.sems, lines)),
             DMA((GroupGather.sems, pieces)),
             DMA((LineSum.sems, lines)),
@@ -1126,17 +1178,17 @@
     lines,
     with_result,
     grad_middle,
-    probs,
-    keyval,
-    queries,
-    mixed,
     tokens,
     gains,
     cosine,
     sine,
-    w_out,
-    w_query,
-    w_keyval,
+    w_out_in,
+    probs_in,
+    keyval_in,
+    queries_in,
+    mixed_in,
+    w_query_in,
+    w_keyval_in,
     down_in,
     *rest,
 ):
@@ -1163,14 +1215,19 @@
         out_parts,
         out_side,
         out_chain,
-        out_stage,
-        probs_stage,
+        w_out,
+        probs,
+        keyval,
+        queries,
+        mixed,
+        w_query,
+        w_keyval,
+        fetch_sems,
         branch_sems,
         linear_sems,
         trade_sems,
         kv_sems,
         out_sems,
-        move_sems,
         piece_sems,
         own_sems,
         *rest,
@@ -1178,14 +1235,23 @@
     p = Place(lines)
     rows, width = grad_middle.shape
     heads = queries.shape[0]
-    length = probs.shape[2]
+    length = probs_in.shape[2]
+    long = is_long(length)
+    operands = [
+        (w_out_in, w_out),
+        (keyval_in, keyval),
+        (queries_in, queries),
+        (mixed_in, mixed),
+        (w_query_in, w_query),
+        (w_keyval_in, w_keyval),
+    ]
+    fetch = Fetch(operands if long else operands + [(probs_in, probs)], fetch_sems)
     shard = w_out.shape[0]
     kv_width = 2 * HD
     per_owner = 2 * lines // 4
     tall = shard // per_owner
-    out_move = BlockMove(p, per_owner, out_stage, out_out, move_sems)
     others = [(jnp.full((), True), {"ctx": (p.c + d) % (2 * lines)}) for d in range(1, 2 * lines)]
-    p.barrier(ctx=False, also=others + out_move.greets())
+    p.barrier(ctx=False, also=others)
     if with_result:
         result_parts, result_side, result_chain, result_sems = rest
         result_sum = LineSum(p, result_parts, result_side, result_chain, result_sems)
@@ -1208,6 +1274,7 @@
         trade_parts[0, g] = contract_rows(branch_all[g], w_out[...]).astype(bf16)
 
     group.local().wait()
+    fetch.wait(0)
     mixed_back(p.f)
     back_trade.own().start()
     group.near(0)
@@ -1230,8 +1297,8 @@
             out_parts[4 * r + g] = product[r * tall : (r + 1) * tall].astype(bf16)
         return carry
 
+    fetch.wait(3)
     lax.fori_loop(0, 4, out_blocks, 0)
-    out_sum.start(2)
     if with_result:
         result_sum.near(0, 0)
     back_trade.wait()
@@ -1241,7 +1308,10 @@
     kv_total[...] = jnp.zeros_like(kv_total)
     kv_at, q_at = pl.ds(0, kv_width), pl.ds(kv_width, heads * HD)
 
-    batch = 1 if is_long(length) else 2
+    batch = 1 if long else 2
+    fetch.wait(1, 2)
+    if not long:
+        fetch.wait(6)
 
     def some_heads(i, carry):
         keys = keyval[:, :, :HD].reshape(length, HD)
@@ -1249,10 +1319,10 @@
         at = [pl.multiple_of((i * batch + h) * HD, 128) for h in range(batch)]
         outer = jnp.concatenate([grad_mixed[:, pl.ds(a, HD)] for a in at], axis=0)
         if batch == 1:
-            fetch = pltpu.make_async_copy(probs.at[i], probs_stage, own_sems.at[5])
-            fetch.start()
-            fetch.wait()
-            weights = probs_stage[...]
+            one = pltpu.make_async_copy(probs_in.at[i], probs, own_sems.at[5])
+            one.start()
+            one.wait()
+            weights = probs[...]
         else:
             weights = probs[pl.ds(batch * i, batch)].reshape(batch * rows, length)
         wide = weights.astype(f32)
@@ -1273,10 +1343,6 @@
         p, linear, linear_all, linear_sems, own_sems.at[1], 2, (q_at, kv_at)
     )
     linear_group.give(0)
-    if with_result:
-        result_sum.far(0)
-        result_sum.near(1, 0)
-    out_sum.near(0, 0)
     kv_parts[...] = kv_total[...].astype(bf16).reshape(kv_parts.shape)
     kv_sum = LineSum(p, kv_parts, kv_side, kv_chain, kv_sems)
     kv_sum.start(lines)
@@ -1289,12 +1355,10 @@
     if with_result:
         for turn in range(2, lines):
             result_sum.across(turn).start()
-        result_sum.far(1)
-    for turn in range(2, lines):
-        out_sum.across(turn).start()
-    out_sum.far(0)
-    out_sum.near(1, 0)
-    out_sum.far(1)
+        result_sum.near(1, 0)
+        result_sum.far(0)
+    out_sum.start(lines)
+    fetch.wait(4, 5)
     linear_group.pass_on(0)
     linear_group.pass_on(1)
     linear_group.local().wait()
@@ -1320,10 +1384,6 @@
     last_trade.send(3)
     normed_back(p.f)
     last_trade.own().start()
-    if with_result:
-        for turn in range(2, lines):
-            result_sum.near(turn, 0)
-            result_sum.far(turn)
     last_trade.wait()
     for g in range(4):
         grad_mixed[:, g * shard : (g + 1) * shard] = trade_slots[1, g]
@@ -1331,11 +1391,13 @@
     grad_values, gain = norm_back(source, gains[0:1], grad_mixed[...].astype(f32))
     input_grad_out[...] = (grad_middle[...] + grad_values).astype(bf16)
     gain_out[...] = gain
-    for turn in range(2, lines):
-        out_sum.near(turn, 0)
-        out_sum.far(turn)
-    out_stage[...] = out_sum.total().astype(bf16)
-    out_move.start()
+    if with_result:
+        result_sum.far(1)
+        for turn in range(2, lines):
+            result_sum.near(turn, 0)
+            result_sum.far(turn)
+    out_sum.turns(0)
+    out_out[...] = out_sum.total().astype(bf16)
     if with_result:
         result_out[...] = (middle[...] + result_sum.total()).astype(bf16)
         result_sum.finish()
@@ -1349,12 +1411,11 @@
     linear_copy.wait()
     out_sum.finish()
     down_move.finish()
-    out_move.finish()
 
 
 def back(lines, operands, result_operands):
     rows, width = operands[0].shape
-    heads = operands[3].shape[0]
+    heads = operands[8].shape[0]
     places = 2 * lines
     length = places * rows
     shard = width // 4
@@ -1366,6 +1427,9 @@
     shape = jax.ShapeDtypeStruct
     with_result = bool(result_operands)
     long = is_long(length)
+    scratch = held(operands[5:12])
+    if long:
+        scratch[1] = VMEM((rows, length), bf16)
     result_scratch = [
         VMEM((places, rows, width), bf16),
         VMEM((lines, rows, width), bf16),
@@ -1383,8 +1447,8 @@
             shape((tall, shard), bf16),
             shape(pieces, bf16),
         ),
-        in_specs=[in_vmem, anywhere if long else in_vmem] + [in_vmem] * 10 + [anywhere] + ([in_vmem, anywhere] if with_result else []),
-        out_specs=[in_vmem] * (3 if with_result else 2) + [anywhere] * 4,
+        in_specs=[in_vmem] * 5 + [anywhere] * 8 + ([in_vmem, anywhere] if with_result else []),
+        out_specs=[in_vmem] * (3 if with_result else 2) + [anywhere] * 2 + [in_vmem, anywhere],
         scratch_shapes=[
             VMEM((4, rows, width), bf16),
             VMEM((4, rows, linear_width), bf16),
@@ -1400,14 +1464,13 @@
             VMEM((places, tall, shard), bf16),
             VMEM((lines, tall, shard), bf16),
             VMEM((2, lines - 1, tall, shard), bf16),
-            VMEM((tall, shard), bf16),
-            VMEM((rows, length if long else 128), bf16),
+            *scratch,
+            DMA((7,)),
             DMA((GroupGather.sems, 1)),
             DMA((GroupGather.sems, 2)),
             DMA((2, GroupTrade.sems, 4)),
             DMA((LineSum.sems, lines)),
             DMA((LineSum.sems, lines)),
-            DMA((3,)),
             DMA((3, 4)),
             DMA((6,)),
         ]
@@ -1419,10 +1482,10 @@
     )(*operands, *result_operands)
 
 
-def grads_kernel(lines, with_columns, normed, linear_all, gain_one, gain_two, *rest):
+def grads_kernel(lines, with_columns, gain_one, gain_two, out_in, normed_in, linear_in, *rest):
     if with_columns:
-        normed_two, hidden_grads, *rest = rest
-    projection_out, gains_out, *rest = rest
+        normed_two_in, hidden_grads_in, *rest = rest
+    projection_out, gains_out, out_out, *rest = rest
     if with_columns:
         columns_out, *rest = rest
     (
@@ -1434,14 +1497,22 @@
         gain_side,
         gain_chain,
         gain_slots,
+        normed,
+        linear_all,
+        fetch_sems,
         projection_sems,
         gain_sems,
         slot_sems,
         move_sems,
+        out_move_sems,
         *rest,
     ) = rest
     if with_columns:
-        chunk_parts, near, passing, far, chunks, group_sems, trade_sems = rest
+        chunk_parts, near, passing, far, chunks, group_sems, trade_sems, normed_two, hidden_grads = rest
+    operands = [(normed_in, normed), (linear_in, linear_all)]
+    if with_columns:
+        operands += [(normed_two_in, normed_two), (hidden_grads_in, hidden_grads)]
+    fetch = Fetch(operands, fetch_sems)
     p = Place(lines)
     places = 2 * lines
     shard = normed.shape[2]
@@ -1452,6 +1523,8 @@
     move = BlockMove(p, per_owner, stage, projection_out, move_sems)
     others = [(jnp.full((), True), {"ctx": (p.c + d) % places}) for d in range(1, places)]
     p.barrier(ctx=False, also=others + move.greets())
+    out_move = BlockMove(p, per_owner, out_in, out_out, out_move_sems)
+    out_move.start()
 
     for c in range(places):
         cols = slice(c * tall, (c + 1) * tall)
@@ -1474,16 +1547,22 @@
             parts[4 * r + g, :, shard:] = kv_product[rows].astype(bf16)
         return carry
 
-    lax.fori_loop(0, 4, projection_blocks, 0)
-    projection_sum.start(2)
+    def start_projections():
+        fetch.wait(0, 1)
+        lax.fori_loop(0, 4, projection_blocks, 0)
+        projection_sum.start(2)
+
+    if not with_columns:
+        start_projections()
 
     if with_columns:
+        fetch.wait(2, 3)
         block = columns_out.shape[2]
         chunk = chunk_parts.shape[1]
         every = slice(None)
 
         def chunk_of(k):
-            return (p.line + k) % lines
+            return (p.line + (k + 1) % lines) % lines
 
         def group(k):
             return GroupSum(p, chunk_parts, near.at[k], passing.at[k % 2], far.at[k], group_sems)
@@ -1533,20 +1612,24 @@
         for k in range(lines):
             if k >= 1:
                 group(k - 1).given(k - 1, every)
+            compute(k)
             if k >= 2:
-                complete(k - 2)
                 group(k - 2).passed(k - 2, every)
-            compute(k)
             group(k).pass_on(k, every)
             if k == 0:
+                start_projections()
                 gain_sum.turns(0)
-            projection_sum.near(k, 2)
-            if k > 0:
-                projection_sum.far(k - 1)
+            if k >= 1:
+                complete(k - 1)
+                projection_sum.near(k - 1, 2)
+            if k >= 2:
+                projection_sum.far(k - 2)
+        complete(lines - 1)
         for k in (lines - 2, lines - 1):
-            complete(k)
             group(k).passed(k, every)
         group(lines - 1).given(lines - 1, every)
+        projection_sum.near(lines - 1, 2)
+        projection_sum.far(lines - 2)
         projection_sum.far(lines - 1)
     else:
         gain_sum.turns(0)
@@ -1586,11 +1669,12 @@
             pl.when(p.c != i)(lambda i=i: arrival(i).wait_recv())
     gain_sum.finish()
     projection_sum.finish()
+    out_move.finish()
     move.finish()
 
 
 def weight_grads(lines, operands, column_operands):
-    rows, shard = operands[0].shape[1:]
+    rows, shard = operands[3].shape[1:]
     width = 4 * shard
     places = 2 * lines
     tall = width // places
@@ -1613,12 +1697,13 @@
             VMEM((lines, chunk, block), bf16),
             DMA((GroupSum.sems, lines)),
             DMA((3, places)),
+            *held(column_operands),
         ]
     return pl.pallas_call(
         functools.partial(grads_kernel, lines, with_columns),
-        out_shape=(shape((tall, wide), bf16), shape((8, gain_wide), f32)) + column_shapes,
-        in_specs=[in_vmem] * (4 + len(column_operands)),
-        out_specs=[anywhere, in_vmem] + [anywhere] * len(column_shapes),
+        out_shape=(shape((tall, wide), bf16), shape((8, gain_wide), f32), shape((tall, shard), bf16)) + column_shapes,
+        in_specs=[in_vmem] * 2 + [anywhere] * (3 + len(column_operands)),
+        out_specs=[anywhere, in_vmem, anywhere] + [anywhere] * len(column_shapes),
         scratch_shapes=[
             VMEM((places, tall, wide), bf16),
             VMEM((lines, tall, wide), bf16),
@@ -1628,9 +1713,12 @@
             VMEM((lines, 8, gain_wide), f32),
             VMEM((2, lines - 1, 8, gain_wide), f32),
             VMEM((4, 8, gain_wide), f32),
+            *held(operands[3:5]),
+            DMA((4,)),
             DMA((LineSum.sems, lines)),
             DMA((LineSum.sems, lines)),
             DMA((2, 4)),
+            DMA((3,)),
             DMA((3,)),
         ]
         + column_scratch,
@@ -1763,7 +1851,7 @@
     fits = middle_bytes(lines, rows, width, padded) <= vmem_bytes
     if fits:
         grad_middle, gain_two_term, grad_gate_up, down_part, normed_two, result_parts = middle_part(
-            lines, (cot_all, w_down, gains, normed_two, middle, w_columns), padded
+            lines, (gains, cot_all, w_down, normed_two, middle, w_columns), padded
         )
     else:
         cot_all = cot_all.reshape(length, width)
@@ -1794,15 +1882,15 @@
         ).reshape(fsdp_size, padded_piece, -1)
     operands = (
         grad_middle,
-        weights,
-        window,
-        queries,
-        mixed,
         tokens[0],
         gains,
         cosine,
         sine,
         out_weight,
+        weights,
+        window,
+        queries,
+        mixed,
         query_weight,
         keyval_weight,
         down_part,
@@ -1816,13 +1904,13 @@
         branch_two = lax.psum_scatter(result_parts, "ctx", scatter_dimension=0, tiled=True)
         result = (middle + branch_two.astype(f32)).astype(bf16)
 
-    operands = (normed, grad_linear, gain_one_term, gain_two_term)
+    operands = (gain_one_term, gain_two_term, out_grad, normed, grad_linear)
     if fits:
-        projection_grad, gain_grads, gate_up_part = weight_grads(
+        projection_grad, gain_grads, out_grad, gate_up_part = weight_grads(
             lines, operands, (normed_two, grad_gate_up)
         )
     else:
-        projection_grad, gain_grads = weight_grads(lines, operands, ())
+        projection_grad, gain_grads, out_grad = weight_grads(lines, operands, ())
         gate_up_part = lax.psum_scatter(
             contract_tokens(normed_two, grad_gate_up).astype(bf16),
             "fsdp",

time: 583 us -> 529 us (0.907)
  Pallas kernels: 569 us -> 516 us
    pallas_call x1, Pallas kernels: 159 us -> 142 us  [middle_part(): pl.pallas_call(functools.partial(middle_kernel, lines), out_shape=(shape(...]
    pallas_call x1, Pallas kernels: 152 us -> 137 us  [back(): pl.pallas_call(functools.partial(back_kernel, lines, with_result), out_sh...]
    pallas_call x1, Pallas kernels: 105 us -> 92.5 us  [front(): pl.pallas_call(functools.partial(front_kernel, lines), out_shape=(shape((...]
    pallas_call x1, Pallas kernels: 148 us -> 138 us  [weight_grads(): pl.pallas_call(functools.partial(grads_kernel, lines, with_columns), out_...]
where the time goes in v6:
time: 529 us; the launch traced here: 521 us
  Pallas kernels  516 us (98%)
    pallas_call x1, Pallas kernels, middle_part(): pl.pallas_call(functools.partial(middle_kernel, lines), out_shape=(shape(...  142 us
    pallas_call x1, Pallas kernels, weight_grads(): pl.pallas_call(functools.partial(grads_kernel, lines, with_columns), out_...  138 us
    pallas_call x1, Pallas kernels, back(): pl.pallas_call(functools.partial(back_kernel, lines, with_result), out_sh...  137 us
    pallas_call x1, Pallas kernels, front(): pl.pallas_call(functools.partial(front_kernel, lines), out_shape=(shape((...  92.5 us

profile of v6, /device:TPU:4, one launch (start us, length us, event | category | flops | bytes accessed | tf_op | source)
XLA Modules:
  0.0 521.4 jit_solution(8422530840463529784)
XLA Ops:
  0.6 0.7 stack.10
  1.4 0.7 stack.9
  2.1 0.6 pad_maximum_fusion.gains
  2.7 92.5 %front.1 = (bf16[4,128,640]{2,1,0:T(8,128)(2,1)}, bf16[10,128,256]{2,1,0:T(8,128)(2,1)}, bf16[8,128,512]{2,1,0:T(8,128)(2,1)}, bf16[10,128,1024]{2,1,0:T(8,128)(...) custom-call(s32[1,2]{1,0:T(1,128)} %bounds_ref.1, ...), custom_call_target="tpu_custom_call" | custom-call | tf_op jit(solution)/shard_map/front/pallas_call | solution.py:856
  95.2 142.2 %middle.1 = (f32[128,2560]{1,0:T(8,128)}, f32[1,2560]{1,0:T(1,128)}, bf16[4,256,2048]{2,1,0:T(8,128)(2,1)}, bf16[4,256,640]{2,1,0:T(8,128)(2,1)}, bf16[8,128,256...) custom-call(f32[2,2560]{1,0:T(2,128)} %pad_maximum_fusion.gains, bf16[8,128,2560]{2,1,0:T(8,128)(2,1)} %get-tuple-element.42.cot_in, ...), custom_call_target="tpu_custom_call" | custom-call | tf_op jit(solution)/shard_map/middle/pallas_call | solution.py:1135
  237.4 136.5 %back.1 = (bf16[128,2560]{1,0:T(8,128)(2,1)}, bf16[128,2560]{1,0:T(8,128)(2,1)}, f32[1,2560]{1,0:T(1,128)}, bf16[4,128,2560]{2,1,0:T(8,128)(2,1)}, bf16[4,128,30...) custom-call(f32[128,2560]{1,0:T(8,128)} %get-tuple-element.47.grad_middle, ...), custom_call_target="tpu_custom_call" | custom-call | tf_op jit(solution)/shard_map/back/pallas_call | solution.py:1439
  373.9 137.8 %grads.1 = (bf16[320,768]{1,0:T(8,128)(2,1)}, f32[8,384]{1,0:T(8,128)}, bf16[320,640]{1,0:T(8,128)(2,1)}, bf16[8,320,512]{2,1,0:T(8,128)(2,1)}) custom-call(f32[1,2560]{1,0:T(1,128)} %get-tuple-element.58.gain_one, f32[1,2560]{1,0:T(1,128)} %get-tuple-element.59.gain_two, bf16[320,640]{1,0:T(8,128)(2,1)} %get-tuple-element.60.out_in, ...), custom_call_target="tpu_custom_call" | custom-call | tf_op jit(solution)/shard_map/grads/pallas_call | solution.py:1702
  511.7 0.0 copy-start.1
  511.7 0.0 copy-start
  511.7 6.5 %assemble.1 = (f32[320,640]{1,0:T(8,128)}, f32[320,128]{1,0:T(8,128)}, f32[320,640]{1,0:T(8,128)}, f32[960,640]{1,0:T(8,128)}, f32[320,3840]{1,0:T(8,128)}) custom-call(bf16[320,768]{1,0:T(8,128)(2,1)} %get-tuple-element.66.projection, bf16[320,640]{1,0:T(8,128)(2,1)} %get-tuple-element.67.out, bf16[4,256,640]{2,1,0:T(8,128)(2,1)} %get-tuple-element.68.down, ...), custom_call_target="tpu_custom_call" | custom-call | tf_op jit(solution)/shard_map/assemble/pallas_call | solution.py:1762
  518.3 0.8 constant_dynamic-slice_fusion
  519.0 0.5 slice_bitcast_fusion
  519.5 0.0 copy-done.1
  519.6 0.8 copy.21
  520.4 0.0 copy-done
  520.4 0.8 copy.22
Async XLA Ops:
  511.7 7.8 %copy-start.1 = (bf16[128,2560]{1,0:T(8,128)(2,1)S(1)}, bf16[128,2560]{1,0:T(8,128)(2,1)}, u32[]{:S(2)}) copy-start(bf16[128,2560]{1,0:T(8,128)(2,1)} %get-tuple-element.56) | copy-start | bytes 1966084
  511.7 8.7 %copy-start = (bf16[128,2560]{1,0:T(8,128)(2,1)S(1)}, bf16[128,2560]{1,0:T(8,128)(2,1)}, u32[]{:S(2)}) copy-start(bf16[128,2560]{1,0:T(8,128)(2,1)} %get-tuple-element.57) | copy-start | bytes 1966084

commit v7 on v6

--- a/solution.py
+++ b/solution.py
@@ -304,6 +304,29 @@
             pl.when(t < p.line)(lambda t=t: self.leftward(t).wait_send())
 
 
+class Turns:
+    def __init__(self, line_sum, ahead=2):
+        self.sum, self.ahead, self.nears, self.fars = line_sum, ahead, 0, 0
+
+    def start(self):
+        self.sum.start(self.ahead)
+
+    def near(self, upto):
+        while self.nears < min(upto, self.sum.p.lines):
+            self.sum.near(self.nears, self.ahead)
+            self.nears += 1
+
+    def far(self, upto):
+        while self.fars < min(upto, self.sum.p.lines):
+            self.near(self.fars + 1)
+            self.sum.far(self.fars)
+            self.fars += 1
+
+    def total(self):
+        self.far(self.sum.p.lines)
+        return self.sum.total()
+
+
 class GroupSum:
     sems = 6
 
@@ -397,38 +420,44 @@
             self.copy(d).wait_send()
 
 
-class BlockMove:
-    def __init__(self, place, per_owner, src, dst, sems):
-        p = place
-        self.src, self.dst, self.s = src, dst, sems
-        self.to_ctx, self.to_f = per_owner * p.f + p.c // 4, p.c % 4
-        self.from_ctx, self.from_f = 4 * (p.c % per_owner) + p.f, p.c // per_owner
-        self.moves = (self.to_ctx != p.c) | (self.to_f != p.f)
-
-    def greets(self):
-        return [
-            (self.moves, {"ctx": self.to_ctx, "fsdp": self.to_f}),
-            (self.moves, {"ctx": self.from_ctx, "fsdp": self.from_f}),
-        ]
-
-    def copy(self):
-        device = {"ctx": self.to_ctx, "fsdp": self.to_f}
-        return remote(self.src, self.dst, self.s.at[0], self.s.at[1], device)
-
-    def stay(self):
-        return pltpu.make_async_copy(self.src, self.dst, self.s.at[2])
-
-    def start(self):
-        pl.when(self.moves)(lambda: self.copy().start())
-        pl.when(~self.moves)(lambda: self.stay().start())
-
-    def finish(self):
-        @pl.when(self.moves)
-        def _():
-            self.copy().wait_send()
-            self.copy().wait_recv()
-
-        pl.when(~self.moves)(lambda: self.stay().wait())
+class GroupScatter:
+    sems = 4
+
+    def __init__(self, place, per_owner, stage, slots, sems):
+        self.p, self.half, self.stage, self.slots, self.s = place, per_owner // 2, stage, slots, sems
+        self.places = (place.twin_f, place.cross_f, place.diag_f)
+        self.devices = (place.twin, place.cross, place.diag)
+
+    def slot(self, f, half):
+        return self.slots.at[pl.ds((2 * f + half) * self.half, self.half)]
+
+    def own(self):
+        return self.slots.at[pl.ds(2 * self.p.f * self.half, 2 * self.half)]
+
+    def copy(self, kind, half):
+        return remote(
+            self.stage.at[kind, pl.ds(half * self.half, self.half)],
+            self.slot(self.p.f, half),
+            self.s.at[half, kind],
+            self.s.at[2 + half, kind],
+            self.devices[kind],
+        )
+
+    def arrived(self, kind):
+        for half in range(2):
+            slot = self.slot(self.places[kind], half)
+            remote(
+                slot, slot, self.s.at[half, kind], self.s.at[2 + half, kind], self.devices[kind]
+            ).wait_recv()
+
+    def send(self, kind):
+        for half in range(2):
+            self.copy(kind, half).start()
+
+    def sent(self):
+        for kind in range(3):
+            for half in range(2):
+                self.copy(kind, half).wait_send()
 
 
 class PieceMove:
@@ -754,12 +783,15 @@
     group.pass_on(2, spans[2])
 
     linear = group.take(0, spans[0])
-    keyval[p.c] = jnp.concatenate(
-        [rotated(linear[:, :HD], cosine[...], sine[...]), linear[:, HD:]], axis=1
-    ).astype(bf16)
-    kv_gather = LineGather(p, keyval.at[p.c], keyval, keyval_sems)
-    kv_gather.start()
-    kv_gather.step(0)
+    keyval[0, p.c] = rotated(linear[:, :HD], cosine[...], sine[...]).astype(bf16)
+    keyval[1, p.c] = linear[:, HD:].astype(bf16)
+    kv_gathers = [
+        LineGather(p, keyval.at[i, p.c], keyval.at[i], keyval_sems.at[i]) for i in range(2)
+    ]
+    for gather in kv_gathers:
+        gather.start()
+    for gather in kv_gathers:
+        gather.step(0)
 
     def take_queries(i):
         linear = group.take(i, spans[i])
@@ -768,19 +800,21 @@
             at = h if i == 1 else h + heads // 2
             query_out[at] = (turned * HD**-0.5).astype(bf16)
 
+    give(1, 5)
     take_queries(1)
     for step in range(1, lines - 1):
-        kv_gather.step(step)
+        for gather in kv_gathers:
+            gather.step(step)
     cot_gather.step(0)
     take_queries(2)
-    give(1, 4)
-    kv_gather.finish()
+    for gather in kv_gathers:
+        gather.finish()
     keyval_out[...] = keyval[...]
 
 
     def two_heads(i, carry):
-        keys = keyval[:, :, :HD].reshape(length, HD)
-        values = keyval[:, :, HD:].reshape(length, HD)
+        keys = keyval[0].reshape(length, HD)
+        values = keyval[1].reshape(length, HD)
         two = query_out[pl.ds(2 * i, 2)].reshape(2 * rows, HD)
         scores = contract_rows(two, keys).reshape(2, rows, length) + bias[...][None]
         scores = scores.reshape(2 * rows, length)
@@ -797,15 +831,15 @@
     lax.fori_loop(0, heads // 2, two_heads, 0)
     trade_two = GroupTrade(p, mixed, slots.at[1], trade_sems.at[1], slots.shape[3])
     trade_two.start()
+    give(5, 7)
     for q in range(4):
         pack_columns(q)
+    if lines > 2:
+        cot_gather.step(1)
     for i in range(len(chunks)):
         group.finish(i, spans[i])
-    give(4, 6)
     trade_two.wait()
     mixed_out[...] = slots[1]
-    if lines > 2:
-        cot_gather.step(1)
     fetch.wait(2)
 
     half = width // 2
@@ -816,10 +850,10 @@
         group_two.give(i, spans_two[i])
     for i in range(2):
         group_two.pass_on(i, spans_two[i])
-    give(6, 8)
+    give(7, 8)
     for q in range(4, 8):
         pack_columns(q)
-    pass_on(0, 6)
+    pass_on(0, 7)
     for step in range(2, lines - 1):
         cot_gather.step(step)
     for i in range(2):
@@ -828,7 +862,7 @@
         )
     normed_two_out[...] = rms_norm(middle_out[...], gains[1:2]).astype(bf16)
 
-    pass_on(6, 8)
+    pass_on(7, 8)
     for i in range(2):
         group_two.finish(i, spans_two[i])
     trade.finish()
@@ -858,7 +892,7 @@
         out_shape=(
             shape((4, rows, shard), bf16),
             shape((heads, rows, HD), bf16),
-            shape((places, rows, 2 * HD), bf16),
+            shape((2, places, rows, HD), bf16),
             shape((heads, rows, length), bf16),
             shape((4, rows, shard), bf16),
             shape((rows, width), f32),
@@ -878,7 +912,7 @@
             VMEM((2, rows, parts_width), bf16),
             VMEM((rows, parts_width), bf16),
             VMEM((rows, parts_width), bf16),
-            VMEM((places, rows, 2 * HD), bf16),
+            VMEM((2, places, rows, HD), bf16),
             VMEM((rows, inner), bf16),
             VMEM((rows, length), f32),
             VMEM((padded_piece, width), bf16),
@@ -887,7 +921,7 @@
             DMA((3,)),
             DMA((2, GroupTrade.sems, 4)),
             DMA((2, GroupSum.sems, 3)),
-            DMA((LineGather.sems, lines)),
+            DMA((2, LineGather.sems, lines)),
             DMA((LineGather.sems, lines)),
             DMA((GroupGather.sems, pieces)),
             DMA((5,)),
@@ -1000,7 +1034,17 @@
     normed_local = pltpu.make_async_copy(normed_all, normed_all_out, own_sems.at[1])
     normed_local.start()
 
-    line_sum = LineSum(p, parts, side, chain, sum_sems)
+    line_sums = [
+        LineSum(p, parts.at[i], side.at[i], chain.at[i], sum_sems.at[i]) for i in range(2)
+    ]
+
+    def near(turn):
+        for line_sum in line_sums:
+            line_sum.near(turn, 0)
+
+    def far(turn):
+        for line_sum in line_sums:
+            line_sum.far(turn)
 
     def feed_forward(line):
         def one(i, carry):
@@ -1024,8 +1068,8 @@
 
         def back(g, carry):
             product = contract_rows(grads_out[line], weights[g]).astype(bf16)
-            cols = pl.ds(pl.multiple_of(g * shard, 128), shard)
-            parts[pl.ds(2 * line, 2), :, cols] = product.reshape(2, rows, shard)
+            cols = pl.ds(pl.multiple_of(g % 2 * shard, 128), shard)
+            parts[g // 2, pl.ds(2 * line, 2), :, cols] = product.reshape(2, rows, shard)
             return carry
 
         lax.fori_loop(0, 4, back, 0)
@@ -1070,46 +1114,50 @@
         down_group(i).give(i, every)
 
     for turn in range(lines):
-        feed_forward(line_sum.order(turn))
-        line_sum.across(turn).start()
+        feed_forward(line_sums[0].order(turn))
+        for line_sum in line_sums:
+            line_sum.across(turn).start()
         if turn == lines - 2:
-            line_sum.near(0, 0)
+            near(0)
     normed_local.wait()
 
     for i in range(4):
         if i >= 1:
             down_group(i - 1).given(i - 1, every)
         if i >= 2:
-            down_out[i - 2] = down_group(i - 2).take(i - 2, every, down_out[i - 2]).astype(bf16)
             down_group(i - 2).passed(i - 2, every)
         down_chunk(i)
         down_group(i).pass_on(i, every)
-        if i < 2:
-            if i + 1 < lines - 1:
-                line_sum.near(i + 1, 0)
-            line_sum.far(i)
-        if i < lines:
-            result_part(i)
-    for turn in range(2, lines - 1):
-        if turn > 2:
-            line_sum.near(turn, 0)
-        line_sum.far(turn)
-    for line in range(4, lines):
+        if i == 1:
+            if lines > 2:
+                near(1)
+            far(0)
+        if i == 2 and lines > 3:
+            near(2)
+            far(1)
+            far(2)
+    for line in range(lines):
         result_part(line)
-    line_sum.near(lines - 1, 0)
-    line_sum.far(lines - 1)
-    grad = line_sum.total()
+    for turn in range(3, lines - 1):
+        near(turn)
+        far(turn)
+    near(lines - 1)
+    far(lines - 1)
+    grad = jnp.concatenate([line_sum.total() for line_sum in line_sums], axis=1)
     middle_local.wait()
     grad_values, gain = norm_back(grad_middle_out[...], gains[1:2], grad)
     grad_middle_out[...] = cot_all[p.c].astype(f32) + grad_values
     gain_out[...] = gain
+    for i in range(2):
+        down_out[i] = down_group(i).take(i, every, down_out[i]).astype(bf16)
     for i in (2, 3):
         down_out[i] = down_group(i).take(i, every, down_out[i]).astype(bf16)
         down_group(i).passed(i, every)
     down_group(3).given(3, every)
     for line in range(lines):
         result_copy(line).wait()
-    line_sum.finish()
+    for line_sum in line_sums:
+        line_sum.finish()
 
 
 def middle_bytes(lines, rows, width, padded):
@@ -1149,9 +1197,9 @@
             VMEM((4, shard, 2 * padded), bf16),
             VMEM((lines, 2 * rows, padded), f32),
             VMEM((lines, 2 * rows, padded), bf16),
-            VMEM((places, rows, width), bf16),
-            VMEM((lines, rows, width), bf16),
-            VMEM((2, lines - 1, rows, width), bf16),
+            VMEM((2, places, rows, width // 2), bf16),
+            VMEM((2, lines, rows, width // 2), bf16),
+            VMEM((2, 2, lines - 1, rows, width // 2), bf16),
             VMEM((4, 2, quarter, shard), bf16),
             VMEM((2, quarter, shard), bf16),
             VMEM((4, quarter, shard), bf16),
@@ -1159,7 +1207,7 @@
             DMA((2,)),
             DMA((LineGather.sems, lines)),
             DMA((GroupGather.sems, pieces)),
-            DMA((LineSum.sems, lines)),
+            DMA((2, LineSum.sems, lines)),
             DMA((GroupSum.sems, 4)),
             DMA((4 + lines,)),
         ],
@@ -1197,9 +1245,8 @@
     (
         input_grad_out,
         gain_out,
-        branch_out,
         linear_out,
-        out_out,
+        out_slots,
         down_out,
         branch_all,
         linear_all,
@@ -1212,9 +1259,7 @@
         kv_parts,
         kv_side,
         kv_chain,
-        out_parts,
-        out_side,
-        out_chain,
+        out_stage,
         w_out,
         probs,
         keyval,
@@ -1249,14 +1294,32 @@
     shard = w_out.shape[0]
     kv_width = 2 * HD
     per_owner = 2 * lines // 4
-    tall = shard // per_owner
     others = [(jnp.full((), True), {"ctx": (p.c + d) % (2 * lines)}) for d in range(1, 2 * lines)]
     p.barrier(ctx=False, also=others)
     if with_result:
         result_parts, result_side, result_chain, result_sems = rest
-        result_sum = LineSum(p, result_parts, result_side, result_chain, result_sems)
-        result_copy = pltpu.make_async_copy(result_in, result_parts, own_sems.at[2])
-        result_copy.start()
+        result_sum = Turns(
+            LineSum(p, result_parts, result_side, result_chain, result_sems), lines
+        )
+        half = width // 2
+        result_copies = [
+            pltpu.make_async_copy(
+                result_in.at[:, :, pl.ds(i * half, half)], result_parts.at[i], own_sems.at[2 + i]
+            )
+            for i in range(2)
+        ]
+        for copy in result_copies:
+            copy.start()
+        result_sums = [
+            Turns(
+                LineSum(
+                    p, result_parts.at[i], result_side.at[i], result_chain.at[i], result_sems.at[i]
+                ),
+                lines,
+            )
+            for i in range(2)
+        ]
+    out_scatter = GroupScatter(p, per_owner, out_stage, out_slots, out_sems)
 
     branch[...] = grad_middle[...].astype(bf16)
     group = GroupGather(p, branch, branch_all, branch_sems, own_sems.at[0], 1)
@@ -1264,10 +1327,9 @@
     group.local().start()
     down_move = PieceMove(p, per_owner, down_in, down_out, piece_sems)
     down_move.start()
-    out_sum = LineSum(p, out_parts, out_side, out_chain, out_sems)
     if with_result:
-        result_copy.wait()
-        result_sum.start(2)
+        result_copies[0].wait()
+        result_sums[0].start()
     back_trade = GroupReturn(p, trade_parts.at[0], trade_slots.at[0], trade_sems.at[0])
 
     def mixed_back(g):
@@ -1286,21 +1348,24 @@
     mixed_back(p.diag_f)
     back_trade.send(1)
     back_trade.send(3)
-    branch_copy = pltpu.make_async_copy(branch_all, branch_out, own_sems.at[3])
-    branch_copy.start()
-
-    def out_blocks(g, carry):
+
+    def out_block(i, g):
         left = mixed[...].reshape(4 * rows, shard)
         right = branch_all[:, :, pl.ds(pl.multiple_of(g * shard, 128), shard)]
-        product = contract_tokens(left, right.reshape(4 * rows, shard))
-        for r in range(per_owner):
-            out_parts[4 * r + g] = product[r * tall : (r + 1) * tall].astype(bf16)
-        return carry
+        product = contract_tokens(left, right.reshape(4 * rows, shard)).astype(bf16)
+        out_stage[i] = product.reshape(out_stage.shape[1:])
 
     fetch.wait(3)
-    lax.fori_loop(0, 4, out_blocks, 0)
+    out_block(1, p.cross_f)
+    out_scatter.copy(1, 0).start()
+    out_block(0, p.twin_f)
+    out_scatter.send(0)
+    out_block(2, p.diag_f)
+    out_block(3, p.f)
+    out_own = pltpu.make_async_copy(out_stage.at[3], out_scatter.own(), own_sems.at[7])
+    out_own.start()
     if with_result:
-        result_sum.near(0, 0)
+        result_sums[0].near(2)
     back_trade.wait()
     for g in range(4):
         grad_mixed[:, g * shard : (g + 1) * shard] = trade_slots[0, g]
@@ -1314,8 +1379,8 @@
         fetch.wait(6)
 
     def some_heads(i, carry):
-        keys = keyval[:, :, :HD].reshape(length, HD)
-        values = keyval[:, :, HD:].reshape(length, HD)
+        keys = keyval[0].reshape(length, HD)
+        values = keyval[1].reshape(length, HD)
         at = [pl.multiple_of((i * batch + h) * HD, 128) for h in range(batch)]
         outer = jnp.concatenate([grad_mixed[:, pl.ds(a, HD)] for a in at], axis=0)
         if batch == 1:
@@ -1346,18 +1411,21 @@
     kv_parts[...] = kv_total[...].astype(bf16).reshape(kv_parts.shape)
     kv_sum = LineSum(p, kv_parts, kv_side, kv_chain, kv_sems)
     kv_sum.start(lines)
+    if with_result:
+        result_copies[1].wait()
+        result_sums[1].start()
+        result_sums[0].near(lines)
+        result_sums[0].far(1)
     kv_sum.turns(0)
     own = kv_sum.total()
     linear[:, :HD] = rotated(own[:, :HD], cosine[...], -sine[...]).astype(bf16)
     linear[:, pl.ds(HD, HD)] = own[:, HD:].astype(bf16)
     linear_group.give(1)
+    out_scatter.copy(1, 1).start()
     linear_group.local().start()
     if with_result:
-        for turn in range(2, lines):
-            result_sum.across(turn).start()
-        result_sum.near(1, 0)
-        result_sum.far(0)
-    out_sum.start(lines)
+        result_sums[0].far(2)
+        result_sums[1].near(2)
     fetch.wait(4, 5)
     linear_group.pass_on(0)
     linear_group.pass_on(1)
@@ -1382,8 +1450,12 @@
     normed_back(p.twin_f)
     last_trade.send(1)
     last_trade.send(3)
+    out_scatter.send(2)
     normed_back(p.f)
     last_trade.own().start()
+    if with_result:
+        result_sums[0].far(3)
+        result_sums[1].far(2)
     last_trade.wait()
     for g in range(4):
         grad_mixed[:, g * shard : (g + 1) * shard] = trade_slots[1, g]
@@ -1392,24 +1464,21 @@
     input_grad_out[...] = (grad_middle[...] + grad_values).astype(bf16)
     gain_out[...] = gain
     if with_result:
-        result_sum.far(1)
-        for turn in range(2, lines):
-            result_sum.near(turn, 0)
-            result_sum.far(turn)
-    out_sum.turns(0)
-    out_out[...] = out_sum.total().astype(bf16)
-    if with_result:
-        result_out[...] = (middle[...] + result_sum.total()).astype(bf16)
-        result_sum.finish()
+        for i in range(2):
+            cols = pl.ds(i * half, half)
+            result_out[:, cols] = (middle[:, cols] + result_sums[i].total()).astype(bf16)
+            result_sums[i].sum.finish()
     back_trade.finish()
     last_trade.finish()
     group.sent(0)
     linear_group.sent(0)
     linear_group.sent(1)
     kv_sum.finish()
-    branch_copy.wait()
+    out_own.wait()
+    for kind in range(3):
+        out_scatter.arrived(kind)
+    out_scatter.sent()
     linear_copy.wait()
-    out_sum.finish()
     down_move.finish()
 
 
@@ -1431,10 +1500,10 @@
     if long:
         scratch[1] = VMEM((rows, length), bf16)
     result_scratch = [
-        VMEM((places, rows, width), bf16),
-        VMEM((lines, rows, width), bf16),
-        VMEM((2, lines - 1, rows, width), bf16),
-        DMA((LineSum.sems, lines)),
+        VMEM((2, places, rows, width // 2), bf16),
+        VMEM((2, lines, rows, width // 2), bf16),
+        VMEM((2, 2, lines - 1, rows, width // 2), bf16),
+        DMA((2, LineSum.sems, lines)),
     ]
     return pl.pallas_call(
         functools.partial(back_kernel, lines, with_result),
@@ -1442,13 +1511,12 @@
         + (
             shape((rows, width), bf16),
             shape((1, width), f32),
-            shape((4, rows, width), bf16),
             shape((4, rows, linear_width), bf16),
-            shape((tall, shard), bf16),
+            shape((places, tall, shard), bf16),
             shape(pieces, bf16),
         ),
         in_specs=[in_vmem] * 5 + [anywhere] * 8 + ([in_vmem, anywhere] if with_result else []),
-        out_specs=[in_vmem] * (3 if with_result else 2) + [anywhere] * 2 + [in_vmem, anywhere],
+        out_specs=[in_vmem] * (3 if with_result else 2) + [anywhere] * 3,
         scratch_shapes=[
             VMEM((4, rows, width), bf16),
             VMEM((4, rows, linear_width), bf16),
@@ -1461,18 +1529,16 @@
             VMEM((places, rows, 2 * HD), bf16),
             VMEM((lines, rows, 2 * HD), bf16),
             VMEM((2, lines - 1, rows, 2 * HD), bf16),
-            VMEM((places, tall, shard), bf16),
-            VMEM((lines, tall, shard), bf16),
-            VMEM((2, lines - 1, tall, shard), bf16),
+            VMEM((4, places // 4, tall, shard), bf16),
             *scratch,
             DMA((7,)),
             DMA((GroupGather.sems, 1)),
             DMA((GroupGather.sems, 2)),
             DMA((2, GroupTrade.sems, 4)),
             DMA((LineSum.sems, lines)),
-            DMA((LineSum.sems, lines)),
+            DMA((GroupScatter.sems, 3)),
             DMA((3, 4)),
-            DMA((6,)),
+            DMA((8,)),
         ]
         + (result_scratch if with_result else []),
         compiler_params=pltpu.CompilerParams(
@@ -1493,6 +1559,9 @@
         side,
         chain,
         stage,
+        out_parts,
+        out_side,
+        out_chain,
         gain_parts,
         gain_side,
         gain_chain,
@@ -1501,30 +1570,38 @@
         linear_all,
         fetch_sems,
         projection_sems,
+        out_sems,
         gain_sems,
         slot_sems,
-        move_sems,
-        out_move_sems,
+        scatter_sems,
         *rest,
     ) = rest
+    p = Place(lines)
+    operands = [(out_in, out_parts)]
     if with_columns:
-        chunk_parts, near, passing, far, chunks, group_sems, trade_sems, normed_two, hidden_grads = rest
-    operands = [(normed_in, normed), (linear_in, linear_all)]
+        (
+            chunk_parts,
+            near,
+            passing,
+            far,
+            chunks,
+            group_sems,
+            trade_sems,
+            normed_two,
+            hidden_grads,
+        ) = rest
     if with_columns:
         operands += [(normed_two_in, normed_two), (hidden_grads_in, hidden_grads)]
+    operands += [(normed_in, normed), (linear_in, linear_all)]
     fetch = Fetch(operands, fetch_sems)
-    p = Place(lines)
     places = 2 * lines
     shard = normed.shape[2]
     tokens = 4 * normed.shape[1]
     per_owner = places // 4
     tall = shard // per_owner
     kv_share = 2 * HD // 4
-    move = BlockMove(p, per_owner, stage, projection_out, move_sems)
     others = [(jnp.full((), True), {"ctx": (p.c + d) % places}) for d in range(1, places)]
-    p.barrier(ctx=False, also=others + move.greets())
-    out_move = BlockMove(p, per_owner, out_in, out_out, out_move_sems)
-    out_move.start()
+    p.barrier(ctx=False, also=others)
 
     for c in range(places):
         cols = slice(c * tall, (c + 1) * tall)
@@ -1533,36 +1610,23 @@
     gain_sum = LineSum(p, gain_parts, gain_side, gain_chain, gain_sems)
     gain_sum.start(lines)
 
-    projection_sum = LineSum(p, parts, side, chain, projection_sems)
-
-    def projection_blocks(g, carry):
-        left = normed[...].reshape(tokens, shard)
-        right = linear_all[:, :, pl.ds(pl.multiple_of(2 * HD + g * shard, 128), shard)]
-        product = contract_tokens(left, right.reshape(tokens, shard))
-        right = linear_all[:, :, pl.ds(pl.multiple_of(g * kv_share, 128), kv_share)]
-        kv_product = contract_tokens(left, right.reshape(tokens, kv_share))
-        for r in range(per_owner):
-            rows = slice(r * tall, (r + 1) * tall)
-            parts[4 * r + g, :, :shard] = product[rows].astype(bf16)
-            parts[4 * r + g, :, shard:] = kv_product[rows].astype(bf16)
-        return carry
-
-    def start_projections():
-        fetch.wait(0, 1)
-        lax.fori_loop(0, 4, projection_blocks, 0)
-        projection_sum.start(2)
-
-    if not with_columns:
-        start_projections()
+    projection_sums = [
+        Turns(LineSum(p, parts.at[i], side.at[i], chain.at[i], projection_sems.at[i]))
+        for i in range(2)
+    ]
+    out_sum = Turns(LineSum(p, out_parts, out_side, out_chain, out_sems))
+    fetch.wait(0)
+    out_sum.start()
 
     if with_columns:
-        fetch.wait(2, 3)
+        fetch.wait(1, 2)
         block = columns_out.shape[2]
         chunk = chunk_parts.shape[1]
         every = slice(None)
 
         def chunk_of(k):
-            return (p.line + (k + 1) % lines) % lines
+            order = sorted(range(lines), key=lambda d: (d == 0, abs(d - lines // 2), d))
+            return (p.line + order[k]) % lines
 
         def group(k):
             return GroupSum(p, chunk_parts, near.at[k], passing.at[k % 2], far.at[k], group_sems)
@@ -1609,31 +1673,79 @@
                 )
                 pl.when(dest == p.c)(lambda src=src: place_own(src).start())
 
-        for k in range(lines):
+        def chunk_step(k):
             if k >= 1:
                 group(k - 1).given(k - 1, every)
             compute(k)
             if k >= 2:
                 group(k - 2).passed(k - 2, every)
             group(k).pass_on(k, every)
-            if k == 0:
-                start_projections()
-                gain_sum.turns(0)
-            if k >= 1:
-                complete(k - 1)
-                projection_sum.near(k - 1, 2)
-            if k >= 2:
-                projection_sum.far(k - 2)
-        complete(lines - 1)
+
+        chunk_step(0)
+
+    scatters = [
+        GroupScatter(p, per_owner, stage.at[i], parts.at[i], scatter_sems.at[i]) for i in range(2)
+    ]
+
+    def projection_block(first, second, g):
+        left = normed[...].reshape(tokens, shard)
+        right = linear_all[:, :, pl.ds(pl.multiple_of(2 * HD + g * shard, 128), shard)]
+        product = contract_tokens(left, right.reshape(tokens, shard)).astype(bf16)
+        right = linear_all[:, :, pl.ds(pl.multiple_of(g * kv_share, 128), kv_share)]
+        kv_product = contract_tokens(left, right.reshape(tokens, kv_share)).astype(bf16)
+        first[...] = product[:, :half].reshape(per_owner, tall, half)
+        if half < shard:
+            kv_product = jnp.concatenate([product[:, half:], kv_product], axis=1)
+        second[...] = kv_product.reshape(per_owner, tall, half)
+
+    half = (shard + kv_share) // 2
+    fetch.wait(*((3, 4) if with_columns else (1, 2)))
+    for kind in (1, 2, 0):
+        projection_block(stage.at[0, kind], stage.at[1, kind], scatters[0].places[kind])
+        scatters[0].send(kind)
+    for kind in (1, 2, 0):
+        scatters[1].send(kind)
+    projection_block(scatters[0].own(), scatters[1].own(), p.f)
+
+    first, second = projection_sums
+    if with_columns:
+        chunk_step(1)
+    out_sum.near(2)
+    out_sum.far(1)
+    if with_columns:
+        complete(0)
+        if lines > 2:
+            chunk_step(2)
+    out_sum.near(lines)
+    for k in range(lines):
+        gain_sum.near(k, 0)
+    for kind in range(3):
+        scatters[0].arrived(kind)
+    first.start()
+    out_sum.far(2)
+    first.near(2)
+    out_sum.far(3)
+    first.near(lines)
+    for kind in range(3):
+        scatters[1].arrived(kind)
+    second.start()
+    first.far(1)
+    for k in range(lines):
+        gain_sum.far(k)
+    out_out[...] = out_sum.total().astype(bf16)
+    first.far(2)
+    if with_columns:
+        for k in range(1, lines):
+            second.near(k)
+            complete(k)
+            if k + 2 < lines:
+                chunk_step(k + 2)
+            first.far(k + 2)
+            second.near(k + 1)
+            second.far(k)
         for k in (lines - 2, lines - 1):
             group(k).passed(k, every)
         group(lines - 1).given(lines - 1, every)
-        projection_sum.near(lines - 1, 2)
-        projection_sum.far(lines - 2)
-        projection_sum.far(lines - 1)
-    else:
-        gain_sum.turns(0)
-        projection_sum.turns(2)
 
     own = gain_sum.total()
     gain_parts[p.c] = own
@@ -1649,8 +1761,8 @@
 
     for d in (1, 2, 3):
         gain_copy(d).start()
-    stage[...] = projection_sum.total().astype(bf16)
-    move.start()
+    for i in range(2):
+        projection_out[:, i * half : (i + 1) * half] = projection_sums[i].total().astype(bf16)
     for d in (1, 2, 3):
         gain_copy(d).wait_recv()
         own = own + gain_slots[d]
@@ -1668,9 +1780,11 @@
         for i in range(places):
             pl.when(p.c != i)(lambda i=i: arrival(i).wait_recv())
     gain_sum.finish()
-    projection_sum.finish()
-    out_move.finish()
-    move.finish()
+    for projection_sum in projection_sums:
+        projection_sum.sum.finish()
+    out_sum.sum.finish()
+    for scatter in scatters:
+        scatter.sent()
 
 
 def weight_grads(lines, operands, column_operands):
@@ -1703,23 +1817,26 @@
         functools.partial(grads_kernel, lines, with_columns),
         out_shape=(shape((tall, wide), bf16), shape((8, gain_wide), f32), shape((tall, shard), bf16)) + column_shapes,
         in_specs=[in_vmem] * 2 + [anywhere] * (3 + len(column_operands)),
-        out_specs=[anywhere, in_vmem, anywhere] + [anywhere] * len(column_shapes),
+        out_specs=[in_vmem] * 3 + [anywhere] * len(column_shapes),
         scratch_shapes=[
-            VMEM((places, tall, wide), bf16),
-            VMEM((lines, tall, wide), bf16),
-            VMEM((2, lines - 1, tall, wide), bf16),
-            VMEM((tall, wide), bf16),
+            VMEM((2, places, tall, wide // 2), bf16),
+            VMEM((2, lines, tall, wide // 2), bf16),
+            VMEM((2, 2, lines - 1, tall, wide // 2), bf16),
+            VMEM((2, 3, places // 4, tall, wide // 2), bf16),
+            VMEM((places, tall, shard), bf16),
+            VMEM((lines, tall, shard), bf16),
+            VMEM((2, lines - 1, tall, shard), bf16),
             VMEM((places, 8, gain_wide), f32),
             VMEM((lines, 8, gain_wide), f32),
             VMEM((2, lines - 1, 8, gain_wide), f32),
             VMEM((4, 8, gain_wide), f32),
             *held(operands[3:5]),
-            DMA((4,)),
+            DMA((5,)),
+            DMA((2, LineSum.sems, lines)),
             DMA((LineSum.sems, lines)),
             DMA((LineSum.sems, lines)),
             DMA((2, 4)),
-            DMA((3,)),
-            DMA((3,)),
+            DMA((2, GroupScatter.sems, 3)),
         ]
         + column_scratch,
         compiler_params=pltpu.CompilerParams(
@@ -1896,15 +2013,15 @@
         down_part,
     )
     if fits:
-        result, input_grad, gain_one_term, _, grad_linear, out_grad, down_grad = back(
-            lines, operands, (middle, result_parts.reshape(ctx_size, rows, width))
+        result, input_grad, gain_one_term, grad_linear, out_parts, down_grad = back(
+            lines, operands, (middle, result_parts)
         )
     else:
-        input_grad, gain_one_term, _, grad_linear, out_grad, down_grad = back(lines, operands, ())
+        input_grad, gain_one_term, grad_linear, out_parts, down_grad = back(lines, operands, ())
         branch_two = lax.psum_scatter(result_parts, "ctx", scatter_dimension=0, tiled=True)
         result = (middle + branch_two.astype(f32)).astype(bf16)
 
-    operands = (gain_one_term, gain_two_term, out_grad, normed, grad_linear)
+    operands = (gain_one_term, gain_two_term, out_parts, normed, grad_linear)
     if fits:
         projection_grad, gain_grads, out_grad, gate_up_part = weight_grads(
             lines, operands, (normed_two, grad_gate_up)

time: 529 us -> 483 us (0.913)
  the two profiles are of different devices: /device:TPU:4 before, /device:TPU:24 now
where the time goes in v7:
time: 483 us; the launch traced here: 477 us
  Pallas kernels  471 us (98%)
    pallas_call x1, Pallas kernels, middle_part(): pl.pallas_call(functools.partial(middle_kernel, lines), out_shape=(shape(...  142 us
    pallas_call x1, Pallas kernels, weight_grads(): pl.pallas_call(functools.partial(grads_kernel, lines, with_columns), out_...  137 us
    pallas_call x1, Pallas kernels, back(): pl.pallas_call(functools.partial(back_kernel, lines, with_result), out_sh...  99.6 us
    pallas_call x1, Pallas kernels, front(): pl.pallas_call(functools.partial(front_kernel, lines), out_shape=(shape((...  86.4 us

profile of v7, /device:TPU:24, one launch (start us, length us, event | category | flops | bytes accessed | tf_op | source)
XLA Modules:
  0.0 476.9 jit_solution(4972416595984812954)
XLA Ops:
  0.6 0.7 stack.10
  1.4 0.7 stack.9
  2.1 0.6 pad_maximum_fusion.gains
  2.7 86.4 %front.1 = (bf16[4,128,640]{2,1,0:T(8,128)(2,1)}, bf16[10,128,256]{2,1,0:T(8,128)(2,1)}, bf16[2,8,128,256]{3,2,1,0:T(8,128)(2,1)}, bf16[10,128,1024]{2,1,0:T(8,1...) custom-call(s32[1,2]{1,0:T(1,128)} %bounds_ref.1, ...), custom_call_target="tpu_custom_call" | custom-call | tf_op jit(solution)/shard_map/front/pallas_call | solution.py:890
  89.1 141.7 %middle.1 = (f32[128,2560]{1,0:T(8,128)}, f32[1,2560]{1,0:T(1,128)}, bf16[4,256,2048]{2,1,0:T(8,128)(2,1)}, bf16[4,256,640]{2,1,0:T(8,128)(2,1)}, bf16[8,128,256...) custom-call(f32[2,2560]{1,0:T(2,128)} %pad_maximum_fusion.gains, bf16[8,128,2560]{2,1,0:T(8,128)(2,1)} %get-tuple-element.42.cot_in, ...), custom_call_target="tpu_custom_call" | custom-call | tf_op jit(solution)/shard_map/middle/pallas_call | solution.py:1183
  230.8 99.6 %back.1 = (bf16[128,2560]{1,0:T(8,128)(2,1)}, bf16[128,2560]{1,0:T(8,128)(2,1)}, f32[1,2560]{1,0:T(1,128)}, bf16[4,128,3072]{2,1,0:T(8,128)(2,1)}, bf16[8,320,64...) custom-call(f32[128,2560]{1,0:T(8,128)} %get-tuple-element.47.grad_middle, bf16[128,2560]{1,0:T(8,128)(2,1)} %bitcast.11, ...), custom_call_target="tpu_custom_call" | custom-call | tf_op jit(solution)/shard_map/back/pallas_call | solution.py:1508
  330.4 136.5 %grads.1 = (bf16[320,768]{1,0:T(8,128)(2,1)}, f32[8,384]{1,0:T(8,128)}, bf16[320,640]{1,0:T(8,128)(2,1)}, bf16[8,320,512]{2,1,0:T(8,128)(2,1)}) custom-call(f32[1,2560]{1,0:T(1,128)} %get-tuple-element.58.gain_one, f32[1,2560]{1,0:T(1,128)} %get-tuple-element.59.gain_two, bf16[8,320,640]{2,1,0:T(8,128)(2,1)} %get-tuple-element.60.out_in, ...), custom_call_target="tpu_custom_call" | custom-call | tf_op jit(solution)/shard_map/grads/pallas_call | solution.py:1816
  467.0 0.0 copy-start.1
  467.0 0.0 copy-start
  467.0 6.5 %assemble.1 = (f32[320,640]{1,0:T(8,128)}, f32[320,128]{1,0:T(8,128)}, f32[320,640]{1,0:T(8,128)}, f32[960,640]{1,0:T(8,128)}, f32[320,3840]{1,0:T(8,128)}) custom-call(bf16[320,768]{1,0:T(8,128)(2,1)} %get-tuple-element.66.projection, bf16[320,640]{1,0:T(8,128)(2,1)} %get-tuple-element.67.out, bf16[4,256,640]{2,1,0:T(8,128)(2,1)} %get-tuple-element.68.down, ...), custom_call_target="tpu_custom_call" | custom-call | tf_op jit(solution)/shard_map/assemble/pallas_call | solution.py:1879
  473.5 0.8 constant_dynamic-slice_fusion
  474.3 0.5 slice_bitcast_fusion
  474.8 0.0 copy-done.1
  474.8 0.8 copy.21
  475.7 0.0 copy-done
  475.7 0.8 copy.22
Async XLA Ops:
  467.0 7.8 %copy-start.1 = (bf16[128,2560]{1,0:T(8,128)(2,1)S(1)}, bf16[128,2560]{1,0:T(8,128)(2,1)}, u32[]{:S(2)}) copy-start(bf16[128,2560]{1,0:T(8,128)(2,1)} %get-tuple-element.56) | copy-start | bytes 1966084
  467.0 8.7 %copy-start = (bf16[128,2560]{1,0:T(8,128)(2,1)S(1)}, bf16[128,2560]{1,0:T(8,128)(2,1)}, u32[]{:S(2)}) copy-start(bf16[128,2560]{1,0:T(8,128)(2,1)} %get-tuple-element.57) | copy-start | bytes 1966084

commit v8 on v7

--- a/solution.py
+++ b/solution.py
@@ -620,16 +620,16 @@
     cot,
     w_down,
     w_gate_up,
-    normed_out,
-    query_out,
-    keyval_out,
-    probs_out,
-    mixed_out,
+    normed_dst,
+    query_dst,
+    keyval_dst,
+    probs_dst,
+    mixed_dst,
     middle_out,
     normed_two_out,
     cosine,
     sine,
-    columns_out,
+    columns_dst,
     cot_all,
     rows_all,
     whole,
@@ -643,6 +643,13 @@
     bias,
     w_rows,
     windows,
+    normed_out,
+    query_out,
+    keyval_out,
+    probs_out,
+    mixed_out,
+    columns_out,
+    put_sems,
     w_keyval,
     w_query,
     w_out,
@@ -664,6 +671,12 @@
         ((w_keyval_in, w_keyval), (w_query_in, w_query), (w_out_in, w_out)), fetch_sems
     )
     p.barrier()
+    puts = []
+
+    def put(src, dst):
+        puts.append(pltpu.make_async_copy(src, dst, put_sems.at[len(puts)]))
+        puts[-1].start()
+
 
     units = w_gate_up.shape[1] // 2
     piece = units // (4 * 2 * lines)
@@ -756,6 +769,7 @@
     give(0, 1)
     trade.wait()
     normed_out[...] = slots[0]
+    put(normed_out, normed_dst)
 
     half = (heads // 2) * HD
     chunks = [(0, kv_width), (kv_width, half), (kv_width + half, inner - half)]
@@ -800,7 +814,7 @@
             at = h if i == 1 else h + heads // 2
             query_out[at] = (turned * HD**-0.5).astype(bf16)
 
-    give(1, 5)
+    give(1, 4)
     take_queries(1)
     for step in range(1, lines - 1):
         for gather in kv_gathers:
@@ -810,6 +824,8 @@
     for gather in kv_gathers:
         gather.finish()
     keyval_out[...] = keyval[...]
+    put(keyval_out, keyval_dst)
+    put(query_out, query_dst)
 
 
     def two_heads(i, carry):
@@ -831,7 +847,8 @@
     lax.fori_loop(0, heads // 2, two_heads, 0)
     trade_two = GroupTrade(p, mixed, slots.at[1], trade_sems.at[1], slots.shape[3])
     trade_two.start()
-    give(5, 7)
+    give(4, 6)
+    put(probs_out, probs_dst)
     for q in range(4):
         pack_columns(q)
     if lines > 2:
@@ -840,6 +857,7 @@
         group.finish(i, spans[i])
     trade_two.wait()
     mixed_out[...] = slots[1]
+    put(mixed_out, mixed_dst)
     fetch.wait(2)
 
     half = width // 2
@@ -850,10 +868,11 @@
         group_two.give(i, spans_two[i])
     for i in range(2):
         group_two.pass_on(i, spans_two[i])
-    give(7, 8)
+    give(6, 8)
     for q in range(4, 8):
         pack_columns(q)
-    pass_on(0, 7)
+    put(columns_out, columns_dst)
+    pass_on(0, 6)
     for step in range(2, lines - 1):
         cot_gather.step(step)
     for i in range(2):
@@ -862,11 +881,13 @@
         )
     normed_two_out[...] = rms_norm(middle_out[...], gains[1:2]).astype(bf16)
 
-    pass_on(7, 8)
+    pass_on(6, 8)
     for i in range(2):
         group_two.finish(i, spans_two[i])
     trade.finish()
     trade_two.finish()
+    for copy in puts:
+        copy.wait()
     down.local().wait()
     cot_local.wait()
     for i in range(down.pieces):
@@ -887,24 +908,29 @@
     shape = jax.ShapeDtypeStruct
     pieces = 8 if padded_piece % 128 == 0 else 1
     assert inner == width
+    copied = [
+        shape((4, rows, shard), bf16),
+        shape((heads, rows, HD), bf16),
+        shape((2, places, rows, HD), bf16),
+        shape((heads, rows, length), bf16),
+        shape((4, rows, shard), bf16),
+        shape((shard, 8 * padded_piece), bf16),
+    ]
+    outs = (
+        *copied[:5],
+        shape((rows, width), f32),
+        shape((rows, width), bf16),
+        shape((rows, 128), f32),
+        shape((rows, 128), f32),
+        copied[5],
+        shape((places, rows, width), bf16),
+        shape((4, padded_piece, width), bf16),
+    )
     return pl.pallas_call(
         functools.partial(front_kernel, lines),
-        out_shape=(
-            shape((4, rows, shard), bf16),
-            shape((heads, rows, HD), bf16),
-            shape((2, places, rows, HD), bf16),
-            shape((heads, rows, length), bf16),
-            shape((4, rows, shard), bf16),
-            shape((rows, width), f32),
-            shape((rows, width), bf16),
-            shape((rows, 128), f32),
-            shape((rows, 128), f32),
-            shape((shard, 8 * padded_piece), bf16),
-            shape((places, rows, width), bf16),
-            shape((4, padded_piece, width), bf16),
-        ),
+        out_shape=outs,
         in_specs=[pl.BlockSpec(memory_space=pltpu.SMEM)] + [in_vmem] * 2 + [anywhere] * 6,
-        out_specs=[in_vmem] * 10 + [anywhere] * 2,
+        out_specs=[anywhere] * 5 + [in_vmem] * 4 + [anywhere] * 3,
         scratch_shapes=[
             VMEM((rows, width), bf16),
             VMEM((2, 4, rows, shard), bf16),
@@ -917,6 +943,8 @@
             VMEM((rows, length), f32),
             VMEM((padded_piece, width), bf16),
             VMEM((2, shard, (padded_piece + 127) // 128 * 128 + 128), bf16),
+            *held(copied),
+            DMA((6,)),
             *held(operands[3:6]),
             DMA((3,)),
             DMA((2, GroupTrade.sems, 4)),
@@ -960,7 +988,7 @@
     w_columns,
     grad_middle_out,
     gain_out,
-    grads_out,
+    grads_dst,
     down_out,
     normed_all_out,
     result_parts,
@@ -976,6 +1004,8 @@
     down_far,
     cot_all,
     w_rows,
+    grads_out,
+    put_sems,
     fetch_sems,
     gather_sems,
     column_sems,
@@ -1046,7 +1076,9 @@
         for line_sum in line_sums:
             line_sum.far(turn)
 
-    def feed_forward(line):
+    def feed_forward(turn):
+        line = line_sums[0].order(turn)
+
         def one(i, carry):
             cols = pl.ds(pl.multiple_of(i * tile, 128), tile)
             up_cols = pl.ds(pl.multiple_of(i * tile + padded, 128), tile)
@@ -1064,7 +1096,7 @@
             grads_out[line, :, up_cols] = (grad * gelu).astype(bf16)
             return carry
 
-        lax.fori_loop(0, padded // tile, one, 0)
+        lax.fori_loop(0, padded // tile, one, 0, unroll=True)
 
         def back(g, carry):
             product = contract_rows(grads_out[line], weights[g]).astype(bf16)
@@ -1072,7 +1104,10 @@
             parts[g // 2, pl.ds(2 * line, 2), :, cols] = product.reshape(2, rows, shard)
             return carry
 
-        lax.fori_loop(0, 4, back, 0)
+        pltpu.make_async_copy(grads_out.at[line], grads_dst.at[line], put_sems.at[turn]).start()
+        for half in range(2):
+            lax.fori_loop(2 * half, 2 * half + 2, back, 0, unroll=True)
+            line_sums[half].across(turn).start()
 
     result_stage = normed_all
 
@@ -1091,7 +1126,7 @@
             result_stage[pl.ds(2 * line, 2), :, cols] = product.reshape(2, rows, shard)
             return carry
 
-        lax.fori_loop(0, 4, one, 0)
+        lax.fori_loop(0, 4, one, 0, unroll=True)
         result_copy(line).start()
 
     quarter = padded // 4
@@ -1109,17 +1144,18 @@
             down_parts[g] = contract_tokens(left, right).astype(bf16)
             return carry
 
-        lax.fori_loop(0, 4, one, 0)
+        lax.fori_loop(0, 4, one, 0, unroll=True)
         down_out[i] = down_parts[p.f]
         down_group(i).give(i, every)
 
     for turn in range(lines):
-        feed_forward(line_sums[0].order(turn))
-        for line_sum in line_sums:
-            line_sum.across(turn).start()
+        feed_forward(turn)
         if turn == lines - 2:
             near(0)
     normed_local.wait()
+    for turn in range(lines):
+        line = line_sums[0].order(turn)
+        pltpu.make_async_copy(grads_out.at[line], grads_dst.at[line], put_sems.at[turn]).wait()
 
     for i in range(4):
         if i >= 1:
@@ -1191,7 +1227,7 @@
             shape((places, rows, width), bf16),
         ),
         in_specs=[in_vmem] + [anywhere] * 5,
-        out_specs=[in_vmem] * 4 + [anywhere] * 2,
+        out_specs=[in_vmem] * 2 + [anywhere, in_vmem] + [anywhere] * 2,
         scratch_shapes=[
             VMEM((places, rows, width), bf16),
             VMEM((4, shard, 2 * padded), bf16),
@@ -1204,6 +1240,8 @@
             VMEM((2, quarter, shard), bf16),
             VMEM((4, quarter, shard), bf16),
             *held(operands[1:3]),
+            VMEM((lines, 2 * rows, 2 * padded), bf16),
+            DMA((lines,)),
             DMA((2,)),
             DMA((LineGather.sems, lines)),
             DMA((GroupGather.sems, pieces)),
@@ -1366,6 +1404,8 @@
     out_own.start()
     if with_result:
         result_sums[0].near(2)
+        result_copies[1].wait()
+        result_sums[1].sum.start(1)
     back_trade.wait()
     for g in range(4):
         grad_mixed[:, g * shard : (g + 1) * shard] = trade_slots[0, g]
@@ -1408,12 +1448,13 @@
         p, linear, linear_all, linear_sems, own_sems.at[1], 2, (q_at, kv_at)
     )
     linear_group.give(0)
+    out_scatter.copy(1, 1).start()
     kv_parts[...] = kv_total[...].astype(bf16).reshape(kv_parts.shape)
     kv_sum = LineSum(p, kv_parts, kv_side, kv_chain, kv_sems)
     kv_sum.start(lines)
     if with_result:
-        result_copies[1].wait()
-        result_sums[1].start()
+        for turn in range(1, lines):
+            result_sums[1].sum.across(turn).start()
         result_sums[0].near(lines)
         result_sums[0].far(1)
     kv_sum.turns(0)
@@ -1421,7 +1462,7 @@
     linear[:, :HD] = rotated(own[:, :HD], cosine[...], -sine[...]).astype(bf16)
     linear[:, pl.ds(HD, HD)] = own[:, HD:].astype(bf16)
     linear_group.give(1)
-    out_scatter.copy(1, 1).start()
+    out_scatter.copy(2, 0).start()
     linear_group.local().start()
     if with_result:
         result_sums[0].far(2)
@@ -1450,7 +1491,7 @@
     normed_back(p.twin_f)
     last_trade.send(1)
     last_trade.send(3)
-    out_scatter.send(2)
+    out_scatter.copy(2, 1).start()
     normed_back(p.f)
     last_trade.own().start()
     if with_result:
@@ -1611,7 +1652,9 @@
     gain_sum.start(lines)
 
     projection_sums = [
-        Turns(LineSum(p, parts.at[i], side.at[i], chain.at[i], projection_sems.at[i]))
+        Turns(
+            LineSum(p, parts.at[i], side.at[i], chain.at[i], projection_sems.at[i]), lines
+        )
         for i in range(2)
     ]
     out_sum = Turns(LineSum(p, out_parts, out_side, out_chain, out_sems))
@@ -1735,14 +1778,15 @@
     out_out[...] = out_sum.total().astype(bf16)
     first.far(2)
     if with_columns:
+        second.near(1)
         for k in range(1, lines):
-            second.near(k)
             complete(k)
             if k + 2 < lines:
                 chunk_step(k + 2)
-            first.far(k + 2)
-            second.near(k + 1)
-            second.far(k)
+            if k == 1:
+                first.far(lines)
+                second.near(lines)
+            second.far(k + 1)
         for k in (lines - 2, lines - 1):
             group(k).passed(k, every)
         group(lines - 1).given(lines - 1, every)

time: 483 us -> 476 us (0.986)
  the two profiles are of different devices: /device:TPU:24 before, /device:TPU:4 now
where the time goes in v8:
time: 476 us; the launch traced here: 469 us
  Pallas kernels  463 us (97%)
    pallas_call x1, Pallas kernels, weight_grads(): pl.pallas_call(functools.partial(grads_kernel, lines, with_columns), out_...  143 us
    pallas_call x1, Pallas kernels, middle_part(): pl.pallas_call(functools.partial(middle_kernel, lines), out_shape=(shape(...  132 us
    pallas_call x1, Pallas kernels, back(): pl.pallas_call(functools.partial(back_kernel, lines, with_result), out_sh...  97.7 us
    pallas_call x1, Pallas kernels, front(): pl.pallas_call(functools.partial(front_kernel, lines), out_shape=outs, in...  83.9 us

profile of v8, /device:TPU:4, one launch (start us, length us, event | category | flops | bytes accessed | tf_op | source)
XLA Modules:
  0.0 468.7 jit_solution(6887645025160683110)
XLA Ops:
  0.6 0.7 stack.10
  1.4 0.7 stack.9
  2.1 0.6 pad_maximum_fusion.gains
  2.7 83.9 %front.1 = (bf16[4,128,640]{2,1,0:T(8,128)(2,1)}, bf16[10,128,256]{2,1,0:T(8,128)(2,1)}, bf16[2,8,128,256]{3,2,1,0:T(8,128)(2,1)}, bf16[10,128,1024]{2,1,0:T(8,1...) custom-call(s32[1,2]{1,0:T(1,128)} %bounds_ref.1, ...), custom_call_target="tpu_custom_call" | custom-call | tf_op jit(solution)/shard_map/front/pallas_call | solution.py:929
  86.6 132.2 %middle.1 = (f32[128,2560]{1,0:T(8,128)}, f32[1,2560]{1,0:T(1,128)}, bf16[4,256,2048]{2,1,0:T(8,128)(2,1)}, bf16[4,256,640]{2,1,0:T(8,128)(2,1)}, bf16[8,128,256...) custom-call(f32[2,2560]{1,0:T(2,128)} %pad_maximum_fusion.gains, bf16[8,128,2560]{2,1,0:T(8,128)(2,1)} %get-tuple-element.42.cot_in, ...), custom_call_target="tpu_custom_call" | custom-call | tf_op jit(solution)/shard_map/middle/pallas_call | solution.py:1219
  218.8 97.7 %back.1 = (bf16[128,2560]{1,0:T(8,128)(2,1)}, bf16[128,2560]{1,0:T(8,128)(2,1)}, f32[1,2560]{1,0:T(1,128)}, bf16[4,128,3072]{2,1,0:T(8,128)(2,1)}, bf16[8,320,64...) custom-call(f32[128,2560]{1,0:T(8,128)} %get-tuple-element.47.grad_middle, bf16[128,2560]{1,0:T(8,128)(2,1)} %bitcast.11, ...), custom_call_target="tpu_custom_call" | custom-call | tf_op jit(solution)/shard_map/back/pallas_call | solution.py:1549
  316.5 142.5 %grads.1 = (bf16[320,768]{1,0:T(8,128)(2,1)}, f32[8,384]{1,0:T(8,128)}, bf16[320,640]{1,0:T(8,128)(2,1)}, bf16[8,320,512]{2,1,0:T(8,128)(2,1)}) custom-call(f32[1,2560]{1,0:T(1,128)} %get-tuple-element.58.gain_one, f32[1,2560]{1,0:T(1,128)} %get-tuple-element.59.gain_two, bf16[8,320,640]{2,1,0:T(8,128)(2,1)} %get-tuple-element.60.out_in, ...), custom_call_target="tpu_custom_call" | custom-call | tf_op jit(solution)/shard_map/grads/pallas_call | solution.py:1860
  459.0 0.0 copy-start.1
  459.0 0.0 copy-start
  459.1 6.5 %assemble.1 = (f32[320,640]{1,0:T(8,128)}, f32[320,128]{1,0:T(8,128)}, f32[320,640]{1,0:T(8,128)}, f32[960,640]{1,0:T(8,128)}, f32[320,3840]{1,0:T(8,128)}) custom-call(bf16[320,768]{1,0:T(8,128)(2,1)} %get-tuple-element.66.projection, bf16[320,640]{1,0:T(8,128)(2,1)} %get-tuple-element.67.out, bf16[4,256,640]{2,1,0:T(8,128)(2,1)} %get-tuple-element.68.down, ...), custom_call_target="tpu_custom_call" | custom-call | tf_op jit(solution)/shard_map/assemble/pallas_call | solution.py:1923
  465.6 0.8 constant_dynamic-slice_fusion
  466.4 0.5 slice_bitcast_fusion
  466.9 0.0 copy-done.1
  466.9 0.8 copy.21
  467.7 0.0 copy-done
  467.7 0.8 copy.22
Async XLA Ops:
  459.0 7.8 %copy-start.1 = (bf16[128,2560]{1,0:T(8,128)(2,1)S(1)}, bf16[128,2560]{1,0:T(8,128)(2,1)}, u32[]{:S(2)}) copy-start(bf16[128,2560]{1,0:T(8,128)(2,1)} %get-tuple-element.56) | copy-start | bytes 1966084
  459.0 8.7 %copy-start = (bf16[128,2560]{1,0:T(8,128)(2,1)S(1)}, bf16[128,2560]{1,0:T(8,128)(2,1)}, u32[]{:S(2)}) copy-start(bf16[128,2560]{1,0:T(8,128)(2,1)} %get-tuple-element.57) | copy-start | bytes 1966084

commit v9 on v8

--- a/solution.py
+++ b/solution.py
@@ -596,6 +596,10 @@
         self.sent(i)
 
 
+def is_long(length):
+    return length > 2048
+
+
 def tiles_of(first, count, tile):
     tile = tile if count % tile == 0 else 128
 
@@ -604,7 +608,7 @@
             body(pl.ds(pl.multiple_of(first + i * tile, 128), tile))
             return carry
 
-        lax.fori_loop(0, count // tile, one, 0)
+        lax.fori_loop(0, count // tile, one, 0, unroll=True)
 
     return loop
 
@@ -844,7 +848,7 @@
         mixed[:, pl.ds(at + HD, HD)] = product[rows:]
         return carry
 
-    lax.fori_loop(0, heads // 2, two_heads, 0)
+    lax.fori_loop(0, heads // 2, two_heads, 0, unroll=not is_long(length))
     trade_two = GroupTrade(p, mixed, slots.at[1], trade_sems.at[1], slots.shape[3])
     trade_two.start()
     give(4, 6)
@@ -1256,10 +1260,6 @@
     )(*operands)
 
 
-def is_long(length):
-    return length > 2048
-
-
 def back_kernel(
     lines,
     with_result,
@@ -1297,6 +1297,7 @@
         kv_parts,
         kv_side,
         kv_chain,
+        query_parts,
         out_stage,
         w_out,
         probs,
@@ -1443,7 +1444,7 @@
         kv_total[:, HD:] += contract_tokens(weights, outer)
         return carry
 
-    lax.fori_loop(0, heads // batch, some_heads, 0)
+    lax.fori_loop(0, heads // batch, some_heads, 0, unroll=not long)
     linear_group = GroupGather(
         p, linear, linear_all, linear_sems, own_sems.at[1], 2, (q_at, kv_at)
     )
@@ -1457,7 +1458,19 @@
             result_sums[1].sum.across(turn).start()
         result_sums[0].near(lines)
         result_sums[0].far(1)
+    fetch.wait(4, 5)
+
+    def query_back(g, block):
+        query_parts[g] = contract_rows(block, w_query[...])
+
+    query_back(p.f, linear[:, q_at])
+    linear_group.near(0)
+    query_back(p.twin_f, linear_all[p.twin_f, :, q_at])
     kv_sum.turns(0)
+    linear_group.pass_on(0)
+    query_back(p.cross_f, linear_all[p.cross_f, :, q_at])
+    linear_group.last(0)
+    query_back(p.diag_f, linear_all[p.diag_f, :, q_at])
     own = kv_sum.total()
     linear[:, :HD] = rotated(own[:, :HD], cosine[...], -sine[...]).astype(bf16)
     linear[:, pl.ds(HD, HD)] = own[:, HD:].astype(bf16)
@@ -1467,14 +1480,10 @@
     if with_result:
         result_sums[0].far(2)
         result_sums[1].near(2)
-    fetch.wait(4, 5)
-    linear_group.pass_on(0)
     linear_group.pass_on(1)
     linear_group.local().wait()
-    for i in range(2):
-        linear_group.near(i)
-        linear_group.last(i)
-
+    linear_group.near(1)
+    linear_group.last(1)
     linear_copy = pltpu.make_async_copy(linear_all, linear_out, own_sems.at[4])
     linear_copy.start()
 
@@ -1482,8 +1491,7 @@
 
     def normed_back(g):
         product = contract_rows(linear_all[g, :, kv_at], w_keyval[...])
-        product += contract_rows(linear_all[g, :, q_at], w_query[...])
-        trade_parts[1, g] = product.astype(bf16)
+        trade_parts[1, g] = (product + query_parts[g]).astype(bf16)
 
     normed_back(p.cross_f)
     last_trade.send(2)
@@ -1570,6 +1578,7 @@
             VMEM((places, rows, 2 * HD), bf16),
             VMEM((lines, rows, 2 * HD), bf16),
             VMEM((2, lines - 1, rows, 2 * HD), bf16),
+            VMEM((4, rows, shard), f32),
             VMEM((4, places // 4, tall, shard), bf16),
             *scratch,
             DMA((7,)),
@@ -1683,7 +1692,7 @@
                 chunk_parts[g] = contract_tokens(left, right.reshape(-1, block)).astype(bf16)
                 return carry
 
-            lax.fori_loop(0, 4, one, 0)
+            lax.fori_loop(0, 4, one, 0, unroll=True)
             chunks[k] = chunk_parts[p.f]
             group(k).give(k, every)
 
@@ -1786,7 +1795,7 @@
             if k == 1:
                 first.far(lines)
                 second.near(lines)
-            second.far(k + 1)
+            second.far(k)
         for k in (lines - 2, lines - 1):
             group(k).passed(k, every)
         group(lines - 1).given(lines - 1, every)

time: 476 us -> 473 us (level)
  the two profiles are of different devices: /device:TPU:4 before, /device:TPU:8 now
where the time goes in v9:
time: 473 us; the launch traced here: 464 us
  Pallas kernels  458 us (97%)
    pallas_call x1, Pallas kernels, weight_grads(): pl.pallas_call(functools.partial(grads_kernel, lines, with_columns), out_...  138 us
    pallas_call x1, Pallas kernels, middle_part(): pl.pallas_call(functools.partial(middle_kernel, lines), out_shape=(shape(...  136 us
    pallas_call x1, Pallas kernels, back(): pl.pallas_call(functools.partial(back_kernel, lines, with_result), out_sh...  93.5 us
    pallas_call x1, Pallas kernels, front(): pl.pallas_call(functools.partial(front_kernel, lines), out_shape=outs, in...  83.8 us

profile of v9, /device:TPU:8, one launch (start us, length us, event | category | flops | bytes accessed | tf_op | source)
XLA Modules:
  0.0 463.7 jit_solution(9307590315124097014)
XLA Ops:
  0.6 0.7 stack.10
  1.4 0.7 stack.9
  2.1 0.6 pad_maximum_fusion.gains
  2.7 83.8 %front.1 = (bf16[4,128,640]{2,1,0:T(8,128)(2,1)}, bf16[10,128,256]{2,1,0:T(8,128)(2,1)}, bf16[2,8,128,256]{3,2,1,0:T(8,128)(2,1)}, bf16[10,128,1024]{2,1,0:T(8,1...) custom-call(s32[1,2]{1,0:T(1,128)} %bounds_ref.1, ...), custom_call_target="tpu_custom_call" | custom-call | tf_op jit(solution)/shard_map/front/pallas_call | solution.py:933
  86.5 135.9 %middle.1 = (f32[128,2560]{1,0:T(8,128)}, f32[1,2560]{1,0:T(1,128)}, bf16[4,256,2048]{2,1,0:T(8,128)(2,1)}, bf16[4,256,640]{2,1,0:T(8,128)(2,1)}, bf16[8,128,256...) custom-call(f32[2,2560]{1,0:T(2,128)} %pad_maximum_fusion.gains, bf16[8,128,2560]{2,1,0:T(8,128)(2,1)} %get-tuple-element.42.cot_in, ...), custom_call_target="tpu_custom_call" | custom-call | tf_op jit(solution)/shard_map/middle/pallas_call | solution.py:1223
  222.3 93.5 %back.1 = (bf16[128,2560]{1,0:T(8,128)(2,1)}, bf16[128,2560]{1,0:T(8,128)(2,1)}, f32[1,2560]{1,0:T(1,128)}, bf16[4,128,3072]{2,1,0:T(8,128)(2,1)}, bf16[8,320,64...) custom-call(f32[128,2560]{1,0:T(8,128)} %get-tuple-element.47.grad_middle, bf16[128,2560]{1,0:T(8,128)(2,1)} %bitcast.11, ...), custom_call_target="tpu_custom_call" | custom-call | tf_op jit(solution)/shard_map/back/pallas_call | solution.py:1557
  315.9 138.1 %grads.1 = (bf16[320,768]{1,0:T(8,128)(2,1)}, f32[8,384]{1,0:T(8,128)}, bf16[320,640]{1,0:T(8,128)(2,1)}, bf16[8,320,512]{2,1,0:T(8,128)(2,1)}) custom-call(f32[1,2560]{1,0:T(1,128)} %get-tuple-element.58.gain_one, f32[1,2560]{1,0:T(1,128)} %get-tuple-element.59.gain_two, bf16[8,320,640]{2,1,0:T(8,128)(2,1)} %get-tuple-element.60.out_in, ...), custom_call_target="tpu_custom_call" | custom-call | tf_op jit(solution)/shard_map/grads/pallas_call | solution.py:1869
  454.0 0.0 copy-start.1
  454.0 0.0 copy-start
  454.0 6.5 %assemble.1 = (f32[320,640]{1,0:T(8,128)}, f32[320,128]{1,0:T(8,128)}, f32[320,640]{1,0:T(8,128)}, f32[960,640]{1,0:T(8,128)}, f32[320,3840]{1,0:T(8,128)}) custom-call(bf16[320,768]{1,0:T(8,128)(2,1)} %get-tuple-element.66.projection, bf16[320,640]{1,0:T(8,128)(2,1)} %get-tuple-element.67.out, bf16[4,256,640]{2,1,0:T(8,128)(2,1)} %get-tuple-element.68.down, ...), custom_call_target="tpu_custom_call" | custom-call | tf_op jit(solution)/shard_map/assemble/pallas_call | solution.py:1932
  460.6 0.8 constant_dynamic-slice_fusion
  461.3 0.5 slice_bitcast_fusion
  461.9 0.0 copy-done.1
  461.9 0.8 copy.21
  462.7 0.0 copy-done
  462.7 0.8 copy.22
Async XLA Ops:
  454.0 7.8 %copy-start.1 = (bf16[128,2560]{1,0:T(8,128)(2,1)S(1)}, bf16[128,2560]{1,0:T(8,128)(2,1)}, u32[]{:S(2)}) copy-start(bf16[128,2560]{1,0:T(8,128)(2,1)} %get-tuple-element.56) | copy-start | bytes 1966084
  454.0 8.7 %copy-start = (bf16[128,2560]{1,0:T(8,128)(2,1)S(1)}, bf16[128,2560]{1,0:T(8,128)(2,1)}, u32[]{:S(2)}) copy-start(bf16[128,2560]{1,0:T(8,128)(2,1)} %get-tuple-element.57) | copy-start | bytes 1966084

commit v10 on v9

--- a/solution.py
+++ b/solution.py
@@ -1504,7 +1504,7 @@
     last_trade.own().start()
     if with_result:
         result_sums[0].far(3)
-        result_sums[1].far(2)
+        result_sums[1].far(3)
     last_trade.wait()
     for g in range(4):
         grad_mixed[:, g * shard : (g + 1) * shard] = trade_slots[1, g]

time: 473 us -> 472 us (level)
  no operation moved by 1% of the time
where the time goes in v10:
time: 472 us; the launch traced here: 463 us
  Pallas kernels  457 us (97%)
    pallas_call x1, Pallas kernels, weight_grads(): pl.pallas_call(functools.partial(grads_kernel, lines, with_columns), out_...  138 us
    pallas_call x1, Pallas kernels, middle_part(): pl.pallas_call(functools.partial(middle_kernel, lines), out_shape=(shape(...  136 us
    pallas_call x1, Pallas kernels, back(): pl.pallas_call(functools.partial(back_kernel, lines, with_result), out_sh...  93.3 us
    pallas_call x1, Pallas kernels, front(): pl.pallas_call(functools.partial(front_kernel, lines), out_shape=outs, in...  83.8 us

profile of v10, /device:TPU:8, one launch (start us, length us, event | category | flops | bytes accessed | tf_op | source)
XLA Modules:
  0.0 462.9 jit_solution(8514067161198426080)
XLA Ops:
  0.6 0.7 stack.10
  1.4 0.7 stack.9
  2.1 0.6 pad_maximum_fusion.gains
  2.7 83.8 %front.1 = (bf16[4,128,640]{2,1,0:T(8,128)(2,1)}, bf16[10,128,256]{2,1,0:T(8,128)(2,1)}, bf16[2,8,128,256]{3,2,1,0:T(8,128)(2,1)}, bf16[10,128,1024]{2,1,0:T(8,1...) custom-call(s32[1,2]{1,0:T(1,128)} %bounds_ref.1, ...), custom_call_target="tpu_custom_call" | custom-call | tf_op jit(solution)/shard_map/front/pallas_call | solution.py:933
  86.5 135.9 %middle.1 = (f32[128,2560]{1,0:T(8,128)}, f32[1,2560]{1,0:T(1,128)}, bf16[4,256,2048]{2,1,0:T(8,128)(2,1)}, bf16[4,256,640]{2,1,0:T(8,128)(2,1)}, bf16[8,128,256...) custom-call(f32[2,2560]{1,0:T(2,128)} %pad_maximum_fusion.gains, bf16[8,128,2560]{2,1,0:T(8,128)(2,1)} %get-tuple-element.42.cot_in, ...), custom_call_target="tpu_custom_call" | custom-call | tf_op jit(solution)/shard_map/middle/pallas_call | solution.py:1223
  222.3 93.3 %back.1 = (bf16[128,2560]{1,0:T(8,128)(2,1)}, bf16[128,2560]{1,0:T(8,128)(2,1)}, f32[1,2560]{1,0:T(1,128)}, bf16[4,128,3072]{2,1,0:T(8,128)(2,1)}, bf16[8,320,64...) custom-call(f32[128,2560]{1,0:T(8,128)} %get-tuple-element.47.grad_middle, bf16[128,2560]{1,0:T(8,128)(2,1)} %bitcast.11, ...), custom_call_target="tpu_custom_call" | custom-call | tf_op jit(solution)/shard_map/back/pallas_call | solution.py:1557
  315.6 137.5 %grads.1 = (bf16[320,768]{1,0:T(8,128)(2,1)}, f32[8,384]{1,0:T(8,128)}, bf16[320,640]{1,0:T(8,128)(2,1)}, bf16[8,320,512]{2,1,0:T(8,128)(2,1)}) custom-call(f32[1,2560]{1,0:T(1,128)} %get-tuple-element.58.gain_one, f32[1,2560]{1,0:T(1,128)} %get-tuple-element.59.gain_two, bf16[8,320,640]{2,1,0:T(8,128)(2,1)} %get-tuple-element.60.out_in, ...), custom_call_target="tpu_custom_call" | custom-call | tf_op jit(solution)/shard_map/grads/pallas_call | solution.py:1869
  453.2 0.0 copy-start.1
  453.2 0.0 copy-start
  453.2 6.5 %assemble.1 = (f32[320,640]{1,0:T(8,128)}, f32[320,128]{1,0:T(8,128)}, f32[320,640]{1,0:T(8,128)}, f32[960,640]{1,0:T(8,128)}, f32[320,3840]{1,0:T(8,128)}) custom-call(bf16[320,768]{1,0:T(8,128)(2,1)} %get-tuple-element.66.projection, bf16[320,640]{1,0:T(8,128)(2,1)} %get-tuple-element.67.out, bf16[4,256,640]{2,1,0:T(8,128)(2,1)} %get-tuple-element.68.down, ...), custom_call_target="tpu_custom_call" | custom-call | tf_op jit(solution)/shard_map/assemble/pallas_call | solution.py:1932
  459.7 0.8 constant_dynamic-slice_fusion
  460.5 0.5 slice_bitcast_fusion
  461.0 0.0 copy-done.1
  461.0 0.8 copy.21
  461.9 0.0 copy-done
  461.9 0.8 copy.22
Async XLA Ops:
  453.2 7.8 %copy-start.1 = (bf16[128,2560]{1,0:T(8,128)(2,1)S(1)}, bf16[128,2560]{1,0:T(8,128)(2,1)}, u32[]{:S(2)}) copy-start(bf16[128,2560]{1,0:T(8,128)(2,1)} %get-tuple-element.56) | copy-start | bytes 1966084
  453.2 8.7 %copy-start = (bf16[128,2560]{1,0:T(8,128)(2,1)S(1)}, bf16[128,2560]{1,0:T(8,128)(2,1)}, u32[]{:S(2)}) copy-start(bf16[128,2560]{1,0:T(8,128)(2,1)} %get-tuple-element.57) | copy-start | bytes 1966084
